TPU v7x, 256 devices: a whole 4x4x8 slice. The times are simulated.
256 devices in a mesh: row: 32 (over z, x_lo, core), col: 8 (over y, x_hi).
Axes of the slice: x: 4 (x_hi: 2, x_lo: 2; x = x_hi * 2 + x_lo), y: 4, z: 8, core: 2. Of those that a mesh axis runs over, the one named last changes fastest.
Arguments:
- x_state: float32 [64, 64, 128, 32], P('row', 'col'), may hold values from -6 to 6
- langevin_noise: float32 [64, 64, 128, 32], P('row', 'col'), may hold values from -6 to 6
- observed: float32 [32768], P('row'), may hold values from -6 to 6
- data_weight: float32 [32768], P('row'), may hold values from 0.5 to 2
- sens_tiles: bfloat16 [32, 8, 48, 128, 128], P('row', 'col'), may hold values from -0.109375 to 0.109375
- tile_rows: int32 [32, 8, 48], P('row', 'col'), may hold values from 0 to 7
- tile_cols: int32 [32, 8, 48], P('row', 'col'), may hold values from 0 to 511
- counts: int32 [32, 8], P('row', 'col'), may hold values from 6 to 48, as said below
Outputs:
- x_next: float32 [64, 64, 128, 32], P('row', 'col')
Inputs may be any that keep to these rules, and one draw needn't show every extreme that they name: Only the first counts[r, c] slots of a device hold tiles of G; at least one device uses all 48 slots, the others 48, 24, 12 or 6.
All inputs are finite; a program needn't handle non-finite values.
Results may differ from a plain program's by a relative error of at most 0.0009.
Values may be sent and summed in bfloat16 or wider, within the bound.
No kernel may reach another device: no remote copies, remote signals or barrier semaphores. Data moves between devices by JAX's collectives and lax.ppermute only.
A program may use at most 128 MiB of HBM per device.

v0:
```python
import math

import jax
import jax.numpy as jnp
from jax import lax
from jax.sharding import PartitionSpec as P

ITERS = 3


theta_tv = 0.25
tau_dual = 1.0 / (12.0 * 0.25)
step_size = 0.5
moreau = 1.0
noise_scale = math.sqrt(2.0 * step_size)


def as_sent(value):

    def short(part):
        return part.astype(jnp.bfloat16) if part.dtype == jnp.float32 else part

    return jax.tree.map(short, value)


def shifted(value, axis, by):
    size = lax.axis_size(axis)
    pairs = [(i, i + by) for i in range(size) if 0 <= i + by < size]
    return lax.ppermute(value, axis, pairs)


def forward_part(tile_set, blocks, row_ids, col_ids, slot_valid, segments):
    block_values = blocks[col_ids]
    product = jnp.einsum("sij,sjk->sik", tile_set, block_values, preferred_element_type=jnp.float32)
    product = product * slot_valid[:, None, None]
    return jax.ops.segment_sum(product, row_ids, num_segments=segments)


def adjoint_part(tile_set, residual, row_ids, col_ids, slot_valid, segments):
    res_rows = residual[row_ids]
    product = jnp.einsum("sij,sik->sjk", tile_set, res_rows, preferred_element_type=jnp.float32)
    product = product * slot_valid[:, None, None]
    return jax.ops.segment_sum(product, col_ids, num_segments=segments)


def tiled_sum(part_fn, operand, tile_set, row_ids, col_ids, slot_count, segments):
    slot_total = tile_set.shape[0]
    slot_valid = (jnp.arange(slot_total) < slot_count).astype(jnp.float32)
    return part_fn(tile_set, operand, row_ids, col_ids, slot_valid, segments)


def z_term(along_z):
    return (
        jnp.concatenate([jnp.zeros_like(along_z[:, :, :1]), along_z[:, :, :-1]], axis=2) - along_z
    )


def primal_from_lower(anchor, dual_field, lower_line, lower_plane):
    term_y = jnp.concatenate([lower_line, dual_field[0, :-1]], axis=0) - dual_field[0]
    term_x = jnp.concatenate([lower_plane, dual_field[1, :, :-1]], axis=1) - dual_field[1]
    term_z = z_term(dual_field[2])
    return anchor - theta_tv * (term_y + term_x + term_z)


def tv_prox(anchor):
    own_lines, own_planes = (anchor.shape[0], anchor.shape[1])
    line_ids = lax.axis_index("row") * own_lines + jnp.arange(own_lines)
    plane_ids = lax.axis_index("col") * own_planes + jnp.arange(own_planes)
    keep_y = (line_ids < own_lines * lax.axis_size("row") - 1).astype(jnp.float32)[
        :, None, None, None
    ]
    keep_x = (plane_ids < own_planes * lax.axis_size("col") - 1).astype(jnp.float32)[
        None, :, None, None
    ]
    dual_field = jnp.zeros((3,) + anchor.shape, jnp.float32)
    for step_index in range(ITERS + 1):
        if step_index == 0:
            lower_line = jnp.zeros_like(dual_field[0, :1])
            lower_plane = jnp.zeros_like(dual_field[1, :, :1])
        else:
            lower_line = shifted(as_sent(dual_field[0, -1:]), "row", 1)
            lower_plane = shifted(as_sent(dual_field[1, :, -1:]), "col", 1)
        primal_field = primal_from_lower(anchor, dual_field, lower_line, lower_plane)
        if step_index == ITERS:
            break
        upper_line = shifted(as_sent(primal_field[:1]), "row", -1)
        upper_plane = shifted(as_sent(primal_field[:, :1]), "col", -1)
        upper_y = jnp.concatenate([primal_field[1:], upper_line], axis=0)
        upper_x = jnp.concatenate([primal_field[:, 1:], upper_plane], axis=1)
        diff_y = (upper_y - primal_field) * keep_y
        diff_x = (upper_x - primal_field) * keep_x
        diff_z = jnp.concatenate(
            [
                primal_field[:, :, 1:] - primal_field[:, :, :-1],
                jnp.zeros_like(primal_field[:, :, :1]),
            ],
            axis=2,
        )
        dual_field = jnp.clip(
            dual_field + tau_dual * jnp.stack([diff_y, diff_x, diff_z]), -1.0, 1.0
        )
    return primal_field


def body(x_state, langevin_noise, observed, data_weight, sens_tiles, tile_rows, tile_cols, counts):
    own_lines, own_planes, tile_depth, chains = x_state.shape
    slab_state = lax.all_gather(x_state.astype(jnp.bfloat16), "row", axis=0, tiled=True)
    blocks = slab_state.reshape(-1, tile_depth, chains)
    col_blocks = blocks.shape[0]
    row_blocks = observed.shape[0] // tile_depth
    tile_set = sens_tiles[0, 0]
    row_ids = tile_rows[0, 0]
    col_ids = tile_cols[0, 0]
    slot_count = counts[0, 0]
    partial_value = tiled_sum(
        forward_part, blocks, tile_set, row_ids, col_ids, slot_count, row_blocks
    )
    predicted = lax.psum(partial_value, "col")
    observed_rows = observed.reshape(row_blocks, tile_depth, 1)
    weight_rows = data_weight.reshape(row_blocks, tile_depth, 1)
    residual = (weight_rows * (predicted - observed_rows)).astype(jnp.bfloat16)
    grad_blocks = tiled_sum(
        adjoint_part, residual, tile_set, row_ids, col_ids, slot_count, col_blocks
    )
    grad_lines = grad_blocks.reshape(-1, own_planes, tile_depth, chains)
    whole_grad = lax.psum(grad_lines, "row")
    gradient = lax.dynamic_slice_in_dim(whole_grad, lax.axis_index("row") * own_lines, own_lines, 0)
    prox_field = tv_prox(x_state)
    return (
        x_state
        - step_size * gradient
        - step_size / moreau * (x_state - prox_field)
        + noise_scale * langevin_noise
    )


def solution(mesh):
    placed = (
        P("row", "col", None, None),
        P("row", "col", None, None),
        P("row"),
        P("row"),
        P("row", "col", None, None, None),
        P("row", "col", None),
        P("row", "col", None),
        P("row", "col"),
    )
    return jax.shard_map(
        body, mesh=mesh, in_specs=placed, out_specs=P("row", "col", None, None), check_vma=False
    )
```

profile of v0, /device:TPU:1, one launch (start us, length us, event | category | flops | bytes accessed | tf_op | source)
XLA Modules:
  0.0 447.4 jit_solution(7203648684436176843)
XLA Ops:
  6.5 1.7 convert_element_type.142
  9.0 0.7 fusion.53
  9.7 70.6 %all-gather.2.cloned.1.call-done = bf16[64,8,128,32]{2,3,1,0:T(8,128)(2,1)} async-done(((bf16[2,8,128,32]{2,3,1,0:T(8,128)(2,1)}), bf16[64,8,128,32]{2,3,1,0:T(8,128)(2,1)}) %all-gather.2.cloned.1.call-update) | async-done | bytes 4194320 | tf_op jit(solution)/shard_map/all_gather | solution.py:107
  80.3 2.8 gather_fusion
  83.1 0.9 fusion.7
  84.1 2.5 scatter_fusion
  86.6 0.6 copy-done.2
  87.4 82.9 %all-reduce.9.cloned.1.call-done = f32[8,128,32]{1,2,0:T(8,128)} async-done(((f32[8,128,32]{1,2,0:T(8,128)}), f32[8,128,32]{1,2,0:T(8,128)}) %all-reduce.9.cloned.1.call-update) | async-done | bytes 131088 | tf_op jit(solution)/shard_map/psum | solution.py:118
  170.2 0.9 multiply_convert_fusion
  171.2 0.6 gather_fusion.1
  171.8 0.5 fusion.13
  172.3 4.3 broadcast_in_dim.4
  176.6 6.2 %scatter_fusion.1 = f32[512,128,32]{1,2,0:T(8,128)} fusion(f32[512,128,32]{1,2,0:T(8,128)} %broadcast_in_dim.4, s32[48]{0:T(128)S(1)} %bitcast.160, f32[48,128,32]{1,2,0:T(8,128)S(1)} %fusion.13), kind=kCustom, calls=%fused_computation.3 | custom fusion | flops 196608 | bytes 2359488 | tf_op jit(solution)/shard_map/scatter-add | solution.py:43
  182.8 0.9 copy-done.3
  183.7 1.4 collective-permute-start.1
  185.1 7.8 %collective-permute-start = (bf16[1,8,128,32]{2,3,1,0:T(8,128)(2,1)S(1)}, bf16[1,8,128,32]{2,3,1,0:T(8,128)(2,1)S(1)}, u32[]{:S(2)}, u32[]{:S(2)}) collective-permute-start(bf16[1,8,128,32]{2,3,1,0:T(8,128)(2,1)S(1)} %slice.184), channel_id=1, source_target_pairs={{8,0},{16,8},{24,16},{32,24},{40,32},{48,40},{56,48},{64,56},{72,6... | collective-permute-start | bytes 196616 | tf_op jit(solution)/shard_map/ppermute | solution.py:29
  193.0 0.1 slice_subtract_fusion.2
  193.2 1.9 collective-permute-done
  195.1 0.1 fusion.42
  195.2 6.4 %collective-permute-start.3 = (bf16[2,1,128,32]{2,3,1,0:T(8,128)(2,1)S(1)}, bf16[2,1,128,32]{2,3,1,0:T(8,128)(2,1)S(1)}, u32[]{:S(2)}, u32[]{:S(2)}) collective-permute-start(bf16[2,1,128,32]{2,3,1,0:T(8,128)(2,1)S(1)} %slice_bitcast_fusion.20), channel_id=1, source_target_pairs={{0,1},{1,2},{2,3},{3,4},{4,5},{5,6},{6,7},{8,9},{9,10},{10,11},{11... | collective-permute-start | bytes 49160 | tf_op jit(solution)/shard_map/ppermute | solution.py:29
  201.6 1.9 collective-permute-start.2
  203.6 0.1 fusion.16
  203.8 1.4 collective-permute-done.2
  205.2 0.2 fusion.57
  205.4 1.3 collective-permute-start.5
  206.7 1.9 collective-permute-start.4
  208.7 0.1 slice_subtract_fusion.1
  208.8 4.2 collective-permute-done.5
  213.0 1.1 collective-permute-done.4
  214.2 0.1 fusion.46
  214.3 6.7 %collective-permute-start.7 = (bf16[2,1,128,32]{2,3,1,0:T(8,128)(2,1)S(1)}, bf16[2,1,128,32]{2,3,1,0:T(8,128)(2,1)S(1)}, u32[]{:S(2)}, u32[]{:S(2)}) collective-permute-start(bf16[2,1,128,32]{2,3,1,0:T(8,128)(2,1)S(1)} %slice_bitcast_fusion.19), channel_id=1, source_target_pairs={{0,1},{1,2},{2,3},{3,4},{4,5},{5,6},{6,7},{8,9},{9,10},{10,11},{11... | collective-permute-start | bytes 49160 | tf_op jit(solution)/shard_map/ppermute | solution.py:29
  221.0 1.9 collective-permute-start.6
  222.9 0.2 fusion.18
  223.2 2.0 collective-permute-done.6
  225.2 0.2 fusion.55
  225.4 1.3 collective-permute-start.9
  226.7 1.9 collective-permute-start.8
  228.7 0.1 slice_subtract_fusion
  228.9 3.2 collective-permute-done.9
  232.1 3.4 collective-permute-done.8
  235.5 0.1 fusion.50
  235.6 5.6 %collective-permute-start.11 = (bf16[2,1,128,32]{2,3,1,0:T(8,128)(2,1)S(1)}, bf16[2,1,128,32]{2,3,1,0:T(8,128)(2,1)S(1)}, u32[]{:S(2)}, u32[]{:S(2)}) collective-permute-start(bf16[2,1,128,32]{2,3,1,0:T(8,128)(2,1)S(1)} %slice_bitcast_fusion.18), channel_id=1, source_target_pairs={{0,1},{1,2},{2,3},{3,4},{4,5},{5,6},{6,7},{8,9},{9,10},{10,11},{11... | collective-permute-start | bytes 49160 | tf_op jit(solution)/shard_map/ppermute | solution.py:29
  241.2 0.1 slice_bitcast_fusion.15
  241.3 1.9 collective-permute-start.10
  243.2 0.3 fusion.20
  243.6 1.7 collective-permute-done.10
  245.3 193.6 %all-reduce.11.cloned.1.call-done = f32[64,8,128,32]{2,3,1,0:T(8,128)} async-done(((f32[64,8,128,32]{2,3,1,0:T(8,128)}), f32[64,8,128,32]{2,3,1,0:T(8,128)}) %all-reduce.11.cloned.1.call-update) | async-done | bytes 8388624 | tf_op jit(solution)/shard_map/psum | solution.py:126
  438.9 2.0 fusion.23
  (73 shorter events, 0.7 us)
Async XLA Ops:
  6.5 76.6 %copy-start = (bf16[1,1,48,128,128]{4,3,2,1,0:T(8,128)(2,1)S(1)}, bf16[1,1,48,128,128]{4,3,2,1,0:T(8,128)(2,1)}, u32[]{:S(2)}) copy-start(bf16[1,1,48,128,128]{4,3,2,1,0:T(8,128)(2,1)} %param.12) | copy-start | bytes 4718596
  6.5 73.7 %all-gather.2.cloned.1.call-start = ((), (), s32[]{:S(2)}) async-start(), calls=%async_computation | async-start | bytes 4325376 | tf_op jit(solution)/shard_map/all_gather | solution.py:107
  8.3 161.9 %all-reduce.9.cloned.1.call-start = ((), (), s32[]{:S(2)}) async-start(), calls=%async_computation.1 | async-start | bytes 262144 | tf_op jit(solution)/shard_map/psum | solution.py:118
  83.1 1.0 copy-start.6
  84.0 86.2 %copy-start.4 = (f32[1024]{0:T(1024)S(1)}, f32[1024]{0:T(1024)}, u32[]{:S(2)}) copy-start(f32[1024]{0:T(1024)} %param.10) | copy-start | bytes 12292
  84.0 86.2 %copy-start.5 = (f32[1024]{0:T(1024)S(1)}, f32[1024]{0:T(1024)}, u32[]{:S(2)}) copy-start(f32[1024]{0:T(1024)} %param.11) | copy-start | bytes 12292
  86.6 0.6 copy-start.2
  87.3 351.6 %all-reduce.11.cloned.1.call-start = ((), (), s32[]{:S(2)}) async-start(), calls=%async_computation.2 | async-start | bytes 16777216 | tf_op jit(solution)/shard_map/psum | solution.py:126
  172.3 4.3 copy-start.7
  182.8 0.9 copy-start.3
  182.8 10.2 %copy-start.1 = (f32[2,8,128,32]{2,3,1,0:T(8,128)S(1)}, f32[2,8,128,32]{2,3,1,0:T(8,128)}, u32[]{:S(2)}) copy-start(f32[2,8,128,32]{2,3,1,0:T(8,128)} %param.8) | copy-start | bytes 786436
  183.7 11.4 %slice-start = ((f32[2,8,128,32]{2,3,1,0:T(8,128)}), f32[1,8,128,32]{2,3,1,0:T(8,128)S(1)}, s32[]{:S(2)}) async-start(f32[2,8,128,32]{2,3,1,0:T(8,128)} %param.8), calls=%async_computation.3 | async-start | bytes 262144 | tf_op jit(solution)/shard_map/slice | solution.py:88
  183.7 11.4 %slice-start.1 = ((f32[2,8,128,32]{2,3,1,0:T(8,128)}), f32[2,7,128,32]{2,3,1,0:T(8,128)S(1)}, s32[]{:S(2)}) async-start(f32[2,8,128,32]{2,3,1,0:T(8,128)} %param.8), calls=%async_computation.4 | async-start | bytes 458752 | tf_op jit(solution)/shard_map/slice | solution.py:89
  183.7 9.5 %collective-permute-start.1 = (bf16[2,1,128,32]{2,3,1,0:T(8,128)(2,1)S(1)}, bf16[2,1,128,32]{2,3,1,0:T(8,128)(2,1)S(1)}, u32[]{:S(2)}, u32[]{:S(2)}) collective-permute-start(bf16[2,1,128,32]{2,3,1,0:T(8,128)(2,1)S(1)} %slice.185), channel_id=1, source_target_pairs={{1,0},{2,1},{3,2},{4,3},{5,4},{6,5},{7,6},{9,8},{10,9},{11,10},{12... | collective-permute-start | bytes 49160 | tf_op jit(solution)/shard_map/ppermute | solution.py:29
  185.1 9.9 %collective-permute-start = (bf16[1,8,128,32]{2,3,1,0:T(8,128)(2,1)S(1)}, bf16[1,8,128,32]{2,3,1,0:T(8,128)(2,1)S(1)}, u32[]{:S(2)}, u32[]{:S(2)}) collective-permute-start(bf16[1,8,128,32]{2,3,1,0:T(8,128)(2,1)S(1)} %slice.184), channel_id=1, source_target_pairs={{8,0},{16,8},{24,16},{32,24},{40,32},{48,40},{56,48},{64,56},{72,6... | collective-permute-start | bytes 196616 | tf_op jit(solution)/shard_map/ppermute | solution.py:29
  195.2 8.5 %collective-permute-start.3 = (bf16[2,1,128,32]{2,3,1,0:T(8,128)(2,1)S(1)}, bf16[2,1,128,32]{2,3,1,0:T(8,128)(2,1)S(1)}, u32[]{:S(2)}, u32[]{:S(2)}) collective-permute-start(bf16[2,1,128,32]{2,3,1,0:T(8,128)(2,1)S(1)} %slice_bitcast_fusion.20), channel_id=1, source_target_pairs={{0,1},{1,2},{2,3},{3,4},{4,5},{5,6},{6,7},{8,9},{9,10},{10,11},{11... | collective-permute-start | bytes 49160 | tf_op jit(solution)/shard_map/ppermute | solution.py:29
  201.6 3.6 collective-permute-start.2
  205.4 7.6 %collective-permute-start.5 = (bf16[2,1,128,32]{2,3,1,0:T(8,128)(2,1)S(1)}, bf16[2,1,128,32]{2,3,1,0:T(8,128)(2,1)S(1)}, u32[]{:S(2)}, u32[]{:S(2)}) collective-permute-start(bf16[2,1,128,32]{2,3,1,0:T(8,128)(2,1)S(1)} %slice.197), channel_id=1, source_target_pairs={{1,0},{2,1},{3,2},{4,3},{5,4},{6,5},{7,6},{9,8},{10,9},{11,10},{12... | collective-permute-start | bytes 49160 | tf_op jit(solution)/shard_map/ppermute | solution.py:29
  206.7 7.4 %collective-permute-start.4 = (bf16[1,8,128,32]{2,3,1,0:T(8,128)(2,1)S(1)}, bf16[1,8,128,32]{2,3,1,0:T(8,128)(2,1)S(1)}, u32[]{:S(2)}, u32[]{:S(2)}) collective-permute-start(bf16[1,8,128,32]{2,3,1,0:T(8,128)(2,1)S(1)} %slice.195), channel_id=1, source_target_pairs={{8,0},{16,8},{24,16},{32,24},{40,32},{48,40},{56,48},{64,56},{72,6... | collective-permute-start | bytes 196616 | tf_op jit(solution)/shard_map/ppermute | solution.py:29
  214.3 8.9 %collective-permute-start.7 = (bf16[2,1,128,32]{2,3,1,0:T(8,128)(2,1)S(1)}, bf16[2,1,128,32]{2,3,1,0:T(8,128)(2,1)S(1)}, u32[]{:S(2)}, u32[]{:S(2)}) collective-permute-start(bf16[2,1,128,32]{2,3,1,0:T(8,128)(2,1)S(1)} %slice_bitcast_fusion.19), channel_id=1, source_target_pairs={{0,1},{1,2},{2,3},{3,4},{4,5},{5,6},{6,7},{8,9},{9,10},{10,11},{11... | collective-permute-start | bytes 49160 | tf_op jit(solution)/shard_map/ppermute | solution.py:29
  221.0 4.2 collective-permute-start.6
  225.4 6.7 %collective-permute-start.9 = (bf16[2,1,128,32]{2,3,1,0:T(8,128)(2,1)S(1)}, bf16[2,1,128,32]{2,3,1,0:T(8,128)(2,1)S(1)}, u32[]{:S(2)}, u32[]{:S(2)}) collective-permute-start(bf16[2,1,128,32]{2,3,1,0:T(8,128)(2,1)S(1)} %slice.211), channel_id=1, source_target_pairs={{1,0},{2,1},{3,2},{4,3},{5,4},{6,5},{7,6},{9,8},{10,9},{11,10},{12... | collective-permute-start | bytes 49160 | tf_op jit(solution)/shard_map/ppermute | solution.py:29
  226.7 8.7 %collective-permute-start.8 = (bf16[1,8,128,32]{2,3,1,0:T(8,128)(2,1)S(1)}, bf16[1,8,128,32]{2,3,1,0:T(8,128)(2,1)S(1)}, u32[]{:S(2)}, u32[]{:S(2)}) collective-permute-start(bf16[1,8,128,32]{2,3,1,0:T(8,128)(2,1)S(1)} %slice.209), channel_id=1, source_target_pairs={{8,0},{16,8},{24,16},{32,24},{40,32},{48,40},{56,48},{64,56},{72,6... | collective-permute-start | bytes 196616 | tf_op jit(solution)/shard_map/ppermute | solution.py:29
  235.6 8.0 %collective-permute-start.11 = (bf16[2,1,128,32]{2,3,1,0:T(8,128)(2,1)S(1)}, bf16[2,1,128,32]{2,3,1,0:T(8,128)(2,1)S(1)}, u32[]{:S(2)}, u32[]{:S(2)}) collective-permute-start(bf16[2,1,128,32]{2,3,1,0:T(8,128)(2,1)S(1)} %slice_bitcast_fusion.18), channel_id=1, source_target_pairs={{0,1},{1,2},{2,3},{3,4},{4,5},{5,6},{6,7},{8,9},{9,10},{10,11},{11... | collective-permute-start | bytes 49160 | tf_op jit(solution)/shard_map/ppermute | solution.py:29
  241.3 4.0 collective-permute-start.10
Sparse Core Ops, SparseCore 0:
  9.2 71.0 all-gather.1
  87.4 82.7 all-reduce.8
  182.9 255.9 all-reduce.10
where the time goes:
time: 448 us; the launch traced here: 447 us
  waiting for transfers between devices  366 us (82%)
  starting transfers between devices  40.1 us (9%)
  other arithmetic  16 us (4%)
  between operations  14.4 us (3%)
  local copies, waits for them, and re-layouts  9.57 us (2%)
    psum x1, waiting for transfers between devices, body(): whole_grad = lax.psum(grad_lines, 'row')  194 us
    psum x1, waiting for transfers between devices, body(): predicted = lax.psum(partial_value, 'col')  82.9 us
    all_gather x1, waiting for transfers between devices, body(): lax.all_gather(x_state.astype(jnp.bfloat16), 'row', axis=0, tiled=True)  70.6 us
    ppermute x12, starting transfers between devices, shifted(): return lax.ppermute(value, axis, pairs)  40 us
    ppermute x12, waiting for transfers between devices, shifted(): return lax.ppermute(value, axis, pairs)  18.8 us
  transfers between devices with their start and end apart: 15, of which 11 were waited for; matrix products, arithmetic and copies ran while one was open for 1% of the time, Pallas kernels for 0%

commit v1 on v0

v1 whole, which is shorter than its diff:
```python
import functools
import math

import jax
import jax.numpy as jnp
from jax import lax
from jax.experimental import pallas as pl
from jax.experimental.pallas import tpu as pltpu
from jax.sharding import PartitionSpec as P

theta_tv = 0.25
tau_dual = 1.0 / (12.0 * 0.25)
step_size = 0.5
moreau = 1.0
noise_scale = math.sqrt(2.0 * step_size)

F32 = jnp.float32
BF16 = jnp.bfloat16

N_Z = 8
QUAD = 4
N_ROW = N_Z * QUAD
N_COL = 8
OWN_Y = 2
OWN_X = 8
OWN = OWN_Y * OWN_X
PLANE = QUAD * OWN
HALF = PLANE // 2
LINES = N_Z * PLANE
CH = 32
NZ = 128
RB = 8
SLOTS = 48
GROUP = 8
HALO = 3
WIDE_Y = OWN_Y + 2 * HALO
WIDE_X = OWN_X + 2 * HALO
TOP_Y = N_ROW * OWN_Y - 1
TOP_X = N_COL * OWN_X - 1
SENT = HALF + 3 * PLANE

CORE = [(i, i ^ 1) for i in range(N_ROW)]
X_LO = [(i, i ^ 2) for i in range(N_ROW)]
RING = [(i, (i + (QUAD if i % 2 == 0 else -QUAD)) % N_ROW) for i in range(N_ROW)]
QUADS = [[QUAD * z + q for q in range(QUAD)] for z in range(N_Z)]

VMEM = pl.BlockSpec(memory_space=pltpu.VMEM)
SMEM = pl.BlockSpec(memory_space=pltpu.SMEM)


def over_row(value, pairs):
    return lax.ppermute(value, "row", pairs)


def over_col(value, pairs):
    return lax.ppermute(value, "col", pairs)


def own_half(value, pick):
    half = value.shape[0] // 2
    return jnp.where(pick == 0, value[:half], value[half:])


def params():
    return pltpu.CompilerParams(vmem_limit_bytes=48 * 2**20)


def forward_kernel(place, rows, cols, count, tiles, own, *rest):
    arrived, out, field, total = rest[:-3], rest[-3], rest[-2], rest[-1]
    z = place[0]
    core = place[1]
    up = 1 - 2 * core

    def keep(ref, steps, half):
        plane = lax.rem(z + steps + 2 * N_Z, N_Z)
        field[pl.ds(plane * PLANE + half * HALF, HALF)] = ref[...]

    field[pl.ds(z * PLANE, PLANE)] = own[...]
    for step in range(1, 5):
        keep(arrived[step - 1], -step * up, core)
        keep(arrived[step + 3], step * up, 1 - core)
    for step in range(1, 4):
        keep(arrived[step + 7], -step * up, 1 - core)
        keep(arrived[step + 10], step * up, core)
    total[...] = jnp.zeros_like(total)
    used = count[0]

    def group(index, carry):
        terms = []
        for u in range(GROUP):
            slot = index * GROUP + u
            term = lax.dot_general(
                field[cols[slot]], tiles[slot], (((1,), (1,)), ((), ())), preferred_element_type=F32
            )
            terms.append(jnp.where(slot < used, term, 0.0))
        for u in range(GROUP):
            total[rows[index * GROUP + u]] += terms[u]
        return carry

    lax.fori_loop(0, (used + GROUP - 1) // GROUP, group, 0)
    out[...] = total[...].astype(BF16)


def forward(place, rows, cols, count, tiles, own, arrived):
    return pl.pallas_call(
        forward_kernel,
        out_shape=jax.ShapeDtypeStruct((RB, CH, NZ), BF16),
        in_specs=[SMEM] * 4 + [VMEM] * (2 + len(arrived)),
        out_specs=VMEM,
        scratch_shapes=[pltpu.VMEM((LINES, CH, NZ), BF16), pltpu.VMEM((RB, CH, NZ), F32)],
        compiler_params=params(),
        cost_estimate=pl.CostEstimate(
            flops=2 * SLOTS * NZ * NZ * CH, bytes_accessed=12 * 2**20, transcendentals=0
        ),
        name="forward_tiles",
    )(place, rows, cols, count, tiles, own, *arrived)


def adjoint_kernel(
    place, rows, cols, count, tiles, observed, weight, *rest
):
    parts, (send, mine, own, residual, total, first) = rest[:4], rest[4:]
    z = place[0]
    core = place[1]
    used = count[0]
    for b in range(RB):
        predicted = parts[0][b].astype(F32)
        for part in parts[1:]:
            predicted = predicted + part[b].astype(F32)
        residual[b] = (weight[pl.ds(b, 1), :] * (predicted - observed[pl.ds(b, 1), :])).astype(BF16)
    total[...] = jnp.zeros_like(total)
    send[...] = jnp.zeros_like(send)
    mine[...] = jnp.zeros_like(mine)
    own[...] = jnp.zeros_like(own)

    def mark(index, carry):
        slot = used - 1 - index
        first[cols[slot]] = slot
        return carry

    lax.fori_loop(0, used, mark, 0)

    def group(index, carry):
        terms = []
        for u in range(GROUP):
            slot = index * GROUP + u
            term = lax.dot_general(
                residual[rows[slot]], tiles[slot], (((1,), (0,)), ((), ())), preferred_element_type=F32
            )
            terms.append(term)
        for u in range(GROUP):
            slot = index * GROUP + u

            @pl.when(slot < used)
            def _():
                total[first[cols[slot]]] += terms[u]

        return carry

    lax.fori_loop(0, (used + GROUP - 1) // GROUP, group, 0)

    def place_line(slot, carry):
        line = cols[slot]
        value = total[first[line]].astype(BF16)
        plane = line // PLANE
        inner = lax.rem(line, PLANE)
        half = inner // HALF
        away = lax.rem(plane - z + N_Z, N_Z)
        carrier = jnp.where(away == 4, half, jnp.where(away < 4, 0, 1))
        steps = jnp.where(carrier == 0, away, N_Z - away)
        where = jnp.where(half == carrier, 0, HALF) + lax.rem(inner, HALF)
        where = jnp.where(steps == 4, where, HALF + (3 - steps) * PLANE + where)

        @pl.when(away == 0)
        def _():
            own[inner] = value

        @pl.when((away != 0) & (carrier == core))
        def _():
            mine[where] = value

        @pl.when((away != 0) & (carrier != core))
        def _():
            send[where] = value

        return carry

    lax.fori_loop(0, used, place_line, 0)


def adjoint(place, rows, cols, count, tiles, observed, weight, parts):
    return pl.pallas_call(
        adjoint_kernel,
        out_shape=[
            jax.ShapeDtypeStruct((SENT, CH, NZ), BF16),
            jax.ShapeDtypeStruct((SENT, CH, NZ), BF16),
            jax.ShapeDtypeStruct((PLANE, CH, NZ), BF16),
        ],
        in_specs=[SMEM] * 4 + [VMEM] * (3 + len(parts)),
        out_specs=[VMEM] * 3,
        scratch_shapes=[
            pltpu.VMEM((RB, CH, NZ), BF16),
            pltpu.VMEM((SLOTS, CH, NZ), F32),
            pltpu.SMEM((LINES,), jnp.int32),
        ],
        compiler_params=params(),
        cost_estimate=pl.CostEstimate(
            flops=2 * SLOTS * NZ * NZ * CH, bytes_accessed=12 * 2**20, transcendentals=0
        ),
        name="adjoint_tiles",
    )(place, rows, cols, count, tiles, observed, weight, *parts)


def prox_kernel(start, wide, low, high, anchor, noise, out, field, primal, dual_y, dual_x, dual_z):
    y0 = start[0]
    x0 = start[1]
    lane = lax.broadcasted_iota(jnp.int32, (CH, NZ), 1)
    not_first = lane > 0
    not_last = lane < NZ - 1

    def load_line(y, carry):
        for x in range(OWN_X):
            field[y, HALO + x] = wide[y, x].astype(F32)
        for x in range(HALO):
            field[y, x] = low[y, x].astype(F32)
            field[y, HALO + OWN_X + x] = high[y, x].astype(F32)
        return carry

    lax.fori_loop(0, WIDE_Y, load_line, 0)
    for y in range(OWN_Y):
        for x in range(OWN_X):
            field[HALO + y, HALO + x] = anchor[y, x]

    def primal_at(y, x):
        along_z = dual_z[y, x]
        lower_z = jnp.where(not_first, pltpu.roll(along_z, 1, 1), 0.0)
        term = (dual_y[y - 1, x] - dual_y[y, x]) + (dual_x[y, x - 1] - dual_x[y, x]) + (lower_z - along_z)
        return field[y, x] - theta_tv * term

    for step in range(3):
        source = field if step == 0 else primal
        if step:

            def primal_line(y, carry, step=step):
                for x in range(step, WIDE_X - step):
                    primal[y, x] = primal_at(y, x)
                return carry

            lax.fori_loop(step, WIDE_Y - step, primal_line, 0)

        def dual_line(y, carry, step=step, source=source):
            line = y0 + y
            rate_y = jnp.where((line >= 0) & (line < TOP_Y), tau_dual, 0.0)
            for x in range(step, WIDE_X - 1 - step):
                plane = x0 + x
                rate_x = jnp.where((plane >= 0) & (plane < TOP_X), tau_dual, 0.0)
                here = source[y, x]
                diff_y = rate_y * (source[y + 1, x] - here)
                diff_x = rate_x * (source[y, x + 1] - here)
                diff_z = jnp.where(not_last, tau_dual * (pltpu.roll(here, NZ - 1, 1) - here), 0.0)
                if step:
                    diff_y = dual_y[y, x] + diff_y
                    diff_x = dual_x[y, x] + diff_x
                    diff_z = dual_z[y, x] + diff_z
                dual_y[y, x] = jnp.clip(diff_y, -1.0, 1.0)
                dual_x[y, x] = jnp.clip(diff_x, -1.0, 1.0)
                dual_z[y, x] = jnp.clip(diff_z, -1.0, 1.0)
            return carry

        lax.fori_loop(step, WIDE_Y - 1 - step, dual_line, 0)
    for y in range(OWN_Y):
        for x in range(OWN_X):
            here = field[HALO + y, HALO + x]
            prox = primal_at(HALO + y, HALO + x)
            out[y, x] = here - step_size / moreau * (here - prox) + noise_scale * noise[y, x]


def prox_step(start, wide, low, high, anchor, noise):
    region = pltpu.VMEM((WIDE_Y, WIDE_X, CH, NZ), F32)
    return pl.pallas_call(
        prox_kernel,
        out_shape=jax.ShapeDtypeStruct((OWN_Y, OWN_X, CH, NZ), F32),
        in_specs=[SMEM] + [VMEM] * 5,
        out_specs=VMEM,
        scratch_shapes=[region] * 5,
        compiler_params=params(),
        cost_estimate=pl.CostEstimate(flops=2**24, bytes_accessed=12 * 2**20, transcendentals=0),
        name="tv_prox",
    )(start, wide, low, high, anchor, noise)


def gather_slab(own, core):
    plane = lax.all_gather(own, "row", axis=0, tiled=True, axis_index_groups=QUADS)
    long, short = own_half(plane, core), own_half(plane, 1 - core)
    mine_long, mine_short = [], []
    for step in range(4):
        long = over_row(long, RING)
        mine_long.append(long)
        if step < 3:
            short = over_row(short, RING)
            mine_short.append(short)
    their_long = [over_row(v, CORE) for v in mine_long]
    their_short = [over_row(v, CORE) for v in mine_short]
    return plane, mine_long, their_long, mine_short, their_short


def add(*parts):
    total = parts[0].astype(F32)
    for part in parts[1:]:
        total = total + part.astype(F32)
    return total.astype(BF16)


def scatter_gradient(send, mine, own, x_lo, core):
    came = over_row(send, CORE)

    def chip(start):
        return add(mine[start : start + HALF], came[start : start + HALF])

    long = over_row(chip(0), RING)
    short = over_row(chip(2 * HALF), RING)
    for step in (1, 2):
        long = over_row(add(long, chip((2 * step - 1) * HALF)), RING)
        short = over_row(add(short, chip((2 * step + 2) * HALF)), RING)
    long = over_row(add(long, chip(5 * HALF)), RING)
    low = add(jnp.where(core == 0, long, short), own[:HALF])
    high = add(jnp.where(core == 0, short, long), own[HALF:])
    kept = jnp.where(x_lo == 0, low, high)
    half = add(kept, over_row(jnp.where(x_lo == 0, high, low), X_LO))
    other = over_row(own_half(half, 1 - core), CORE)
    return own_half(half, core).astype(F32) + other.astype(F32)


def body(x_state, langevin_noise, observed, data_weight, sens_tiles, tile_rows, tile_cols, counts):
    row = lax.axis_index("row")
    col = lax.axis_index("col")
    z, x_lo, core = row // QUAD, (row // 2) % 2, row % 2
    place = jnp.stack([z, core]).astype(jnp.int32)
    state = x_state.transpose(0, 1, 3, 2)
    noise = langevin_noise.transpose(0, 1, 3, 2)
    own = state.reshape(OWN, CH, NZ).astype(BF16)
    tiles = sens_tiles[0, 0]
    rows, cols, count = tile_rows[0, 0], tile_cols[0, 0], counts[0]

    plane, mine_long, their_long, mine_short, their_short = gather_slab(own, core)
    part = forward(
        place, rows, cols, count, tiles, plane, mine_long + their_long + mine_short + their_short
    )
    part = add(part, over_col(part, [(i, i ^ 1) for i in range(N_COL)]))
    parts = [part] + [
        over_col(part, [(i, (i + by) % N_COL) for i in range(N_COL)]) for by in (2, 4, 6)
    ]
    send, mine, kept = adjoint(
        place,
        rows,
        cols,
        count,
        tiles,
        observed.reshape(RB, NZ),
        data_weight.reshape(RB, NZ),
        parts,
    )

    below_low = jnp.where(core == 0, mine_long[0], their_long[0])
    below_high = jnp.where(core == 0, mine_short[0], their_short[0])
    above_low = jnp.where(core == 0, their_short[0], mine_short[0])
    above_high = jnp.where(core == 0, their_long[0], mine_long[0])
    near = jnp.concatenate([below_low, below_high, plane, above_low, above_high], axis=0)
    first = PLANE + (row % QUAD) * OWN - HALO * OWN_X
    wide = lax.dynamic_slice_in_dim(near, first, WIDE_Y * OWN_X, 0)
    wide = wide.reshape(WIDE_Y, OWN_X, CH, NZ)
    low = over_col(wide[:, OWN_X - HALO :], [(i, i + 1) for i in range(N_COL - 1)])
    high = over_col(wide[:, :HALO], [(i + 1, i) for i in range(N_COL - 1)])
    start = jnp.stack([row * OWN_Y - HALO, col * OWN_X - HALO]).astype(jnp.int32)
    base = prox_step(start, wide, low, high, state, noise)

    gradient = scatter_gradient(send, mine, kept, x_lo, core)
    out = base - step_size * gradient.reshape(OWN_Y, OWN_X, CH, NZ)
    return out.transpose(0, 1, 3, 2)


def solution(mesh):
    placed = (
        P("row", "col", None, None),
        P("row", "col", None, None),
        P("row"),
        P("row"),
        P("row", "col", None, None, None),
        P("row", "col", None),
        P("row", "col", None),
        P("row", "col"),
    )
    return jax.shard_map(
        body, mesh=mesh, in_specs=placed, out_specs=P("row", "col", None, None), check_vma=False
    )
```

time: 448 us -> 133 us (0.30)
  the two profiles are of different devices: /device:TPU:1 before, /device:TPU:24 now
where the time goes in v1:
time: 133 us; the launch traced here: 131 us
  waiting for transfers between devices  80 us (60%)
  starting transfers between devices  28.9 us (22%)
  Pallas kernels  7.71 us (6%)
  blocking collectives  7.17 us (5%)
  other arithmetic  6.46 us (5%)
    ppermute x24, waiting for transfers between devices, over_row(): return lax.ppermute(value, 'row', pairs)  67.3 us
    ppermute x6, starting transfers between devices, over_col(): return lax.ppermute(value, 'col', pairs)  17.5 us
    ppermute x6, waiting for transfers between devices, over_col(): return lax.ppermute(value, 'col', pairs)  12.7 us
    ppermute x24, starting transfers between devices, over_row(): return lax.ppermute(value, 'row', pairs)  11.4 us
    all_gather x1, blocking collectives, gather_slab(): lax.all_gather(own, 'row', axis=0, tiled=True, axis_index_groups=QUADS)  7.17 us
    pallas_call x1, Pallas kernels, prox_step(): pl.pallas_call(prox_kernel, out_shape=jax.ShapeDtypeStruct((OWN_Y, OWN_X,...  3.88 us
    convert_element_type x6, other arithmetic, add(): return total.astype(BF16)  3.81 us
  transfers between devices with their start and end apart: 30, of which 21 were waited for; matrix products, arithmetic and copies ran while one was open for 1% of the time, Pallas kernels for 3%

profile of v1, /device:TPU:24, one launch (start us, length us, event | category | flops | bytes accessed | tf_op | source)
XLA Modules:
  0.0 131.4 jit_solution(3787585748463264337)
XLA Ops:
  0.0 1.1 bitcast_convert_fusion
  1.1 7.2 %all_gather.3.own = bf16[64,32,128]{2,1,0:T(8,128)(2,1)S(1)} all-gather(bf16[16,32,128]{2,1,0:T(8,128)(2,1)S(1)} %bitcast.33), channel_id=1, replica_groups={{0,8,16,24},{32,40,48,56},{64,72,80,88},{96,104,112,120},{128,136,144,1..., dimensions={0}, use_global_device_ids=true | all-gather | bytes 655360 | tf_op jit(solution)/shard_map/all_gather | solution.py:293
  8.3 2.0 %collective-permute-start = (bf16[32,32,128]{2,1,0:T(8,128)(2,1)S(1)}, bf16[32,32,128]{2,1,0:T(8,128)(2,1)S(1)}, u32[]{:S(2)}, u32[]{:S(2)}) collective-permute-start(bf16[32,32,128]{2,1,0:T(8,128)(2,1)S(1)} %get-tuple-element.23), channel_id=1, source_target_pairs={{0,32},{8,232},{16,48},{24,248},{32,64},{40,8},{48,80},{56,24},{64... | collective-permute-start | bytes 786440 | tf_op jit(solution)/shard_map/ppermute | solution.py:52
  10.3 1.9 %collective-permute-start.2 = (bf16[32,32,128]{2,1,0:T(8,128)(2,1)S(1)}, bf16[32,32,128]{2,1,0:T(8,128)(2,1)S(1)}, u32[]{:S(2)}, u32[]{:S(2)}) collective-permute-start(bf16[32,32,128]{2,1,0:T(8,128)(2,1)S(1)} %get-tuple-element.22), channel_id=1, source_target_pairs={{0,32},{8,232},{16,48},{24,248},{32,64},{40,8},{48,80},{56,24},{64... | collective-permute-start | bytes 786440 | tf_op jit(solution)/shard_map/ppermute | solution.py:52
  12.3 6.4 %collective-permute-done.rest_0_ = bf16[32,32,128]{2,1,0:T(8,128)(2,1)S(1)} collective-permute-done((bf16[32,32,128]{2,1,0:T(8,128)(2,1)S(1)}, bf16[32,32,128]{2,1,0:T(8,128)(2,1)S(1)}, u32[]{:S(2)}, u32[]{:S(2)}) %collective-permute-start) | collective-permute-done | bytes 262176 | tf_op jit(solution)/shard_map/ppermute | solution.py:52
  18.6 2.8 %collective-permute-done.2.rest_8_ = bf16[32,32,128]{2,1,0:T(8,128)(2,1)S(1)} collective-permute-done((bf16[32,32,128]{2,1,0:T(8,128)(2,1)S(1)}, bf16[32,32,128]{2,1,0:T(8,128)(2,1)S(1)}, u32[]{:S(2)}, u32[]{:S(2)}) %collective-permute-start.2) | collective-permute-done | bytes 262176 | tf_op jit(solution)/shard_map/ppermute | solution.py:52
  21.4 4.8 %collective-permute-done.6.rest_1_ = bf16[32,32,128]{2,1,0:T(8,128)(2,1)S(1)} collective-permute-done((bf16[32,32,128]{2,1,0:T(8,128)(2,1)S(1)}, bf16[32,32,128]{2,1,0:T(8,128)(2,1)S(1)}, u32[]{:S(2)}, u32[]{:S(2)}) %collective-permute-start.6) | collective-permute-done | bytes 262176 | tf_op jit(solution)/shard_map/ppermute | solution.py:52
  26.2 1.0 collective-permute-start.3
  27.2 1.9 %collective-permute-done.12.rest_9_ = bf16[32,32,128]{2,1,0:T(8,128)(2,1)} collective-permute-done((bf16[32,32,128]{2,1,0:T(8,128)(2,1)S(1)}, bf16[32,32,128]{2,1,0:T(8,128)(2,1)}, u32[]{:S(2)}, u32[]{:S(2)}) %collective-permute-start.12) | collective-permute-done | bytes 262176 | tf_op jit(solution)/shard_map/ppermute | solution.py:52
  29.1 4.8 %collective-permute-done.7.rest_2_ = bf16[32,32,128]{2,1,0:T(8,128)(2,1)} collective-permute-done((bf16[32,32,128]{2,1,0:T(8,128)(2,1)S(1)}, bf16[32,32,128]{2,1,0:T(8,128)(2,1)}, u32[]{:S(2)}, u32[]{:S(2)}) %collective-permute-start.7) | collective-permute-done | bytes 262176 | tf_op jit(solution)/shard_map/ppermute | solution.py:52
  33.9 0.5 collective-permute-start.9
  34.5 2.5 %collective-permute-done.13.rest_10_ = bf16[32,32,128]{2,1,0:T(8,128)(2,1)} collective-permute-done((bf16[32,32,128]{2,1,0:T(8,128)(2,1)}, bf16[32,32,128]{2,1,0:T(8,128)(2,1)}, u32[]{:S(2)}, u32[]{:S(2)}) %collective-permute-start.13) | collective-permute-done | bytes 262176 | tf_op jit(solution)/shard_map/ppermute | solution.py:52
  37.0 4.8 %collective-permute-done.8.rest_3_ = bf16[32,32,128]{2,1,0:T(8,128)(2,1)} collective-permute-done((bf16[32,32,128]{2,1,0:T(8,128)(2,1)}, bf16[32,32,128]{2,1,0:T(8,128)(2,1)}, u32[]{:S(2)}, u32[]{:S(2)}) %collective-permute-start.8) | collective-permute-done | bytes 262176 | tf_op jit(solution)/shard_map/ppermute | solution.py:52
  42.6 1.1 collective-permute-done.11.rest_7_
  43.7 2.2 %forward_tiles.1 = bf16[8,32,128]{2,1,0:T(8,128)(2,1)S(1)} custom-call(s32[2]{0:T(128)S(1)} %pad_add_fusion.1.place, s32[48]{0:T(128)S(1)} %bitcast.28, s32[48]{0:T(128)S(1)} %bitcast.30, s32[1]{0:T(128)} %bitcast.18.count, bf16[48,128,128]{2,1,0:T(8,128)(2,1)S(1)} %bitcast.20, bf16[64,32,128]{2,1,0:T(8,128)(2,1)S(1)} %all_gather.3.own, ...), custom_call_target="tpu_custom_call" | custom-call | flops 50331648 | bytes 12582912 | tf_op jit(solution)/shard_map/forward_tiles/pallas_call | solution.py:105
  45.9 4.1 %collective-permute-start.16 = (bf16[8,32,128]{2,1,0:T(8,128)(2,1)S(1)}, bf16[8,32,128]{2,1,0:T(8,128)(2,1)S(1)}, u32[]{:S(2)}, u32[]{:S(2)}) collective-permute-start(bf16[8,32,128]{2,1,0:T(8,128)(2,1)S(1)} %forward_tiles.1), channel_id=1, source_target_pairs={{0,1},{1,0},{2,3},{3,2},{4,5},{5,4},{6,7},{7,6},{8,9},{9,8},{10,11... | collective-permute-start | bytes 196616 | tf_op jit(solution)/shard_map/ppermute | solution.py:56
  50.0 2.4 %collective-permute-done.16 = bf16[8,32,128]{2,1,0:T(8,128)(2,1)S(1)} collective-permute-done((bf16[8,32,128]{2,1,0:T(8,128)(2,1)S(1)}, bf16[8,32,128]{2,1,0:T(8,128)(2,1)S(1)}, u32[]{:S(2)}, u32[]{:S(2)}) %collective-permute-start.16) | collective-permute-done | bytes 65568 | tf_op jit(solution)/shard_map/ppermute | solution.py:56
  52.4 0.8 collective-permute-start.19
  53.2 1.6 %collective-permute-start.18 = (bf16[8,32,128]{2,1,0:T(8,128)(2,1)S(1)}, bf16[8,32,128]{2,1,0:T(8,128)(2,1)S(1)}, u32[]{:S(2)}, u32[]{:S(2)}) collective-permute-start(bf16[8,32,128]{2,1,0:T(8,128)(2,1)S(1)} %add_convert_fusion.15.rest_0_), channel_id=1, source_target_pairs={{0,4},{1,5},{2,6},{3,7},{4,0},{5,1},{6,2},{7,3},{8,12},{9,13},{10,... | collective-permute-start | bytes 196616 | tf_op jit(solution)/shard_map/ppermute | solution.py:56
  54.8 2.0 %collective-permute-start.17 = (bf16[8,32,128]{2,1,0:T(8,128)(2,1)S(1)}, bf16[8,32,128]{2,1,0:T(8,128)(2,1)S(1)}, u32[]{:S(2)}, u32[]{:S(2)}) collective-permute-start(bf16[8,32,128]{2,1,0:T(8,128)(2,1)S(1)} %add_convert_fusion.15.rest_0_), channel_id=1, source_target_pairs={{0,2},{1,3},{2,4},{3,5},{4,6},{5,7},{6,0},{7,1},{8,10},{9,11},{10,... | collective-permute-start | bytes 196616 | tf_op jit(solution)/shard_map/ppermute | solution.py:56
  56.8 2.3 %collective-permute-done.19.rest_3_ = bf16[8,32,128]{2,1,0:T(8,128)(2,1)S(1)} collective-permute-done((bf16[8,32,128]{2,1,0:T(8,128)(2,1)S(1)}, bf16[8,32,128]{2,1,0:T(8,128)(2,1)S(1)}, u32[]{:S(2)}, u32[]{:S(2)}) %collective-permute-start.19) | collective-permute-done | bytes 65568 | tf_op jit(solution)/shard_map/ppermute | solution.py:56
  59.1 0.4 collective-permute-done.17.rest_1_
  59.5 1.7 %adjoint_tiles.1 = (bf16[224,32,128]{2,1,0:T(8,128)(2,1)S(1)}, bf16[224,32,128]{2,1,0:T(8,128)(2,1)S(1)}, bf16[64,32,128]{2,1,0:T(8,128)(2,1)S(1)}) custom-call(s32[2]{0:T(128)S(1)} %pad_add_fusion.1.place, s32[48]{0:T(128)S(1)} %bitcast.29, s32[48]{0:T(128)S(1)} %bitcast.31, s32[1]{0:T(128)} %bitcast.19.count, bf16[48,128,128]{2,1,0:T(8,128)(2,1)S(1)} %bitcast.21, ...), custom_call_target="tpu_custom_call" | custom-call | flops 50331648 | bytes 12582912 | tf_op jit(solution)/shard_map/adjoint_tiles/pallas_call | solution.py:192
  61.2 0.1 collective-permute-start.20
  61.3 3.8 %collective-permute-done.20 = bf16[224,32,128]{2,1,0:T(8,128)(2,1)S(1)} collective-permute-done((bf16[224,32,128]{2,1,0:T(8,128)(2,1)S(1)}, bf16[224,32,128]{2,1,0:T(8,128)(2,1)S(1)}, u32[]{:S(2)}, u32[]{:S(2)}) %collective-permute-start.20) | collective-permute-done | bytes 1835040 | tf_op jit(solution)/shard_map/ppermute | solution.py:52
  65.2 2.6 %collective-permute-start.21 = (bf16[32,32,128]{2,1,0:T(8,128)(2,1)S(1)}, bf16[32,32,128]{2,1,0:T(8,128)(2,1)S(1)}, u32[]{:S(2)}, u32[]{:S(2)}) collective-permute-start(bf16[32,32,128]{2,1,0:T(8,128)(2,1)S(1)} %add_convert_fusion.14), channel_id=1, source_target_pairs={{0,32},{8,232},{16,48},{24,248},{32,64},{40,8},{48,80},{56,24},{64... | collective-permute-start | bytes 786440 | tf_op jit(solution)/shard_map/ppermute | solution.py:52
  67.8 5.1 %collective-permute-done.21 = bf16[32,32,128]{2,1,0:T(8,128)(2,1)S(1)} collective-permute-done((bf16[32,32,128]{2,1,0:T(8,128)(2,1)S(1)}, bf16[32,32,128]{2,1,0:T(8,128)(2,1)S(1)}, u32[]{:S(2)}, u32[]{:S(2)}) %collective-permute-start.21) | collective-permute-done | bytes 262176 | tf_op jit(solution)/shard_map/ppermute | solution.py:52
  72.8 1.0 add_convert_fusion.7
  73.8 1.3 collective-permute-start.25
  75.2 6.5 %collective-permute-done.25 = bf16[32,32,128]{2,1,0:T(8,128)(2,1)} collective-permute-done((bf16[32,32,128]{2,1,0:T(8,128)(2,1)}, bf16[32,32,128]{2,1,0:T(8,128)(2,1)}, u32[]{:S(2)}, u32[]{:S(2)}) %collective-permute-start.25) | collective-permute-done | bytes 262176 | tf_op jit(solution)/shard_map/ppermute | solution.py:52
  81.7 2.8 %collective-permute-done.22 = bf16[32,32,128]{2,1,0:T(8,128)(2,1)} collective-permute-done((bf16[32,32,128]{2,1,0:T(8,128)(2,1)}, bf16[32,32,128]{2,1,0:T(8,128)(2,1)}, u32[]{:S(2)}, u32[]{:S(2)}) %collective-permute-start.22) | collective-permute-done | bytes 262176 | tf_op jit(solution)/shard_map/ppermute | solution.py:52
  84.5 1.4 %add_convert_fusion.5 = (bf16[32,32,128]{2,1,0:T(8,128)(2,1)S(1)}, bf16[32,32,128]{2,1,0:T(8,128)(2,1)S(1)}) fusion(bf16[32,32,128]{2,1,0:T(8,128)(2,1)} %collective-permute-done.25, bf16[224,32,128]{2,1,0:T(8,128)(2,1)S(1)} %collective-permute-done.20, bf16[224,32,128]{2,1,0:T(8,128)(2,1)} %copy-done.1, bf16[32,32,128]{2,1,0:T(8,128)(2,1)} %collective-permute-done.22), kind=kLoop, calls=%fused_computation.5 | loop fusion | flops 2097152 | bytes 2097152 | tf_op jit(solution)/shard_map/convert_element_type | solution.py:311
  85.9 0.2 collective-permute-start.26
  86.4 7.2 %collective-permute-done.26 = bf16[32,32,128]{2,1,0:T(8,128)(2,1)S(1)} collective-permute-done((bf16[32,32,128]{2,1,0:T(8,128)(2,1)S(1)}, bf16[32,32,128]{2,1,0:T(8,128)(2,1)S(1)}, u32[]{:S(2)}, u32[]{:S(2)}) %collective-permute-start.26) | collective-permute-done | bytes 262176 | tf_op jit(solution)/shard_map/ppermute | solution.py:52
  93.6 2.8 %collective-permute-done.23 = bf16[32,32,128]{2,1,0:T(8,128)(2,1)S(1)} collective-permute-done((bf16[32,32,128]{2,1,0:T(8,128)(2,1)S(1)}, bf16[32,32,128]{2,1,0:T(8,128)(2,1)S(1)}, u32[]{:S(2)}, u32[]{:S(2)}) %collective-permute-start.23) | collective-permute-done | bytes 262176 | tf_op jit(solution)/shard_map/ppermute | solution.py:52
  96.4 1.2 add_convert_fusion.3
  98.0 7.3 %collective-permute-done.27 = bf16[32,32,128]{2,1,0:T(8,128)(2,1)S(1)} collective-permute-done((bf16[32,32,128]{2,1,0:T(8,128)(2,1)S(1)}, bf16[32,32,128]{2,1,0:T(8,128)(2,1)S(1)}, u32[]{:S(2)}, u32[]{:S(2)}) %collective-permute-start.27) | collective-permute-done | bytes 262176 | tf_op jit(solution)/shard_map/ppermute | solution.py:52
  105.3 2.8 %collective-permute-done.24 = bf16[32,32,128]{2,1,0:T(8,128)(2,1)S(1)} collective-permute-done((bf16[32,32,128]{2,1,0:T(8,128)(2,1)S(1)}, bf16[32,32,128]{2,1,0:T(8,128)(2,1)S(1)}, u32[]{:S(2)}, u32[]{:S(2)}) %collective-permute-start.24) | collective-permute-done | bytes 262176 | tf_op jit(solution)/shard_map/ppermute | solution.py:52
  108.1 0.2 broadcast_select_fusion
  108.3 1.3 collective-permute-start.28
  109.7 7.0 %collective-permute-start.5 = (bf16[8,3,32,128]{3,2,1,0:T(8,128)(2,1)S(1)}, bf16[8,3,32,128]{3,2,1,0:T(8,128)(2,1)S(1)}, u32[]{:S(2)}, u32[]{:S(2)}) collective-permute-start(bf16[8,3,32,128]{3,2,1,0:T(8,128)(2,1)S(1)} %get-tuple-element.20), channel_id=1, source_target_pairs={{1,0},{2,1},{3,2},{4,3},{5,4},{6,5},{7,6},{9,8},{10,9},{11,10},{12... | collective-permute-start | bytes 589832 | tf_op jit(solution)/shard_map/ppermute | solution.py:56
  116.7 1.9 %collective-permute-start.4 = (bf16[8,3,32,128]{3,2,1,0:T(8,128)(2,1)S(1)}, bf16[8,3,32,128]{3,2,1,0:T(8,128)(2,1)S(1)}, u32[]{:S(2)}, u32[]{:S(2)}) collective-permute-start(bf16[8,3,32,128]{3,2,1,0:T(8,128)(2,1)S(1)} %get-tuple-element.21), channel_id=1, source_target_pairs={{0,1},{1,2},{2,3},{3,4},{4,5},{5,6},{6,7},{8,9},{9,10},{10,11},{11... | collective-permute-start | bytes 589832 | tf_op jit(solution)/shard_map/ppermute | solution.py:56
  118.6 0.1 add_convert_fusion
  118.8 0.1 collective-permute-start.29
  119.0 2.4 %collective-permute-done.5.high = bf16[8,3,32,128]{3,2,1,0:T(8,128)(2,1)S(1)} collective-permute-done((bf16[8,3,32,128]{3,2,1,0:T(8,128)(2,1)S(1)}, bf16[8,3,32,128]{3,2,1,0:T(8,128)(2,1)S(1)}, u32[]{:S(2)}, u32[]{:S(2)}) %collective-permute-start.5) | collective-permute-done | bytes 196640 | tf_op jit(solution)/shard_map/ppermute | solution.py:56
  121.3 5.3 %collective-permute-done.4.low = bf16[8,3,32,128]{3,2,1,0:T(8,128)(2,1)S(1)} collective-permute-done((bf16[8,3,32,128]{3,2,1,0:T(8,128)(2,1)S(1)}, bf16[8,3,32,128]{3,2,1,0:T(8,128)(2,1)S(1)}, u32[]{:S(2)}, u32[]{:S(2)}) %collective-permute-start.4) | collective-permute-done | bytes 196640 | tf_op jit(solution)/shard_map/ppermute | solution.py:56
  126.7 3.9 %tv_prox.1 = f32[2,8,32,128]{3,2,1,0:T(8,128)S(1)} custom-call(s32[2]{0:T(128)S(1)} %pad_add_fusion.start, bf16[8,8,32,128]{3,2,1,0:T(8,128)(2,1)S(1)} %bitcast.23, bf16[8,3,32,128]{3,2,1,0:T(8,128)(2,1)S(1)} %collective-permute-done.4.low, bf16[8,3,32,128]{3,2,1,0:T(8,128)(2,1)S(1)} %collective-permute-done.5.high, f32[2,8,32,128]{3,2,1,0:T(8,128)S(1)} %bitcast.24, ...), custom_call_target="tpu_custom_call" | custom-call | flops 16777216 | bytes 12582912 | tf_op jit(solution)/shard_map/tv_prox/pallas_call | solution.py:280
  130.6 0.7 subtract_bitcast_fusion
  (57 shorter events, 1.3 us)
Async XLA Ops:
  0.0 43.7 %copy-start.9 = (s32[1,1,48]{2,1,0:T(1,128)S(1)}, s32[1,1,48]{2,1,0:T(1,128)}, u32[]{:S(2)}) copy-start(s32[1,1,48]{2,1,0:T(1,128)} %param.14) | copy-start | bytes 580
  0.0 43.7 %copy-start.8 = (s32[1,1,48]{2,1,0:T(1,128)S(1)}, s32[1,1,48]{2,1,0:T(1,128)}, u32[]{:S(2)}) copy-start(s32[1,1,48]{2,1,0:T(1,128)} %param.13) | copy-start | bytes 580
  0.0 43.7 %copy-start = (bf16[1,1,48,128,128]{4,3,2,1,0:T(8,128)(2,1)S(1)}, bf16[1,1,48,128,128]{4,3,2,1,0:T(8,128)(2,1)}, u32[]{:S(2)}) copy-start(bf16[1,1,48,128,128]{4,3,2,1,0:T(8,128)(2,1)} %param.12) | copy-start | bytes 4718596
  8.3 10.3 %collective-permute-start = (bf16[32,32,128]{2,1,0:T(8,128)(2,1)S(1)}, bf16[32,32,128]{2,1,0:T(8,128)(2,1)S(1)}, u32[]{:S(2)}, u32[]{:S(2)}) collective-permute-start(bf16[32,32,128]{2,1,0:T(8,128)(2,1)S(1)} %get-tuple-element.23), channel_id=1, source_target_pairs={{0,32},{8,232},{16,48},{24,248},{32,64},{40,8},{48,80},{56,24},{64... | collective-permute-start | bytes 786440 | tf_op jit(solution)/shard_map/ppermute | solution.py:52
  10.3 11.1 %collective-permute-start.2 = (bf16[32,32,128]{2,1,0:T(8,128)(2,1)S(1)}, bf16[32,32,128]{2,1,0:T(8,128)(2,1)S(1)}, u32[]{:S(2)}, u32[]{:S(2)}) collective-permute-start(bf16[32,32,128]{2,1,0:T(8,128)(2,1)S(1)} %get-tuple-element.22), channel_id=1, source_target_pairs={{0,32},{8,232},{16,48},{24,248},{32,64},{40,8},{48,80},{56,24},{64... | collective-permute-start | bytes 786440 | tf_op jit(solution)/shard_map/ppermute | solution.py:52
  18.6 7.6 %collective-permute-start.6 = (bf16[32,32,128]{2,1,0:T(8,128)(2,1)S(1)}, bf16[32,32,128]{2,1,0:T(8,128)(2,1)S(1)}, u32[]{:S(2)}, u32[]{:S(2)}) collective-permute-start(bf16[32,32,128]{2,1,0:T(8,128)(2,1)S(1)} %collective-permute-done.rest_0_), channel_id=1, source_target_pairs={{0,32},{8,232},{16,48},{24,248},{32,64},{40,8},{48,80},{56,24},{64... | collective-permute-start | bytes 786440 | tf_op jit(solution)/shard_map/ppermute | solution.py:52
  21.4 7.7 %collective-permute-start.12 = (bf16[32,32,128]{2,1,0:T(8,128)(2,1)S(1)}, bf16[32,32,128]{2,1,0:T(8,128)(2,1)}, u32[]{:S(2)}, u32[]{:S(2)}) collective-permute-start(bf16[32,32,128]{2,1,0:T(8,128)(2,1)S(1)} %collective-permute-done.2.rest_8_), channel_id=1, source_target_pairs={{0,32},{8,232},{16,48},{24,248},{32,64},{40,8},{48,80},{56,24},{64... | collective-permute-start | bytes 786440 | tf_op jit(solution)/shard_map/ppermute | solution.py:52
  26.2 7.7 %collective-permute-start.7 = (bf16[32,32,128]{2,1,0:T(8,128)(2,1)S(1)}, bf16[32,32,128]{2,1,0:T(8,128)(2,1)}, u32[]{:S(2)}, u32[]{:S(2)}) collective-permute-start(bf16[32,32,128]{2,1,0:T(8,128)(2,1)S(1)} %collective-permute-done.6.rest_1_), channel_id=1, source_target_pairs={{0,32},{8,232},{16,48},{24,248},{32,64},{40,8},{48,80},{56,24},{64... | collective-permute-start | bytes 786440 | tf_op jit(solution)/shard_map/ppermute | solution.py:52
  26.2 7.7 %collective-permute-start.3 = (bf16[32,32,128]{2,1,0:T(8,128)(2,1)S(1)}, bf16[32,32,128]{2,1,0:T(8,128)(2,1)S(1)}, u32[]{:S(2)}, u32[]{:S(2)}) collective-permute-start(bf16[32,32,128]{2,1,0:T(8,128)(2,1)S(1)} %collective-permute-done.2.rest_8_), channel_id=1, source_target_pairs={{0,8},{8,0},{16,24},{24,16},{32,40},{40,32},{48,56},{56,48},{64,72... | collective-permute-start | bytes 786440 | tf_op jit(solution)/shard_map/ppermute | solution.py:52
  27.2 7.2 %collective-permute-start.1 = (bf16[32,32,128]{2,1,0:T(8,128)(2,1)S(1)}, bf16[32,32,128]{2,1,0:T(8,128)(2,1)S(1)}, u32[]{:S(2)}, u32[]{:S(2)}) collective-permute-start(bf16[32,32,128]{2,1,0:T(8,128)(2,1)S(1)} %collective-permute-done.rest_0_), channel_id=1, source_target_pairs={{0,8},{8,0},{16,24},{24,16},{32,40},{40,32},{48,56},{56,48},{64,72... | collective-permute-start | bytes 786440 | tf_op jit(solution)/shard_map/ppermute | solution.py:52
  29.1 7.9 %collective-permute-start.13 = (bf16[32,32,128]{2,1,0:T(8,128)(2,1)}, bf16[32,32,128]{2,1,0:T(8,128)(2,1)}, u32[]{:S(2)}, u32[]{:S(2)}) collective-permute-start(bf16[32,32,128]{2,1,0:T(8,128)(2,1)} %collective-permute-done.12.rest_9_), channel_id=1, source_target_pairs={{0,32},{8,232},{16,48},{24,248},{32,64},{40,8},{48,80},{56,24},{64... | collective-permute-start | bytes 786440 | tf_op jit(solution)/shard_map/ppermute | solution.py:52
  33.9 7.9 %collective-permute-start.8 = (bf16[32,32,128]{2,1,0:T(8,128)(2,1)}, bf16[32,32,128]{2,1,0:T(8,128)(2,1)}, u32[]{:S(2)}, u32[]{:S(2)}) collective-permute-start(bf16[32,32,128]{2,1,0:T(8,128)(2,1)} %collective-permute-done.7.rest_2_), channel_id=1, source_target_pairs={{0,32},{8,232},{16,48},{24,248},{32,64},{40,8},{48,80},{56,24},{64... | collective-permute-start | bytes 786440 | tf_op jit(solution)/shard_map/ppermute | solution.py:52
  33.9 8.6 %collective-permute-start.14 = (bf16[32,32,128]{2,1,0:T(8,128)(2,1)}, bf16[32,32,128]{2,1,0:T(8,128)(2,1)}, u32[]{:S(2)}, u32[]{:S(2)}) collective-permute-start(bf16[32,32,128]{2,1,0:T(8,128)(2,1)} %collective-permute-done.12.rest_9_), channel_id=1, source_target_pairs={{0,8},{8,0},{16,24},{24,16},{32,40},{40,32},{48,56},{56,48},{64,72... | collective-permute-start | bytes 786440 | tf_op jit(solution)/shard_map/ppermute | solution.py:52
  33.9 8.6 %collective-permute-start.9 = (bf16[32,32,128]{2,1,0:T(8,128)(2,1)S(1)}, bf16[32,32,128]{2,1,0:T(8,128)(2,1)}, u32[]{:S(2)}, u32[]{:S(2)}) collective-permute-start(bf16[32,32,128]{2,1,0:T(8,128)(2,1)S(1)} %collective-permute-done.6.rest_1_), channel_id=1, source_target_pairs={{0,8},{8,0},{16,24},{24,16},{32,40},{40,32},{48,56},{56,48},{64,72... | collective-permute-start | bytes 786440 | tf_op jit(solution)/shard_map/ppermute | solution.py:52
  34.4 8.1 %collective-permute-start.10 = (bf16[32,32,128]{2,1,0:T(8,128)(2,1)}, bf16[32,32,128]{2,1,0:T(8,128)(2,1)}, u32[]{:S(2)}, u32[]{:S(2)}) collective-permute-start(bf16[32,32,128]{2,1,0:T(8,128)(2,1)} %collective-permute-done.7.rest_2_), channel_id=1, source_target_pairs={{0,8},{8,0},{16,24},{24,16},{32,40},{40,32},{48,56},{56,48},{64,72... | collective-permute-start | bytes 786440 | tf_op jit(solution)/shard_map/ppermute | solution.py:52
  37.0 5.5 %collective-permute-start.15 = (bf16[32,32,128]{2,1,0:T(8,128)(2,1)}, bf16[32,32,128]{2,1,0:T(8,128)(2,1)}, u32[]{:S(2)}, u32[]{:S(2)}) collective-permute-start(bf16[32,32,128]{2,1,0:T(8,128)(2,1)} %collective-permute-done.13.rest_10_), channel_id=1, source_target_pairs={{0,8},{8,0},{16,24},{24,16},{32,40},{40,32},{48,56},{56,48},{64,72... | collective-permute-start | bytes 786440 | tf_op jit(solution)/shard_map/ppermute | solution.py:52
  41.8 1.9 %collective-permute-start.11 = (bf16[32,32,128]{2,1,0:T(8,128)(2,1)}, bf16[32,32,128]{2,1,0:T(8,128)(2,1)}, u32[]{:S(2)}, u32[]{:S(2)}) collective-permute-start(bf16[32,32,128]{2,1,0:T(8,128)(2,1)} %collective-permute-done.8.rest_3_), channel_id=1, source_target_pairs={{0,8},{8,0},{16,24},{24,16},{32,40},{40,32},{48,56},{56,48},{64,72... | collective-permute-start | bytes 786440 | tf_op jit(solution)/shard_map/ppermute | solution.py:52
  43.7 15.8 %copy-start.6 = (f32[1024]{0:T(1024)S(1)}, f32[1024]{0:T(1024)}, u32[]{:S(2)}) copy-start(f32[1024]{0:T(1024)} %param.10) | copy-start | bytes 12292
  43.7 15.8 %copy-start.7 = (f32[1024]{0:T(1024)S(1)}, f32[1024]{0:T(1024)}, u32[]{:S(2)}) copy-start(f32[1024]{0:T(1024)} %param.11) | copy-start | bytes 12292
  45.9 6.5 %collective-permute-start.16 = (bf16[8,32,128]{2,1,0:T(8,128)(2,1)S(1)}, bf16[8,32,128]{2,1,0:T(8,128)(2,1)S(1)}, u32[]{:S(2)}, u32[]{:S(2)}) collective-permute-start(bf16[8,32,128]{2,1,0:T(8,128)(2,1)S(1)} %forward_tiles.1), channel_id=1, source_target_pairs={{0,1},{1,0},{2,3},{3,2},{4,5},{5,4},{6,7},{7,6},{8,9},{9,8},{10,11... | collective-permute-start | bytes 196616 | tf_op jit(solution)/shard_map/ppermute | solution.py:56
  52.4 6.7 %collective-permute-start.19 = (bf16[8,32,128]{2,1,0:T(8,128)(2,1)S(1)}, bf16[8,32,128]{2,1,0:T(8,128)(2,1)S(1)}, u32[]{:S(2)}, u32[]{:S(2)}) collective-permute-start(bf16[8,32,128]{2,1,0:T(8,128)(2,1)S(1)} %add_convert_fusion.15.rest_0_), channel_id=1, source_target_pairs={{0,6},{1,7},{2,0},{3,1},{4,2},{5,3},{6,4},{7,5},{8,14},{9,15},{10,... | collective-permute-start | bytes 196616 | tf_op jit(solution)/shard_map/ppermute | solution.py:56
  53.2 5.9 %collective-permute-start.18 = (bf16[8,32,128]{2,1,0:T(8,128)(2,1)S(1)}, bf16[8,32,128]{2,1,0:T(8,128)(2,1)S(1)}, u32[]{:S(2)}, u32[]{:S(2)}) collective-permute-start(bf16[8,32,128]{2,1,0:T(8,128)(2,1)S(1)} %add_convert_fusion.15.rest_0_), channel_id=1, source_target_pairs={{0,4},{1,5},{2,6},{3,7},{4,0},{5,1},{6,2},{7,3},{8,12},{9,13},{10,... | collective-permute-start | bytes 196616 | tf_op jit(solution)/shard_map/ppermute | solution.py:56
  54.8 4.7 %collective-permute-start.17 = (bf16[8,32,128]{2,1,0:T(8,128)(2,1)S(1)}, bf16[8,32,128]{2,1,0:T(8,128)(2,1)S(1)}, u32[]{:S(2)}, u32[]{:S(2)}) collective-permute-start(bf16[8,32,128]{2,1,0:T(8,128)(2,1)S(1)} %add_convert_fusion.15.rest_0_), channel_id=1, source_target_pairs={{0,2},{1,3},{2,4},{3,5},{4,6},{5,7},{6,0},{7,1},{8,10},{9,11},{10,... | collective-permute-start | bytes 196616 | tf_op jit(solution)/shard_map/ppermute | solution.py:56
  61.2 11.6 %copy-start.1 = (bf16[224,32,128]{2,1,0:T(8,128)(2,1)}, bf16[224,32,128]{2,1,0:T(8,128)(2,1)S(1)}, u32[]{:S(2)}) copy-start(bf16[224,32,128]{2,1,0:T(8,128)(2,1)S(1)} %get-tuple-element.8) | copy-start | bytes 5505028
  61.2 12.6 %copy-start.3 = (bf16[64,32,128]{2,1,0:T(8,128)(2,1)}, bf16[64,32,128]{2,1,0:T(8,128)(2,1)S(1)}, u32[]{:S(2)}) copy-start(bf16[64,32,128]{2,1,0:T(8,128)(2,1)S(1)} %get-tuple-element.10) | copy-start | bytes 1572868
  61.2 3.9 %collective-permute-start.20 = (bf16[224,32,128]{2,1,0:T(8,128)(2,1)S(1)}, bf16[224,32,128]{2,1,0:T(8,128)(2,1)S(1)}, u32[]{:S(2)}, u32[]{:S(2)}) collective-permute-start(bf16[224,32,128]{2,1,0:T(8,128)(2,1)S(1)} %get-tuple-element.9), channel_id=1, source_target_pairs={{0,8},{8,0},{16,24},{24,16},{32,40},{40,32},{48,56},{56,48},{64,72... | collective-permute-start | bytes 5505032 | tf_op jit(solution)/shard_map/ppermute | solution.py:52
  65.2 7.7 %collective-permute-start.21 = (bf16[32,32,128]{2,1,0:T(8,128)(2,1)S(1)}, bf16[32,32,128]{2,1,0:T(8,128)(2,1)S(1)}, u32[]{:S(2)}, u32[]{:S(2)}) collective-permute-start(bf16[32,32,128]{2,1,0:T(8,128)(2,1)S(1)} %add_convert_fusion.14), channel_id=1, source_target_pairs={{0,32},{8,232},{16,48},{24,248},{32,64},{40,8},{48,80},{56,24},{64... | collective-permute-start | bytes 786440 | tf_op jit(solution)/shard_map/ppermute | solution.py:52
  73.8 7.9 %collective-permute-start.25 = (bf16[32,32,128]{2,1,0:T(8,128)(2,1)}, bf16[32,32,128]{2,1,0:T(8,128)(2,1)}, u32[]{:S(2)}, u32[]{:S(2)}) collective-permute-start(bf16[32,32,128]{2,1,0:T(8,128)(2,1)} %get-tuple-element.18), channel_id=1, source_target_pairs={{0,32},{8,232},{16,48},{24,248},{32,64},{40,8},{48,80},{56,24},{64... | collective-permute-start | bytes 786440 | tf_op jit(solution)/shard_map/ppermute | solution.py:52
  75.1 9.4 %collective-permute-start.22 = (bf16[32,32,128]{2,1,0:T(8,128)(2,1)}, bf16[32,32,128]{2,1,0:T(8,128)(2,1)}, u32[]{:S(2)}, u32[]{:S(2)}) collective-permute-start(bf16[32,32,128]{2,1,0:T(8,128)(2,1)} %get-tuple-element.19), channel_id=1, source_target_pairs={{0,32},{8,232},{16,48},{24,248},{32,64},{40,8},{48,80},{56,24},{64... | collective-permute-start | bytes 786440 | tf_op jit(solution)/shard_map/ppermute | solution.py:52
  85.9 7.7 %collective-permute-start.26 = (bf16[32,32,128]{2,1,0:T(8,128)(2,1)S(1)}, bf16[32,32,128]{2,1,0:T(8,128)(2,1)S(1)}, u32[]{:S(2)}, u32[]{:S(2)}) collective-permute-start(bf16[32,32,128]{2,1,0:T(8,128)(2,1)S(1)} %get-tuple-element.16), channel_id=1, source_target_pairs={{0,32},{8,232},{16,48},{24,248},{32,64},{40,8},{48,80},{56,24},{64... | collective-permute-start | bytes 786440 | tf_op jit(solution)/shard_map/ppermute | solution.py:52
  86.1 10.3 %collective-permute-start.23 = (bf16[32,32,128]{2,1,0:T(8,128)(2,1)S(1)}, bf16[32,32,128]{2,1,0:T(8,128)(2,1)S(1)}, u32[]{:S(2)}, u32[]{:S(2)}) collective-permute-start(bf16[32,32,128]{2,1,0:T(8,128)(2,1)S(1)} %get-tuple-element.17), channel_id=1, source_target_pairs={{0,32},{8,232},{16,48},{24,248},{32,64},{40,8},{48,80},{56,24},{64... | collective-permute-start | bytes 786440 | tf_op jit(solution)/shard_map/ppermute | solution.py:52
  86.3 21.7 %copy-start.4 = (bf16[64,32,128]{2,1,0:T(8,128)(2,1)S(1)}, bf16[64,32,128]{2,1,0:T(8,128)(2,1)}, u32[]{:S(2)}) copy-start(bf16[64,32,128]{2,1,0:T(8,128)(2,1)} %copy-done.3) | copy-start | bytes 1572868
  97.6 7.7 %collective-permute-start.27 = (bf16[32,32,128]{2,1,0:T(8,128)(2,1)S(1)}, bf16[32,32,128]{2,1,0:T(8,128)(2,1)S(1)}, u32[]{:S(2)}, u32[]{:S(2)}) collective-permute-start(bf16[32,32,128]{2,1,0:T(8,128)(2,1)S(1)} %get-tuple-element.14), channel_id=1, source_target_pairs={{0,32},{8,232},{16,48},{24,248},{32,64},{40,8},{48,80},{56,24},{64... | collective-permute-start | bytes 786440 | tf_op jit(solution)/shard_map/ppermute | solution.py:52
  97.7 10.4 %collective-permute-start.24 = (bf16[32,32,128]{2,1,0:T(8,128)(2,1)S(1)}, bf16[32,32,128]{2,1,0:T(8,128)(2,1)S(1)}, u32[]{:S(2)}, u32[]{:S(2)}) collective-permute-start(bf16[32,32,128]{2,1,0:T(8,128)(2,1)S(1)} %get-tuple-element.15), channel_id=1, source_target_pairs={{0,32},{8,232},{16,48},{24,248},{32,64},{40,8},{48,80},{56,24},{64... | collective-permute-start | bytes 786440 | tf_op jit(solution)/shard_map/ppermute | solution.py:52
  108.3 18.4 %copy-start.2 = (f32[2,8,128,32]{2,3,1,0:T(8,128)S(1)}, f32[2,8,128,32]{2,3,1,0:T(8,128)}, u32[]{:S(2)}) copy-start(f32[2,8,128,32]{2,3,1,0:T(8,128)} %param.8) | copy-start | bytes 786436
  108.3 18.4 %copy-start.5 = (f32[2,8,128,32]{2,3,1,0:T(8,128)S(1)}, f32[2,8,128,32]{2,3,1,0:T(8,128)}, u32[]{:S(2)}) copy-start(f32[2,8,128,32]{2,3,1,0:T(8,128)} %param.9) | copy-start | bytes 786436
  108.3 10.3 %collective-permute-start.28 = (bf16[32,32,128]{2,1,0:T(8,128)(2,1)S(1)}, bf16[32,32,128]{2,1,0:T(8,128)(2,1)S(1)}, u32[]{:S(2)}, u32[]{:S(2)}) collective-permute-start(bf16[32,32,128]{2,1,0:T(8,128)(2,1)S(1)} %get-tuple-element.11), channel_id=1, source_target_pairs={{0,16},{8,24},{16,0},{24,8},{32,48},{40,56},{48,32},{56,40},{64,80... | collective-permute-start | bytes 786440 | tf_op jit(solution)/shard_map/ppermute | solution.py:52
  109.7 11.6 %collective-permute-start.5 = (bf16[8,3,32,128]{3,2,1,0:T(8,128)(2,1)S(1)}, bf16[8,3,32,128]{3,2,1,0:T(8,128)(2,1)S(1)}, u32[]{:S(2)}, u32[]{:S(2)}) collective-permute-start(bf16[8,3,32,128]{3,2,1,0:T(8,128)(2,1)S(1)} %get-tuple-element.20), channel_id=1, source_target_pairs={{1,0},{2,1},{3,2},{4,3},{5,4},{6,5},{7,6},{9,8},{10,9},{11,10},{12... | collective-permute-start | bytes 589832 | tf_op jit(solution)/shard_map/ppermute | solution.py:56
  116.7 10.0 %collective-permute-start.4 = (bf16[8,3,32,128]{3,2,1,0:T(8,128)(2,1)S(1)}, bf16[8,3,32,128]{3,2,1,0:T(8,128)(2,1)S(1)}, u32[]{:S(2)}, u32[]{:S(2)}) collective-permute-start(bf16[8,3,32,128]{3,2,1,0:T(8,128)(2,1)S(1)} %get-tuple-element.21), channel_id=1, source_target_pairs={{0,1},{1,2},{2,3},{3,4},{4,5},{5,6},{6,7},{8,9},{9,10},{10,11},{11... | collective-permute-start | bytes 589832 | tf_op jit(solution)/shard_map/ppermute | solution.py:56
  118.8 11.8 %collective-permute-start.29 = (bf16[16,32,128]{2,1,0:T(8,128)(2,1)S(1)}, bf16[16,32,128]{2,1,0:T(8,128)(2,1)S(1)}, u32[]{:S(2)}, u32[]{:S(2)}) collective-permute-start(bf16[16,32,128]{2,1,0:T(8,128)(2,1)S(1)} %broadcast_select_fusion.3), channel_id=1, source_target_pairs={{0,8},{8,0},{16,24},{24,16},{32,40},{40,32},{48,56},{56,48},{64,72... | collective-permute-start | bytes 393224 | tf_op jit(solution)/shard_map/ppermute | solution.py:52

commit v2 on v1

v2 whole, which is shorter than its diff:
```python
import functools
import math

import jax
import jax.numpy as jnp
from jax import lax
from jax.experimental import pallas as pl
from jax.experimental.pallas import tpu as pltpu
from jax.sharding import PartitionSpec as P

theta_tv = 0.25
tau_dual = 1.0 / (12.0 * 0.25)
step_size = 0.5
moreau = 1.0
noise_scale = math.sqrt(2.0 * step_size)

F32 = jnp.float32
BF16 = jnp.bfloat16

N_Z = 8
QUAD = 4
N_ROW = N_Z * QUAD
N_COL = 8
OWN_Y = 2
OWN_X = 8
OWN = OWN_Y * OWN_X
PLANE = QUAD * OWN
HALF = PLANE // 2
LINES = N_Z * PLANE
CH = 32
NZ = 128
RB = 8
SLOTS = 48
GROUP = 8
HALO = 3
WIDE_Y = OWN_Y + 2 * HALO
WIDE_X = OWN_X + 2 * HALO
TOP_Y = N_ROW * OWN_Y - 1
TOP_X = N_COL * OWN_X - 1
LONG = 2 * OWN
SENT = LONG + 3 * PLANE
FIRST = LONG + PLANE

CORE = [(i, i ^ 1) for i in range(N_ROW)]
X_HI = [(i, i ^ 1) for i in range(N_COL)]
ACROSS = [(i, (i - 1 + 2 * (i % 2)) % N_COL) for i in range(N_COL)]
X_LO = [(i, i ^ 2) for i in range(N_ROW)]
RING = [(i, (i + (QUAD if i % 2 == 0 else -QUAD)) % N_ROW) for i in range(N_ROW)]

CHAINS = ((2, 0), (3, 1))
QUADS = [[QUAD * z + q for q in range(QUAD)] for z in range(N_Z)]
MINE = [(0, steps) for steps in range(1, 5)] + [(1, steps) for steps in range(1, 4)]
PIECES = MINE + [(1 - flip, -steps) for flip, steps in MINE]

ANY = pl.BlockSpec(memory_space=pl.ANY)
VMEM = pl.BlockSpec(memory_space=pltpu.VMEM)
SMEM = pl.BlockSpec(memory_space=pltpu.SMEM)


def over_row(value, pairs):
    return lax.ppermute(value, "row", pairs)


def over_col(value, pairs):
    return lax.ppermute(value, "col", pairs)


def after(value, other):
    return lax.optimization_barrier((value, other))[0]


def params():
    return pltpu.CompilerParams(vmem_limit_bytes=20 * 2**20)


def forward_kernel(place, rows, cols, count, tiles, plane, *rest):
    pieces, (out, wide, near, far, field, total, sems) = rest[: len(PIECES)], rest[len(PIECES) :]
    z = place[0]
    quad = place[1]
    core = quad & 1
    up = 1 - 2 * core
    copies = [pltpu.make_async_copy(plane, field.at[pl.ds(z * PLANE, PLANE)], sems.at[len(PIECES)])]
    for i, ((flip, steps), piece) in enumerate(zip(PIECES, pieces)):
        from_plane = lax.rem(z - steps * up + 2 * N_Z, N_Z)
        half = core if flip == 0 else 1 - core
        there = field.at[pl.ds(from_plane * PLANE + half * HALF, HALF)]
        copies.append(pltpu.make_async_copy(piece, there, sems.at[i]))
    for copy in copies:
        copy.start()
    for copy in copies:
        copy.wait()
    total[...] = jnp.zeros_like(total)
    used = count[0]

    def group(index, carry):
        terms = []
        for u in range(GROUP):
            slot = index * GROUP + u
            term = lax.dot_general(
                field[cols[slot]], tiles[slot], (((1,), (1,)), ((), ())), preferred_element_type=F32
            )
            terms.append(jnp.where(slot < used, term, 0.0))
        for u in range(GROUP):
            total[rows[index * GROUP + u]] += terms[u]
        return carry

    lax.fori_loop(0, (used + GROUP - 1) // GROUP, group, 0)
    out[...] = total[...].astype(BF16)
    to_near = jnp.where(place[2] == 0, OWN_X - HALO, 0)
    to_far = OWN_X - HALO - to_near
    for y in range(WIDE_Y):
        line = lax.rem((z * QUAD + quad) * OWN_Y - HALO + y + N_ROW * OWN_Y, N_ROW * OWN_Y) * OWN_X
        wide[y] = field[pl.ds(line, OWN_X)]
        near[y] = field[pl.ds(line + to_near, HALO)]
        far[y] = field[pl.ds(line + to_far, HALO)]


def forward(place, rows, cols, count, tiles, plane, pieces):
    return pl.pallas_call(
        forward_kernel,
        out_shape=[
            jax.ShapeDtypeStruct((RB, CH, NZ), BF16),
            jax.ShapeDtypeStruct((WIDE_Y, OWN_X, CH, NZ), BF16),
            jax.ShapeDtypeStruct((WIDE_Y, HALO, CH, NZ), BF16),
            jax.ShapeDtypeStruct((WIDE_Y, HALO, CH, NZ), BF16),
        ],
        in_specs=[SMEM] * 4 + [VMEM] + [ANY] * (1 + len(pieces)),
        out_specs=[VMEM] * 4,
        scratch_shapes=[
            pltpu.VMEM((LINES, CH, NZ), BF16),
            pltpu.VMEM((RB, CH, NZ), F32),
            pltpu.SemaphoreType.DMA((1 + len(pieces),)),
        ],
        compiler_params=params(),
        cost_estimate=pl.CostEstimate(
            flops=2 * SLOTS * NZ * NZ * CH, bytes_accessed=12 * 2**20, transcendentals=0
        ),
        name="forward_tiles",
    )(place, rows, cols, count, tiles, plane, *pieces)


def adjoint_kernel(
    place, rows, cols, count, tiles, observed, weight, *rest
):
    parts, (soon, later, mine, own, residual, total, first) = rest[:4], rest[4:]
    z = place[0]
    quad = place[1]
    core = quad & 1
    used = count[0]
    for b in range(RB):
        predicted = parts[0][b].astype(F32)
        for part in parts[1:]:
            predicted = predicted + part[b].astype(F32)
        residual[b] = (weight[pl.ds(b, 1), :] * (predicted - observed[pl.ds(b, 1), :])).astype(BF16)
    total[...] = jnp.zeros_like(total)
    soon[...] = jnp.zeros_like(soon)
    later[...] = jnp.zeros_like(later)
    mine[...] = jnp.zeros_like(mine)
    own[...] = jnp.zeros_like(own)

    def mark(index, carry):
        slot = used - 1 - index
        first[cols[slot]] = slot
        return carry

    lax.fori_loop(0, used, mark, 0)

    def group(index, carry):
        terms = []
        for u in range(GROUP):
            slot = index * GROUP + u
            term = lax.dot_general(
                residual[rows[slot]], tiles[slot], (((1,), (0,)), ((), ())), preferred_element_type=F32
            )
            terms.append(term)
        for u in range(GROUP):
            slot = index * GROUP + u

            @pl.when(slot < used)
            def _():
                total[first[cols[slot]]] += terms[u]

        return carry

    lax.fori_loop(0, (used + GROUP - 1) // GROUP, group, 0)

    def place_line(slot, carry):
        line = cols[slot]
        value = total[first[line]].astype(BF16)
        away = lax.rem(line // PLANE - z + N_Z, N_Z)
        other = lax.rem(line // OWN, QUAD)
        inner = lax.rem(line, OWN)
        carrier = jnp.where(away == 4, other & 1, jnp.where(away < 4, 0, 1))
        steps = jnp.where(carrier == 0, away, N_Z - away)
        turn = 2 * ((other & 1) ^ carrier) + 1 - ((other // 2) ^ (quad // 2))
        where = jnp.where(steps == 4, 0, LONG + (3 - steps) * PLANE) + turn * OWN + inner
        own_place = (2 * ((other & 1) ^ core) + 1 - ((other // 2) ^ (quad // 2))) * OWN + inner

        @pl.when(away == 0)
        def _():
            own[own_place] = value

        @pl.when((away != 0) & (carrier == core))
        def _():
            mine[where] = value

        @pl.when((away != 0) & (carrier != core) & (where < FIRST))
        def _():
            soon[where] = value

        @pl.when((away != 0) & (carrier != core) & (where >= FIRST))
        def _():
            later[where - FIRST] = value

        return carry

    lax.fori_loop(0, used, place_line, 0)


def adjoint(place, rows, cols, count, tiles, observed, weight, parts):
    return pl.pallas_call(
        adjoint_kernel,
        out_shape=[
            jax.ShapeDtypeStruct((FIRST, CH, NZ), BF16),
            jax.ShapeDtypeStruct((SENT - FIRST, CH, NZ), BF16),
            jax.ShapeDtypeStruct((SENT, CH, NZ), BF16),
            jax.ShapeDtypeStruct((PLANE, CH, NZ), BF16),
        ],
        in_specs=[SMEM] * 4 + [VMEM] * (3 + len(parts)),
        out_specs=[VMEM] * 4,
        scratch_shapes=[
            pltpu.VMEM((RB, CH, NZ), BF16),
            pltpu.VMEM((SLOTS, CH, NZ), F32),
            pltpu.SMEM((LINES,), jnp.int32),
        ],
        compiler_params=params(),
        cost_estimate=pl.CostEstimate(
            flops=2 * SLOTS * NZ * NZ * CH, bytes_accessed=12 * 2**20, transcendentals=0
        ),
        name="adjoint_tiles",
    )(place, rows, cols, count, tiles, observed, weight, *parts)


def prox_kernel(start, wide, near, far, anchor, noise, out, field, primal, dual_y, dual_x, dual_z):
    y0 = start[0]
    x0 = start[1]
    above = jnp.where(start[2] == 0, HALO + OWN_X, 0)
    below = HALO + OWN_X - above
    lane = lax.broadcasted_iota(jnp.int32, (CH, NZ), 1)
    not_first = lane > 0
    not_last = lane < NZ - 1

    def load_line(y, carry):
        for x in range(OWN_X):
            field[y, HALO + x] = wide[y, x].astype(F32)
        for x in range(HALO):
            field[y, above + x] = near[y, x].astype(F32)
            field[y, below + x] = far[y, x].astype(F32)
        return carry

    lax.fori_loop(0, WIDE_Y, load_line, 0)
    for y in range(OWN_Y):
        for x in range(OWN_X):
            field[HALO + y, HALO + x] = anchor[y, x]

    def primal_at(y, x):
        along_z = dual_z[y, x]
        lower_z = jnp.where(not_first, pltpu.roll(along_z, 1, 1), 0.0)
        term = (dual_y[y - 1, x] - dual_y[y, x]) + (dual_x[y, x - 1] - dual_x[y, x]) + (lower_z - along_z)
        return field[y, x] - theta_tv * term

    for step in range(3):
        source = field if step == 0 else primal
        if step:

            def primal_line(y, carry, step=step):
                for x in range(step, WIDE_X - step):
                    primal[y, x] = primal_at(y, x)
                return carry

            lax.fori_loop(step, WIDE_Y - step, primal_line, 0)

        def dual_line(y, carry, step=step, source=source):
            line = y0 + y
            rate_y = jnp.where((line >= 0) & (line < TOP_Y), tau_dual, 0.0)
            for x in range(step, WIDE_X - 1 - step):
                plane = x0 + x
                rate_x = jnp.where((plane >= 0) & (plane < TOP_X), tau_dual, 0.0)
                here = source[y, x]
                diff_y = rate_y * (source[y + 1, x] - here)
                diff_x = rate_x * (source[y, x + 1] - here)
                diff_z = jnp.where(not_last, tau_dual * (pltpu.roll(here, NZ - 1, 1) - here), 0.0)
                if step:
                    diff_y = dual_y[y, x] + diff_y
                    diff_x = dual_x[y, x] + diff_x
                    diff_z = dual_z[y, x] + diff_z
                dual_y[y, x] = jnp.clip(diff_y, -1.0, 1.0)
                dual_x[y, x] = jnp.clip(diff_x, -1.0, 1.0)
                dual_z[y, x] = jnp.clip(diff_z, -1.0, 1.0)
            return carry

        lax.fori_loop(step, WIDE_Y - 1 - step, dual_line, 0)
    for y in range(OWN_Y):
        for x in range(OWN_X):
            here = field[HALO + y, HALO + x]
            prox = primal_at(HALO + y, HALO + x)
            out[y, x] = here - step_size / moreau * (here - prox) + noise_scale * noise[y, x]


def prox_step(start, wide, near, far, anchor, noise):
    region = pltpu.VMEM((WIDE_Y, WIDE_X, CH, NZ), F32)
    return pl.pallas_call(
        prox_kernel,
        out_shape=jax.ShapeDtypeStruct((OWN_Y, OWN_X, CH, NZ), F32),
        in_specs=[SMEM] + [VMEM] * 5,
        out_specs=VMEM,
        scratch_shapes=[region] * 5,
        compiler_params=params(),
        cost_estimate=pl.CostEstimate(flops=2**24, bytes_accessed=12 * 2**20, transcendentals=0),
        name="tv_prox",
    )(start, wide, near, far, anchor, noise)


def own_half(value, pick):
    half = value.shape[0] // 2
    return jnp.where(pick == 0, value[:half], value[half:])


def gather_slab(own, core):
    plane = lax.all_gather(own, "row", axis=0, tiled=True, axis_index_groups=QUADS)
    chains = [own_half(plane, core), own_half(plane, 1 - core)]
    mine = {}
    for steps in range(1, 5):
        for flip in range(2 if steps < 4 else 1):
            chains[flip] = over_row(chains[flip], RING)
            mine[flip, steps] = chains[flip]
    theirs = [over_row(mine[key], CORE) for key in MINE]
    return [plane] + [mine[key] for key in MINE] + theirs


def add(*parts):
    total = parts[0].astype(F32)
    for part in parts[1:]:
        total = total + part.astype(F32)
    return total.astype(BF16)


def scatter_gradient(soon, later, mine, own, chains, beside):
    came_soon = over_row(soon, CORE)
    came_later = over_row(later, CORE)
    turns = {2: 0, 0: 1, 3: 2, 1: 3}

    def chip(steps, sides, *more):
        start = (0 if steps == 4 else LONG + (3 - steps) * PLANE) + turns[sides[0]] * OWN
        size = len(sides) * OWN
        came = came_soon if start < FIRST else came_later
        first = start if start < FIRST else start - FIRST
        return add(mine[start : start + size], came[first : first + size], *more)

    ring = {}
    last = None
    long, short = chains
    for steps, sides in ((4, long), (3, short), (3, long), (2, short), (2, long), (1, short), (1, long)):
        more = [after(ring[sides], last)] if sides in ring else []
        last = chip(steps, sides, *more)
        ring[sides] = over_row(last, RING)
    pieces = {}
    for sides in chains:
        for i, side in enumerate(sides):
            turn = turns[side]
            pieces[side] = (ring[sides][i * OWN : (i + 1) * OWN], own[turn * OWN : (turn + 1) * OWN])
    give = [add(*pieces[2]), add(*pieces[3])]
    got = [over_row(v, X_LO) for v in give]
    result = beside(give)
    got = after(got, result)
    other = over_row(add(*pieces[1], got[1]), CORE)
    return [*pieces[0], got[0], other], result


def body(x_state, langevin_noise, observed, data_weight, sens_tiles, tile_rows, tile_cols, counts):
    row = lax.axis_index("row")
    col = lax.axis_index("col")
    place = jnp.stack([row // QUAD, row % QUAD, col % 2]).astype(jnp.int32)
    start = jnp.stack([row * OWN_Y - HALO, col * OWN_X - HALO, col % 2]).astype(jnp.int32)
    state = x_state.transpose(0, 1, 3, 2)
    noise = langevin_noise.transpose(0, 1, 3, 2)
    own = after(state, (place, start)).reshape(OWN, CH, NZ).astype(BF16)
    tiles = sens_tiles[0, 0]
    rows, cols, count = tile_rows[0, 0], tile_cols[0, 0], counts[0]

    plane, *pieces = gather_slab(own, row % 2)
    part, wide, to_near, to_far = forward(place, rows, cols, count, tiles, plane, pieces)
    came = over_col(part, X_HI)
    near = over_col(to_near, X_HI)
    part = add(part, came)
    parts = [part] + [
        over_col(part, [(i, (i + by) % N_COL) for i in range(N_COL)]) for by in (2, 4, 6)
    ]
    far = over_col(after(to_far, part), ACROSS)
    parts[0] = after(part, (near, far))
    soon, later, mine, kept = adjoint(
        place,
        rows,
        cols,
        count,
        tiles,
        observed.reshape(RB, NZ),
        data_weight.reshape(RB, NZ),
        parts,
    )
    def beside(give):
        return prox_step(start, wide, after(near, give), far, state, noise)

    terms, base = scatter_gradient(soon, later, mine, kept, CHAINS, beside)
    gradient = sum(v.astype(F32) for v in terms)
    out = base - step_size * gradient.reshape(OWN_Y, OWN_X, CH, NZ)
    return out.transpose(0, 1, 3, 2)


def solution(mesh):
    placed = (
        P("row", "col", None, None),
        P("row", "col", None, None),
        P("row"),
        P("row"),
        P("row", "col", None, None, None),
        P("row", "col", None),
        P("row", "col", None),
        P("row", "col"),
    )
    return jax.shard_map(
        body, mesh=mesh, in_specs=placed, out_specs=P("row", "col", None, None), check_vma=False
    )
```

time: 133 us -> 112 us (0.84)
  the two profiles are of different devices: /device:TPU:24 before, /device:TPU:1 now
where the time goes in v2:
time: 112 us; the launch traced here: 111 us
  starting transfers between devices  60.6 us (54%)
  waiting for transfers between devices  30.1 us (27%)
  blocking collectives  9.55 us (9%)
  Pallas kernels  7.07 us (6%)
  other arithmetic  2.83 us (3%)
    ppermute x26, starting transfers between devices, over_row(): return lax.ppermute(value, 'row', pairs)  50.4 us
    ppermute x26, waiting for transfers between devices, over_row(): return lax.ppermute(value, 'row', pairs)  19.7 us
    ppermute x6, waiting for transfers between devices, over_col(): return lax.ppermute(value, 'col', pairs)  10.3 us
    ppermute x6, starting transfers between devices, over_col(): return lax.ppermute(value, 'col', pairs)  10.2 us
    all_gather x1, blocking collectives, gather_slab(): lax.all_gather(own, 'row', axis=0, tiled=True, axis_index_groups=QUADS)  9.55 us
    pallas_call x1, Pallas kernels, prox_step(): pl.pallas_call(prox_kernel, out_shape=jax.ShapeDtypeStruct((OWN_Y, OWN_X,...  3.88 us
  transfers between devices with their start and end apart: 32, of which 17 were waited for; matrix products, arithmetic and copies ran while one was open for 1% of the time, Pallas kernels for 3%

profile of v2, /device:TPU:1, one launch (start us, length us, event | category | flops | bytes accessed | tf_op | source)
XLA Modules:
  0.0 111.0 jit_solution(13529278257001718639)
XLA Ops:
  0.1 1.1 convert_element_type.135
  1.2 9.6 %all_gather.3.plane = bf16[64,32,128]{2,1,0:T(8,128)(2,1)S(1)} all-gather(bf16[16,32,128]{2,1,0:T(8,128)(2,1)S(1)} %bitcast.31), channel_id=1, replica_groups={{0,8,16,24},{32,40,48,56},{64,72,80,88},{96,104,112,120},{128,136,144,1..., dimensions={0}, use_global_device_ids=true | all-gather | bytes 655360 | tf_op jit(solution)/shard_map/all_gather | solution.py:330
  10.8 4.6 %collective-permute-start = (bf16[32,32,128]{2,1,0:T(8,128)(2,1)S(1)}, bf16[32,32,128]{2,1,0:T(8,128)(2,1)S(1)}, u32[]{:S(2)}, u32[]{:S(2)}) collective-permute-start(bf16[32,32,128]{2,1,0:T(8,128)(2,1)S(1)} %get-tuple-element.48), channel_id=1, source_target_pairs={{0,32},{8,232},{16,48},{24,248},{32,64},{40,8},{48,80},{56,24},{64... | collective-permute-start | bytes 786440 | tf_op jit(solution)/shard_map/ppermute | solution.py:61
  15.4 0.7 collective-permute-start.4
  16.1 2.6 %collective-permute-done.rest_0_ = bf16[32,32,128]{2,1,0:T(8,128)(2,1)S(1)} collective-permute-done((bf16[32,32,128]{2,1,0:T(8,128)(2,1)S(1)}, bf16[32,32,128]{2,1,0:T(8,128)(2,1)S(1)}, u32[]{:S(2)}, u32[]{:S(2)}) %collective-permute-start) | collective-permute-done | bytes 262176 | tf_op jit(solution)/shard_map/ppermute | solution.py:61
  18.7 3.1 %collective-permute-start.1 = (bf16[32,32,128]{2,1,0:T(8,128)(2,1)S(1)}, bf16[32,32,128]{2,1,0:T(8,128)(2,1)S(1)}, u32[]{:S(2)}, u32[]{:S(2)}) collective-permute-start(bf16[32,32,128]{2,1,0:T(8,128)(2,1)S(1)} %collective-permute-done.rest_0_), channel_id=1, source_target_pairs={{0,32},{8,232},{16,48},{24,248},{32,64},{40,8},{48,80},{56,24},{64... | collective-permute-start | bytes 786440 | tf_op jit(solution)/shard_map/ppermute | solution.py:61
  21.9 2.8 %collective-permute-start.5 = (bf16[32,32,128]{2,1,0:T(8,128)(2,1)S(1)}, bf16[32,32,128]{2,1,0:T(8,128)(2,1)S(1)}, u32[]{:S(2)}, u32[]{:S(2)}) collective-permute-start(bf16[32,32,128]{2,1,0:T(8,128)(2,1)S(1)} %collective-permute-done.4.rest_4_), channel_id=1, source_target_pairs={{0,32},{8,232},{16,48},{24,248},{32,64},{40,8},{48,80},{56,24},{64... | collective-permute-start | bytes 786440 | tf_op jit(solution)/shard_map/ppermute | solution.py:61
  24.7 0.5 collective-permute-done.1.rest_1_
  25.2 3.1 %collective-permute-start.2 = (bf16[32,32,128]{2,1,0:T(8,128)(2,1)S(1)}, bf16[32,32,128]{2,1,0:T(8,128)(2,1)S(1)}, u32[]{:S(2)}, u32[]{:S(2)}) collective-permute-start(bf16[32,32,128]{2,1,0:T(8,128)(2,1)S(1)} %collective-permute-done.1.rest_1_), channel_id=1, source_target_pairs={{0,32},{8,232},{16,48},{24,248},{32,64},{40,8},{48,80},{56,24},{64... | collective-permute-start | bytes 786440 | tf_op jit(solution)/shard_map/ppermute | solution.py:61
  28.3 0.5 collective-permute-start.7
  28.8 2.3 %collective-permute-start.6 = (bf16[32,32,128]{2,1,0:T(8,128)(2,1)S(1)}, bf16[32,32,128]{2,1,0:T(8,128)(2,1)S(1)}, u32[]{:S(2)}, u32[]{:S(2)}) collective-permute-start(bf16[32,32,128]{2,1,0:T(8,128)(2,1)S(1)} %collective-permute-done.5.rest_5_), channel_id=1, source_target_pairs={{0,32},{8,232},{16,48},{24,248},{32,64},{40,8},{48,80},{56,24},{64... | collective-permute-start | bytes 786440 | tf_op jit(solution)/shard_map/ppermute | solution.py:61
  31.1 0.5 collective-permute-done.2.rest_2_
  31.6 3.1 %collective-permute-start.3 = (bf16[32,32,128]{2,1,0:T(8,128)(2,1)S(1)}, bf16[32,32,128]{2,1,0:T(8,128)(2,1)S(1)}, u32[]{:S(2)}, u32[]{:S(2)}) collective-permute-start(bf16[32,32,128]{2,1,0:T(8,128)(2,1)S(1)} %collective-permute-done.2.rest_2_), channel_id=1, source_target_pairs={{0,32},{8,232},{16,48},{24,248},{32,64},{40,8},{48,80},{56,24},{64... | collective-permute-start | bytes 786440 | tf_op jit(solution)/shard_map/ppermute | solution.py:61
  34.7 0.7 collective-permute-start.12
  35.5 0.4 collective-permute-start.9
  35.9 2.3 %collective-permute-start.13 = (bf16[32,32,128]{2,1,0:T(8,128)(2,1)S(1)}, bf16[32,32,128]{2,1,0:T(8,128)(2,1)S(1)}, u32[]{:S(2)}, u32[]{:S(2)}) collective-permute-start(bf16[32,32,128]{2,1,0:T(8,128)(2,1)S(1)} %collective-permute-done.6.rest_6_), channel_id=1, source_target_pairs={{0,8},{8,0},{16,24},{24,16},{32,40},{40,32},{48,56},{56,48},{64,72... | collective-permute-start | bytes 786440 | tf_op jit(solution)/shard_map/ppermute | solution.py:61
  38.2 4.8 %collective-permute-start.10 = (bf16[32,32,128]{2,1,0:T(8,128)(2,1)S(1)}, bf16[32,32,128]{2,1,0:T(8,128)(2,1)S(1)}, u32[]{:S(2)}, u32[]{:S(2)}) collective-permute-start(bf16[32,32,128]{2,1,0:T(8,128)(2,1)S(1)} %collective-permute-done.3.rest_3_), channel_id=1, source_target_pairs={{0,8},{8,0},{16,24},{24,16},{32,40},{40,32},{48,56},{56,48},{64,72... | collective-permute-start | bytes 786440 | tf_op jit(solution)/shard_map/ppermute | solution.py:61
  43.7 0.5 collective-permute-done.10.rest_10_
  44.1 1.4 %forward_tiles.1 = (bf16[8,32,128]{2,1,0:T(8,128)(2,1)S(1)}, bf16[8,8,32,128]{3,2,1,0:T(8,128)(2,1)S(1)}, bf16[8,3,32,128]{3,2,1,0:T(8,128)(2,1)S(1)}, bf16[8,3,32,128]{3,2,1,0:T(8,128)(2,1)S(1)}) custom-call(s32[3]{0:T(128)S(1)} %get-tuple-element.50.place, s32[48]{0:T(128)S(1)} %bitcast.26, s32[48]{0:T(128)S(1)} %bitcast.28, s32[1]{0:T(128)} %bitcast.17.count, ...), custom_call_target="tpu_custom_call" | custom-call | flops 50331648 | bytes 12582912 | tf_op jit(solution)/shard_map/forward_tiles/pallas_call | solution.py:119
  45.6 3.8 %collective-permute-start.15 = (bf16[8,32,128]{2,1,0:T(8,128)(2,1)S(1)}, bf16[8,32,128]{2,1,0:T(8,128)(2,1)S(1)}, u32[]{:S(2)}, u32[]{:S(2)}) collective-permute-start(bf16[8,32,128]{2,1,0:T(8,128)(2,1)S(1)} %get-tuple-element.27), channel_id=1, source_target_pairs={{0,1},{1,0},{2,3},{3,2},{4,5},{5,4},{6,7},{7,6},{8,9},{9,8},{10,11... | collective-permute-start | bytes 196616 | tf_op jit(solution)/shard_map/ppermute | solution.py:65
  49.5 2.2 %collective-permute-done.15 = bf16[8,32,128]{2,1,0:T(8,128)(2,1)S(1)} collective-permute-done((bf16[8,32,128]{2,1,0:T(8,128)(2,1)S(1)}, bf16[8,32,128]{2,1,0:T(8,128)(2,1)S(1)}, u32[]{:S(2)}, u32[]{:S(2)}) %collective-permute-start.15) | collective-permute-done | bytes 65568 | tf_op jit(solution)/shard_map/ppermute | solution.py:65
  51.7 3.6 %collective-permute-start.16 = (bf16[8,3,32,128]{3,2,1,0:T(8,128)(2,1)S(1)}, bf16[8,3,32,128]{3,2,1,0:T(8,128)(2,1)S(1)}, u32[]{:S(2)}, u32[]{:S(2)}) collective-permute-start(bf16[8,3,32,128]{3,2,1,0:T(8,128)(2,1)S(1)} %get-tuple-element.29), channel_id=1, source_target_pairs={{0,7},{1,2},{2,1},{3,4},{4,3},{5,6},{6,5},{7,0},{8,15},{9,10},{10,... | collective-permute-start | bytes 589832 | tf_op jit(solution)/shard_map/ppermute | solution.py:65
  55.3 0.5 collective-permute-start.19
  55.8 2.3 %collective-permute-start.18 = (bf16[8,32,128]{2,1,0:T(8,128)(2,1)S(1)}, bf16[8,32,128]{2,1,0:T(8,128)(2,1)S(1)}, u32[]{:S(2)}, u32[]{:S(2)}) collective-permute-start(bf16[8,32,128]{2,1,0:T(8,128)(2,1)S(1)} %add_convert_fusion.10.rest_0_), channel_id=1, source_target_pairs={{0,4},{1,5},{2,6},{3,7},{4,0},{5,1},{6,2},{7,3},{8,12},{9,13},{10,... | collective-permute-start | bytes 196616 | tf_op jit(solution)/shard_map/ppermute | solution.py:65
  58.0 4.4 %collective-permute-done.16.far = bf16[8,3,32,128]{3,2,1,0:T(8,128)(2,1)S(1)} collective-permute-done((bf16[8,3,32,128]{3,2,1,0:T(8,128)(2,1)S(1)}, bf16[8,3,32,128]{3,2,1,0:T(8,128)(2,1)S(1)}, u32[]{:S(2)}, u32[]{:S(2)}) %collective-permute-start.16) | collective-permute-done | bytes 196640 | tf_op jit(solution)/shard_map/ppermute | solution.py:65
  62.4 1.8 %collective-permute-done.18.rest_2_ = bf16[8,32,128]{2,1,0:T(8,128)(2,1)S(1)} collective-permute-done((bf16[8,32,128]{2,1,0:T(8,128)(2,1)S(1)}, bf16[8,32,128]{2,1,0:T(8,128)(2,1)S(1)}, u32[]{:S(2)}, u32[]{:S(2)}) %collective-permute-start.18) | collective-permute-done | bytes 65568 | tf_op jit(solution)/shard_map/ppermute | solution.py:65
  64.3 1.9 %collective-permute-done.17.rest_1_ = bf16[8,32,128]{2,1,0:T(8,128)(2,1)S(1)} collective-permute-done((bf16[8,32,128]{2,1,0:T(8,128)(2,1)S(1)}, bf16[8,32,128]{2,1,0:T(8,128)(2,1)S(1)}, u32[]{:S(2)}, u32[]{:S(2)}) %collective-permute-start.17) | collective-permute-done | bytes 65568 | tf_op jit(solution)/shard_map/ppermute | solution.py:65
  66.1 1.8 %adjoint_tiles.1 = (bf16[96,32,128]{2,1,0:T(8,128)(2,1)S(1)}, bf16[128,32,128]{2,1,0:T(8,128)(2,1)S(1)}, bf16[224,32,128]{2,1,0:T(8,128)(2,1)S(1)}, bf16[64,32,128]{2,1,0:T(8,128)(2,1)S(1)}) custom-call(s32[3]{0:T(128)S(1)} %get-tuple-element.50.place, s32[48]{0:T(128)S(1)} %bitcast.27, s32[48]{0:T(128)S(1)} %bitcast.29, s32[1]{0:T(128)} %bitcast.18.count, ...), custom_call_target="tpu_custom_call" | custom-call | flops 50331648 | bytes 12582912 | tf_op jit(solution)/shard_map/adjoint_tiles/pallas_call | solution.py:221
  67.9 1.2 %collective-permute-start.21 = (bf16[96,32,128]{2,1,0:T(8,128)(2,1)S(1)}, bf16[96,32,128]{2,1,0:T(8,128)(2,1)S(1)}, u32[]{:S(2)}, u32[]{:S(2)}) collective-permute-start(bf16[96,32,128]{2,1,0:T(8,128)(2,1)S(1)} %get-tuple-element.33), channel_id=1, source_target_pairs={{0,8},{8,0},{16,24},{24,16},{32,40},{40,32},{48,56},{56,48},{64,72... | collective-permute-start | bytes 2359304 | tf_op jit(solution)/shard_map/ppermute | solution.py:61
  69.2 1.8 %collective-permute-done.21 = bf16[96,32,128]{2,1,0:T(8,128)(2,1)S(1)} collective-permute-done((bf16[96,32,128]{2,1,0:T(8,128)(2,1)S(1)}, bf16[96,32,128]{2,1,0:T(8,128)(2,1)S(1)}, u32[]{:S(2)}, u32[]{:S(2)}) %collective-permute-start.21) | collective-permute-done | bytes 786464 | tf_op jit(solution)/shard_map/ppermute | solution.py:61
  71.0 0.1 add_convert_fusion.5
  71.3 2.5 %collective-permute-start.24 = (bf16[32,32,128]{2,1,0:T(8,128)(2,1)S(1)}, bf16[32,32,128]{2,1,0:T(8,128)(2,1)S(1)}, u32[]{:S(2)}, u32[]{:S(2)}) collective-permute-start(bf16[32,32,128]{2,1,0:T(8,128)(2,1)S(1)} %get-tuple-element.43), channel_id=1, source_target_pairs={{0,32},{8,232},{16,48},{24,248},{32,64},{40,8},{48,80},{56,24},{64... | collective-permute-start | bytes 786440 | tf_op jit(solution)/shard_map/ppermute | solution.py:61
  73.8 3.3 %collective-permute-done.22 = bf16[32,32,128]{2,1,0:T(8,128)(2,1)S(1)} collective-permute-done((bf16[32,32,128]{2,1,0:T(8,128)(2,1)S(1)}, bf16[32,32,128]{2,1,0:T(8,128)(2,1)S(1)}, u32[]{:S(2)}, u32[]{:S(2)}) %collective-permute-start.22) | collective-permute-done | bytes 262176 | tf_op jit(solution)/shard_map/ppermute | solution.py:61
  77.2 0.7 collective-permute-start.23
  77.9 2.0 %collective-permute-done.24 = bf16[32,32,128]{2,1,0:T(8,128)(2,1)S(1)} collective-permute-done((bf16[32,32,128]{2,1,0:T(8,128)(2,1)S(1)}, bf16[32,32,128]{2,1,0:T(8,128)(2,1)S(1)}, u32[]{:S(2)}, u32[]{:S(2)}) %collective-permute-start.24) | collective-permute-done | bytes 262176 | tf_op jit(solution)/shard_map/ppermute | solution.py:61
  80.0 0.7 collective-permute-start.26
  80.7 1.8 %collective-permute-done.23 = bf16[32,32,128]{2,1,0:T(8,128)(2,1)S(1)} collective-permute-done((bf16[32,32,128]{2,1,0:T(8,128)(2,1)S(1)}, bf16[32,32,128]{2,1,0:T(8,128)(2,1)S(1)}, u32[]{:S(2)}, u32[]{:S(2)}) %collective-permute-start.23) | collective-permute-done | bytes 262176 | tf_op jit(solution)/shard_map/ppermute | solution.py:61
  82.6 1.9 %collective-permute-start.25 = (bf16[32,32,128]{2,1,0:T(8,128)(2,1)S(1)}, bf16[32,32,128]{2,1,0:T(8,128)(2,1)S(1)}, u32[]{:S(2)}, u32[]{:S(2)}) collective-permute-start(bf16[32,32,128]{2,1,0:T(8,128)(2,1)S(1)} %add_convert_fusion.2), channel_id=1, source_target_pairs={{0,32},{8,232},{16,48},{24,248},{32,64},{40,8},{48,80},{56,24},{64... | collective-permute-start | bytes 786440 | tf_op jit(solution)/shard_map/ppermute | solution.py:61
  84.5 1.1 %collective-permute-done.26 = bf16[32,32,128]{2,1,0:T(8,128)(2,1)S(1)} collective-permute-done((bf16[32,32,128]{2,1,0:T(8,128)(2,1)S(1)}, bf16[32,32,128]{2,1,0:T(8,128)(2,1)S(1)}, u32[]{:S(2)}, u32[]{:S(2)}) %collective-permute-start.26) | collective-permute-done | bytes 262176 | tf_op jit(solution)/shard_map/ppermute | solution.py:61
  85.8 1.6 %collective-permute-start.28 = (bf16[32,32,128]{2,1,0:T(8,128)(2,1)S(1)}, bf16[32,32,128]{2,1,0:T(8,128)(2,1)S(1)}, u32[]{:S(2)}, u32[]{:S(2)}) collective-permute-start(bf16[32,32,128]{2,1,0:T(8,128)(2,1)S(1)} %add_convert_fusion.1), channel_id=1, source_target_pairs={{0,32},{8,232},{16,48},{24,248},{32,64},{40,8},{48,80},{56,24},{64... | collective-permute-start | bytes 786440 | tf_op jit(solution)/shard_map/ppermute | solution.py:61
  87.3 1.2 %collective-permute-done.25 = bf16[32,32,128]{2,1,0:T(8,128)(2,1)S(1)} collective-permute-done((bf16[32,32,128]{2,1,0:T(8,128)(2,1)S(1)}, bf16[32,32,128]{2,1,0:T(8,128)(2,1)S(1)}, u32[]{:S(2)}, u32[]{:S(2)}) %collective-permute-start.25) | collective-permute-done | bytes 262176 | tf_op jit(solution)/shard_map/ppermute | solution.py:61
  88.6 2.5 %collective-permute-start.27 = (bf16[32,32,128]{2,1,0:T(8,128)(2,1)S(1)}, bf16[32,32,128]{2,1,0:T(8,128)(2,1)S(1)}, u32[]{:S(2)}, u32[]{:S(2)}) collective-permute-start(bf16[32,32,128]{2,1,0:T(8,128)(2,1)S(1)} %add_convert_fusion), channel_id=1, source_target_pairs={{0,32},{8,232},{16,48},{24,248},{32,64},{40,8},{48,80},{56,24},{64... | collective-permute-start | bytes 786440 | tf_op jit(solution)/shard_map/ppermute | solution.py:61
  91.1 3.3 %collective-permute-done.27 = bf16[32,32,128]{2,1,0:T(8,128)(2,1)S(1)} collective-permute-done((bf16[32,32,128]{2,1,0:T(8,128)(2,1)S(1)}, bf16[32,32,128]{2,1,0:T(8,128)(2,1)S(1)}, u32[]{:S(2)}, u32[]{:S(2)}) %collective-permute-start.27) | collective-permute-done | bytes 262176 | tf_op jit(solution)/shard_map/ppermute | solution.py:61
  94.5 1.5 %collective-permute-start.30 = (bf16[16,32,128]{2,1,0:T(8,128)(2,1)S(1)}, bf16[16,32,128]{2,1,0:T(8,128)(2,1)S(1)}, u32[]{:S(2)}, u32[]{:S(2)}) collective-permute-start(bf16[16,32,128]{2,1,0:T(8,128)(2,1)S(1)} %get-tuple-element.45), channel_id=1, source_target_pairs={{0,16},{8,24},{16,0},{24,8},{32,48},{40,56},{48,32},{56,40},{64,80... | collective-permute-start | bytes 393224 | tf_op jit(solution)/shard_map/ppermute | solution.py:61
  96.2 3.9 %tv_prox.1 = f32[2,8,32,128]{3,2,1,0:T(8,128)S(1)} custom-call(s32[3]{0:T(128)S(1)} %get-tuple-element.49.start, bf16[8,8,32,128]{3,2,1,0:T(8,128)(2,1)S(1)} %get-tuple-element.25.wide, bf16[8,3,32,128]{3,2,1,0:T(8,128)(2,1)S(1)} %collective-permute-done.14.near, bf16[8,3,32,128]{3,2,1,0:T(8,128)(2,1)S(1)} %collective-permute-done.16.far, ...), custom_call_target="tpu_custom_call" | custom-call | flops 16777216 | bytes 12582912 | tf_op jit(solution)/shard_map/tv_prox/pallas_call | solution.py:312
  100.2 9.0 %collective-permute-start.31 = (bf16[16,32,128]{2,1,0:T(8,128)(2,1)S(1)}, bf16[16,32,128]{2,1,0:T(8,128)(2,1)S(1)}, u32[]{:S(2)}, u32[]{:S(2)}) collective-permute-start(bf16[16,32,128]{2,1,0:T(8,128)(2,1)S(1)} %add_convert_fusion.7), channel_id=1, source_target_pairs={{0,8},{8,0},{16,24},{24,16},{32,40},{40,32},{48,56},{56,48},{64,72... | collective-permute-start | bytes 393224 | tf_op jit(solution)/shard_map/ppermute | solution.py:61
  109.2 1.0 collective-permute-done.31
  110.3 0.7 subtract_bitcast_fusion
  (48 shorter events, 1.5 us)
Async XLA Ops:
  0.0 44.1 %copy-start.6 = (s32[1,1,48]{2,1,0:T(1,128)S(1)}, s32[1,1,48]{2,1,0:T(1,128)}, u32[]{:S(2)}) copy-start(s32[1,1,48]{2,1,0:T(1,128)} %param.14) | copy-start | bytes 580
  0.0 44.1 %copy-start.5 = (s32[1,1,48]{2,1,0:T(1,128)S(1)}, s32[1,1,48]{2,1,0:T(1,128)}, u32[]{:S(2)}) copy-start(s32[1,1,48]{2,1,0:T(1,128)} %param.13) | copy-start | bytes 580
  0.0 44.1 %copy-start = (bf16[1,1,48,128,128]{4,3,2,1,0:T(8,128)(2,1)S(1)}, bf16[1,1,48,128,128]{4,3,2,1,0:T(8,128)(2,1)}, u32[]{:S(2)}) copy-start(bf16[1,1,48,128,128]{4,3,2,1,0:T(8,128)(2,1)} %param.12) | copy-start | bytes 4718596
  10.8 7.9 %collective-permute-start = (bf16[32,32,128]{2,1,0:T(8,128)(2,1)S(1)}, bf16[32,32,128]{2,1,0:T(8,128)(2,1)S(1)}, u32[]{:S(2)}, u32[]{:S(2)}) collective-permute-start(bf16[32,32,128]{2,1,0:T(8,128)(2,1)S(1)} %get-tuple-element.48), channel_id=1, source_target_pairs={{0,32},{8,232},{16,48},{24,248},{32,64},{40,8},{48,80},{56,24},{64... | collective-permute-start | bytes 786440 | tf_op jit(solution)/shard_map/ppermute | solution.py:61
  15.4 6.4 %collective-permute-start.4 = (bf16[32,32,128]{2,1,0:T(8,128)(2,1)S(1)}, bf16[32,32,128]{2,1,0:T(8,128)(2,1)S(1)}, u32[]{:S(2)}, u32[]{:S(2)}) collective-permute-start(bf16[32,32,128]{2,1,0:T(8,128)(2,1)S(1)} %get-tuple-element.47), channel_id=1, source_target_pairs={{0,32},{8,232},{16,48},{24,248},{32,64},{40,8},{48,80},{56,24},{64... | collective-permute-start | bytes 786440 | tf_op jit(solution)/shard_map/ppermute | solution.py:61
  18.7 6.4 %collective-permute-start.1 = (bf16[32,32,128]{2,1,0:T(8,128)(2,1)S(1)}, bf16[32,32,128]{2,1,0:T(8,128)(2,1)S(1)}, u32[]{:S(2)}, u32[]{:S(2)}) collective-permute-start(bf16[32,32,128]{2,1,0:T(8,128)(2,1)S(1)} %collective-permute-done.rest_0_), channel_id=1, source_target_pairs={{0,32},{8,232},{16,48},{24,248},{32,64},{40,8},{48,80},{56,24},{64... | collective-permute-start | bytes 786440 | tf_op jit(solution)/shard_map/ppermute | solution.py:61
  21.9 6.9 %collective-permute-start.5 = (bf16[32,32,128]{2,1,0:T(8,128)(2,1)S(1)}, bf16[32,32,128]{2,1,0:T(8,128)(2,1)S(1)}, u32[]{:S(2)}, u32[]{:S(2)}) collective-permute-start(bf16[32,32,128]{2,1,0:T(8,128)(2,1)S(1)} %collective-permute-done.4.rest_4_), channel_id=1, source_target_pairs={{0,32},{8,232},{16,48},{24,248},{32,64},{40,8},{48,80},{56,24},{64... | collective-permute-start | bytes 786440 | tf_op jit(solution)/shard_map/ppermute | solution.py:61
  25.2 6.4 %collective-permute-start.2 = (bf16[32,32,128]{2,1,0:T(8,128)(2,1)S(1)}, bf16[32,32,128]{2,1,0:T(8,128)(2,1)S(1)}, u32[]{:S(2)}, u32[]{:S(2)}) collective-permute-start(bf16[32,32,128]{2,1,0:T(8,128)(2,1)S(1)} %collective-permute-done.1.rest_1_), channel_id=1, source_target_pairs={{0,32},{8,232},{16,48},{24,248},{32,64},{40,8},{48,80},{56,24},{64... | collective-permute-start | bytes 786440 | tf_op jit(solution)/shard_map/ppermute | solution.py:61
  28.3 7.1 %collective-permute-start.11 = (bf16[32,32,128]{2,1,0:T(8,128)(2,1)S(1)}, bf16[32,32,128]{2,1,0:T(8,128)(2,1)S(1)}, u32[]{:S(2)}, u32[]{:S(2)}) collective-permute-start(bf16[32,32,128]{2,1,0:T(8,128)(2,1)S(1)} %collective-permute-done.4.rest_4_), channel_id=1, source_target_pairs={{0,8},{8,0},{16,24},{24,16},{32,40},{40,32},{48,56},{56,48},{64,72... | collective-permute-start | bytes 786440 | tf_op jit(solution)/shard_map/ppermute | solution.py:61
  28.3 7.2 %collective-permute-start.7 = (bf16[32,32,128]{2,1,0:T(8,128)(2,1)S(1)}, bf16[32,32,128]{2,1,0:T(8,128)(2,1)S(1)}, u32[]{:S(2)}, u32[]{:S(2)}) collective-permute-start(bf16[32,32,128]{2,1,0:T(8,128)(2,1)S(1)} %collective-permute-done.rest_0_), channel_id=1, source_target_pairs={{0,8},{8,0},{16,24},{24,16},{32,40},{40,32},{48,56},{56,48},{64,72... | collective-permute-start | bytes 786440 | tf_op jit(solution)/shard_map/ppermute | solution.py:61
  28.8 7.1 %collective-permute-start.6 = (bf16[32,32,128]{2,1,0:T(8,128)(2,1)S(1)}, bf16[32,32,128]{2,1,0:T(8,128)(2,1)S(1)}, u32[]{:S(2)}, u32[]{:S(2)}) collective-permute-start(bf16[32,32,128]{2,1,0:T(8,128)(2,1)S(1)} %collective-permute-done.5.rest_5_), channel_id=1, source_target_pairs={{0,32},{8,232},{16,48},{24,248},{32,64},{40,8},{48,80},{56,24},{64... | collective-permute-start | bytes 786440 | tf_op jit(solution)/shard_map/ppermute | solution.py:61
  31.6 6.6 %collective-permute-start.3 = (bf16[32,32,128]{2,1,0:T(8,128)(2,1)S(1)}, bf16[32,32,128]{2,1,0:T(8,128)(2,1)S(1)}, u32[]{:S(2)}, u32[]{:S(2)}) collective-permute-start(bf16[32,32,128]{2,1,0:T(8,128)(2,1)S(1)} %collective-permute-done.2.rest_2_), channel_id=1, source_target_pairs={{0,32},{8,232},{16,48},{24,248},{32,64},{40,8},{48,80},{56,24},{64... | collective-permute-start | bytes 786440 | tf_op jit(solution)/shard_map/ppermute | solution.py:61
  34.7 8.9 %collective-permute-start.12 = (bf16[32,32,128]{2,1,0:T(8,128)(2,1)S(1)}, bf16[32,32,128]{2,1,0:T(8,128)(2,1)S(1)}, u32[]{:S(2)}, u32[]{:S(2)}) collective-permute-start(bf16[32,32,128]{2,1,0:T(8,128)(2,1)S(1)} %collective-permute-done.5.rest_5_), channel_id=1, source_target_pairs={{0,8},{8,0},{16,24},{24,16},{32,40},{40,32},{48,56},{56,48},{64,72... | collective-permute-start | bytes 786440 | tf_op jit(solution)/shard_map/ppermute | solution.py:61
  35.4 8.2 %collective-permute-start.8 = (bf16[32,32,128]{2,1,0:T(8,128)(2,1)S(1)}, bf16[32,32,128]{2,1,0:T(8,128)(2,1)S(1)}, u32[]{:S(2)}, u32[]{:S(2)}) collective-permute-start(bf16[32,32,128]{2,1,0:T(8,128)(2,1)S(1)} %collective-permute-done.1.rest_1_), channel_id=1, source_target_pairs={{0,8},{8,0},{16,24},{24,16},{32,40},{40,32},{48,56},{56,48},{64,72... | collective-permute-start | bytes 786440 | tf_op jit(solution)/shard_map/ppermute | solution.py:61
  35.5 8.2 %collective-permute-start.9 = (bf16[32,32,128]{2,1,0:T(8,128)(2,1)S(1)}, bf16[32,32,128]{2,1,0:T(8,128)(2,1)S(1)}, u32[]{:S(2)}, u32[]{:S(2)}) collective-permute-start(bf16[32,32,128]{2,1,0:T(8,128)(2,1)S(1)} %collective-permute-done.2.rest_2_), channel_id=1, source_target_pairs={{0,8},{8,0},{16,24},{24,16},{32,40},{40,32},{48,56},{56,48},{64,72... | collective-permute-start | bytes 786440 | tf_op jit(solution)/shard_map/ppermute | solution.py:61
  35.9 7.7 %collective-permute-start.13 = (bf16[32,32,128]{2,1,0:T(8,128)(2,1)S(1)}, bf16[32,32,128]{2,1,0:T(8,128)(2,1)S(1)}, u32[]{:S(2)}, u32[]{:S(2)}) collective-permute-start(bf16[32,32,128]{2,1,0:T(8,128)(2,1)S(1)} %collective-permute-done.6.rest_6_), channel_id=1, source_target_pairs={{0,8},{8,0},{16,24},{24,16},{32,40},{40,32},{48,56},{56,48},{64,72... | collective-permute-start | bytes 786440 | tf_op jit(solution)/shard_map/ppermute | solution.py:61
  38.2 5.9 %collective-permute-start.10 = (bf16[32,32,128]{2,1,0:T(8,128)(2,1)S(1)}, bf16[32,32,128]{2,1,0:T(8,128)(2,1)S(1)}, u32[]{:S(2)}, u32[]{:S(2)}) collective-permute-start(bf16[32,32,128]{2,1,0:T(8,128)(2,1)S(1)} %collective-permute-done.3.rest_3_), channel_id=1, source_target_pairs={{0,8},{8,0},{16,24},{24,16},{32,40},{40,32},{48,56},{56,48},{64,72... | collective-permute-start | bytes 786440 | tf_op jit(solution)/shard_map/ppermute | solution.py:61
  44.1 22.0 %copy-start.3 = (f32[1024]{0:T(1024)S(1)}, f32[1024]{0:T(1024)}, u32[]{:S(2)}) copy-start(f32[1024]{0:T(1024)} %param.10) | copy-start | bytes 12292
  44.1 22.0 %copy-start.4 = (f32[1024]{0:T(1024)S(1)}, f32[1024]{0:T(1024)}, u32[]{:S(2)}) copy-start(f32[1024]{0:T(1024)} %param.11) | copy-start | bytes 12292
  45.6 6.1 %collective-permute-start.15 = (bf16[8,32,128]{2,1,0:T(8,128)(2,1)S(1)}, bf16[8,32,128]{2,1,0:T(8,128)(2,1)S(1)}, u32[]{:S(2)}, u32[]{:S(2)}) collective-permute-start(bf16[8,32,128]{2,1,0:T(8,128)(2,1)S(1)} %get-tuple-element.27), channel_id=1, source_target_pairs={{0,1},{1,0},{2,3},{3,2},{4,5},{5,4},{6,7},{7,6},{8,9},{9,8},{10,11... | collective-permute-start | bytes 196616 | tf_op jit(solution)/shard_map/ppermute | solution.py:65
  49.4 8.6 %collective-permute-start.14 = (bf16[8,3,32,128]{3,2,1,0:T(8,128)(2,1)S(1)}, bf16[8,3,32,128]{3,2,1,0:T(8,128)(2,1)S(1)}, u32[]{:S(2)}, u32[]{:S(2)}) collective-permute-start(bf16[8,3,32,128]{3,2,1,0:T(8,128)(2,1)S(1)} %get-tuple-element.26), channel_id=1, source_target_pairs={{0,1},{1,0},{2,3},{3,2},{4,5},{5,4},{6,7},{7,6},{8,9},{9,8},{10,11... | collective-permute-start | bytes 589832 | tf_op jit(solution)/shard_map/ppermute | solution.py:65
  51.7 10.7 %collective-permute-start.16 = (bf16[8,3,32,128]{3,2,1,0:T(8,128)(2,1)S(1)}, bf16[8,3,32,128]{3,2,1,0:T(8,128)(2,1)S(1)}, u32[]{:S(2)}, u32[]{:S(2)}) collective-permute-start(bf16[8,3,32,128]{3,2,1,0:T(8,128)(2,1)S(1)} %get-tuple-element.29), channel_id=1, source_target_pairs={{0,7},{1,2},{2,1},{3,4},{4,3},{5,6},{6,5},{7,0},{8,15},{9,10},{10,... | collective-permute-start | bytes 589832 | tf_op jit(solution)/shard_map/ppermute | solution.py:65
  55.3 7.1 %collective-permute-start.19 = (bf16[8,32,128]{2,1,0:T(8,128)(2,1)S(1)}, bf16[8,32,128]{2,1,0:T(8,128)(2,1)S(1)}, u32[]{:S(2)}, u32[]{:S(2)}) collective-permute-start(bf16[8,32,128]{2,1,0:T(8,128)(2,1)S(1)} %add_convert_fusion.10.rest_0_), channel_id=1, source_target_pairs={{0,6},{1,7},{2,0},{3,1},{4,2},{5,3},{6,4},{7,5},{8,14},{9,15},{10,... | collective-permute-start | bytes 196616 | tf_op jit(solution)/shard_map/ppermute | solution.py:65
  55.8 8.5 %collective-permute-start.18 = (bf16[8,32,128]{2,1,0:T(8,128)(2,1)S(1)}, bf16[8,32,128]{2,1,0:T(8,128)(2,1)S(1)}, u32[]{:S(2)}, u32[]{:S(2)}) collective-permute-start(bf16[8,32,128]{2,1,0:T(8,128)(2,1)S(1)} %add_convert_fusion.10.rest_0_), channel_id=1, source_target_pairs={{0,4},{1,5},{2,6},{3,7},{4,0},{5,1},{6,2},{7,3},{8,12},{9,13},{10,... | collective-permute-start | bytes 196616 | tf_op jit(solution)/shard_map/ppermute | solution.py:65
  58.0 8.1 %collective-permute-start.17 = (bf16[8,32,128]{2,1,0:T(8,128)(2,1)S(1)}, bf16[8,32,128]{2,1,0:T(8,128)(2,1)S(1)}, u32[]{:S(2)}, u32[]{:S(2)}) collective-permute-start(bf16[8,32,128]{2,1,0:T(8,128)(2,1)S(1)} %add_convert_fusion.10.rest_0_), channel_id=1, source_target_pairs={{0,2},{1,3},{2,4},{3,5},{4,6},{5,7},{6,0},{7,1},{8,10},{9,11},{10,... | collective-permute-start | bytes 196616 | tf_op jit(solution)/shard_map/ppermute | solution.py:65
  67.9 3.1 %collective-permute-start.21 = (bf16[96,32,128]{2,1,0:T(8,128)(2,1)S(1)}, bf16[96,32,128]{2,1,0:T(8,128)(2,1)S(1)}, u32[]{:S(2)}, u32[]{:S(2)}) collective-permute-start(bf16[96,32,128]{2,1,0:T(8,128)(2,1)S(1)} %get-tuple-element.33), channel_id=1, source_target_pairs={{0,8},{8,0},{16,24},{24,16},{32,40},{40,32},{48,56},{56,48},{64,72... | collective-permute-start | bytes 2359304 | tf_op jit(solution)/shard_map/ppermute | solution.py:61
  69.1 10.8 %collective-permute-start.20 = (bf16[128,32,128]{2,1,0:T(8,128)(2,1)S(1)}, bf16[128,32,128]{2,1,0:T(8,128)(2,1)S(1)}, u32[]{:S(2)}, u32[]{:S(2)}) collective-permute-start(bf16[128,32,128]{2,1,0:T(8,128)(2,1)S(1)} %get-tuple-element.32), channel_id=1, source_target_pairs={{0,8},{8,0},{16,24},{24,16},{32,40},{40,32},{48,56},{56,48},{64,72... | collective-permute-start | bytes 3145736 | tf_op jit(solution)/shard_map/ppermute | solution.py:61
  71.2 5.9 %collective-permute-start.22 = (bf16[32,32,128]{2,1,0:T(8,128)(2,1)S(1)}, bf16[32,32,128]{2,1,0:T(8,128)(2,1)S(1)}, u32[]{:S(2)}, u32[]{:S(2)}) collective-permute-start(bf16[32,32,128]{2,1,0:T(8,128)(2,1)S(1)} %get-tuple-element.44), channel_id=1, source_target_pairs={{0,32},{8,232},{16,48},{24,248},{32,64},{40,8},{48,80},{56,24},{64... | collective-permute-start | bytes 786440 | tf_op jit(solution)/shard_map/ppermute | solution.py:61
  71.3 8.6 %collective-permute-start.24 = (bf16[32,32,128]{2,1,0:T(8,128)(2,1)S(1)}, bf16[32,32,128]{2,1,0:T(8,128)(2,1)S(1)}, u32[]{:S(2)}, u32[]{:S(2)}) collective-permute-start(bf16[32,32,128]{2,1,0:T(8,128)(2,1)S(1)} %get-tuple-element.43), channel_id=1, source_target_pairs={{0,32},{8,232},{16,48},{24,248},{32,64},{40,8},{48,80},{56,24},{64... | collective-permute-start | bytes 786440 | tf_op jit(solution)/shard_map/ppermute | solution.py:61
  77.2 5.3 %collective-permute-start.23 = (bf16[32,32,128]{2,1,0:T(8,128)(2,1)S(1)}, bf16[32,32,128]{2,1,0:T(8,128)(2,1)S(1)}, u32[]{:S(2)}, u32[]{:S(2)}) collective-permute-start(bf16[32,32,128]{2,1,0:T(8,128)(2,1)S(1)} %add_convert_fusion.4), channel_id=1, source_target_pairs={{0,32},{8,232},{16,48},{24,248},{32,64},{40,8},{48,80},{56,24},{64... | collective-permute-start | bytes 786440 | tf_op jit(solution)/shard_map/ppermute | solution.py:61
  80.0 16.1 %copy-start.1 = (f32[2,8,128,32]{2,3,1,0:T(8,128)S(1)}, f32[2,8,128,32]{2,3,1,0:T(8,128)}, u32[]{:S(2)}) copy-start(f32[2,8,128,32]{2,3,1,0:T(8,128)} %param.8) | copy-start | bytes 786436
  80.0 16.1 %copy-start.2 = (f32[2,8,128,32]{2,3,1,0:T(8,128)S(1)}, f32[2,8,128,32]{2,3,1,0:T(8,128)}, u32[]{:S(2)}) copy-start(f32[2,8,128,32]{2,3,1,0:T(8,128)} %param.9) | copy-start | bytes 786436
  80.0 5.6 %collective-permute-start.26 = (bf16[32,32,128]{2,1,0:T(8,128)(2,1)S(1)}, bf16[32,32,128]{2,1,0:T(8,128)(2,1)S(1)}, u32[]{:S(2)}, u32[]{:S(2)}) collective-permute-start(bf16[32,32,128]{2,1,0:T(8,128)(2,1)S(1)} %add_convert_fusion.3), channel_id=1, source_target_pairs={{0,32},{8,232},{16,48},{24,248},{32,64},{40,8},{48,80},{56,24},{64... | collective-permute-start | bytes 786440 | tf_op jit(solution)/shard_map/ppermute | solution.py:61
  82.6 5.9 %collective-permute-start.25 = (bf16[32,32,128]{2,1,0:T(8,128)(2,1)S(1)}, bf16[32,32,128]{2,1,0:T(8,128)(2,1)S(1)}, u32[]{:S(2)}, u32[]{:S(2)}) collective-permute-start(bf16[32,32,128]{2,1,0:T(8,128)(2,1)S(1)} %add_convert_fusion.2), channel_id=1, source_target_pairs={{0,32},{8,232},{16,48},{24,248},{32,64},{40,8},{48,80},{56,24},{64... | collective-permute-start | bytes 786440 | tf_op jit(solution)/shard_map/ppermute | solution.py:61
  85.8 5.4 %collective-permute-start.28 = (bf16[32,32,128]{2,1,0:T(8,128)(2,1)S(1)}, bf16[32,32,128]{2,1,0:T(8,128)(2,1)S(1)}, u32[]{:S(2)}, u32[]{:S(2)}) collective-permute-start(bf16[32,32,128]{2,1,0:T(8,128)(2,1)S(1)} %add_convert_fusion.1), channel_id=1, source_target_pairs={{0,32},{8,232},{16,48},{24,248},{32,64},{40,8},{48,80},{56,24},{64... | collective-permute-start | bytes 786440 | tf_op jit(solution)/shard_map/ppermute | solution.py:61
  88.6 5.8 %collective-permute-start.27 = (bf16[32,32,128]{2,1,0:T(8,128)(2,1)S(1)}, bf16[32,32,128]{2,1,0:T(8,128)(2,1)S(1)}, u32[]{:S(2)}, u32[]{:S(2)}) collective-permute-start(bf16[32,32,128]{2,1,0:T(8,128)(2,1)S(1)} %add_convert_fusion), channel_id=1, source_target_pairs={{0,32},{8,232},{16,48},{24,248},{32,64},{40,8},{48,80},{56,24},{64... | collective-permute-start | bytes 786440 | tf_op jit(solution)/shard_map/ppermute | solution.py:61
  94.5 5.5 %collective-permute-start.30 = (bf16[16,32,128]{2,1,0:T(8,128)(2,1)S(1)}, bf16[16,32,128]{2,1,0:T(8,128)(2,1)S(1)}, u32[]{:S(2)}, u32[]{:S(2)}) collective-permute-start(bf16[16,32,128]{2,1,0:T(8,128)(2,1)S(1)} %get-tuple-element.45), channel_id=1, source_target_pairs={{0,16},{8,24},{16,0},{24,8},{32,48},{40,56},{48,32},{56,40},{64,80... | collective-permute-start | bytes 393224 | tf_op jit(solution)/shard_map/ppermute | solution.py:61
  96.0 4.1 %collective-permute-start.29 = (bf16[16,32,128]{2,1,0:T(8,128)(2,1)S(1)}, bf16[16,32,128]{2,1,0:T(8,128)(2,1)S(1)}, u32[]{:S(2)}, u32[]{:S(2)}) collective-permute-start(bf16[16,32,128]{2,1,0:T(8,128)(2,1)S(1)} %get-tuple-element.46), channel_id=1, source_target_pairs={{0,16},{8,24},{16,0},{24,8},{32,48},{40,56},{48,32},{56,40},{64,80... | collective-permute-start | bytes 393224 | tf_op jit(solution)/shard_map/ppermute | solution.py:61
  100.2 10.0 %collective-permute-start.31 = (bf16[16,32,128]{2,1,0:T(8,128)(2,1)S(1)}, bf16[16,32,128]{2,1,0:T(8,128)(2,1)S(1)}, u32[]{:S(2)}, u32[]{:S(2)}) collective-permute-start(bf16[16,32,128]{2,1,0:T(8,128)(2,1)S(1)} %add_convert_fusion.7), channel_id=1, source_target_pairs={{0,8},{8,0},{16,24},{24,16},{32,40},{40,32},{48,56},{56,48},{64,72... | collective-permute-start | bytes 393224 | tf_op jit(solution)/shard_map/ppermute | solution.py:61

commit v3 on v2

--- a/solution.py
+++ b/solution.py
@@ -40,6 +40,7 @@
 LONG = 2 * OWN
 SENT = LONG + 3 * PLANE
 FIRST = LONG + PLANE
+KEPT = SENT + PLANE
 
 CORE = [(i, i ^ 1) for i in range(N_ROW)]
 X_HI = [(i, i ^ 1) for i in range(N_COL)]
@@ -142,7 +143,7 @@
 def adjoint_kernel(
     place, rows, cols, count, tiles, observed, weight, *rest
 ):
-    parts, (soon, later, mine, own, residual, total, first) = rest[:4], rest[4:]
+    parts, (soon, later, kept, residual, total, first) = rest[:4], rest[4:]
     z = place[0]
     quad = place[1]
     core = quad & 1
@@ -155,8 +156,7 @@
     total[...] = jnp.zeros_like(total)
     soon[...] = jnp.zeros_like(soon)
     later[...] = jnp.zeros_like(later)
-    mine[...] = jnp.zeros_like(mine)
-    own[...] = jnp.zeros_like(own)
+    kept[...] = jnp.zeros_like(kept)
 
     def mark(index, carry):
         slot = used - 1 - index
@@ -164,73 +164,63 @@
         return carry
 
     lax.fori_loop(0, used, mark, 0)
+    groups = (used + GROUP - 1) // GROUP
 
     def group(index, carry):
         terms = []
         for u in range(GROUP):
             slot = index * GROUP + u
-            term = lax.dot_general(
-                residual[rows[slot]], tiles[slot], (((1,), (0,)), ((), ())), preferred_element_type=F32
+            terms.append(
+                lax.dot_general(
+                    residual[rows[slot]], tiles[slot], (((1,), (0,)), ((), ())), preferred_element_type=F32
+                )
             )
-            terms.append(term)
         for u in range(GROUP):
             slot = index * GROUP + u
-
-            @pl.when(slot < used)
-            def _():
-                total[first[cols[slot]]] += terms[u]
-
+            total[jnp.where(slot < used, first[cols[slot]], SLOTS)] += terms[u]
         return carry
 
-    lax.fori_loop(0, (used + GROUP - 1) // GROUP, group, 0)
-
-    def place_line(slot, carry):
+    lax.fori_loop(0, groups, group, 0)
+
+    def place_line(slot):
         line = cols[slot]
-        value = total[first[line]].astype(BF16)
         away = lax.rem(line // PLANE - z + N_Z, N_Z)
         other = lax.rem(line // OWN, QUAD)
         inner = lax.rem(line, OWN)
         carrier = jnp.where(away == 4, other & 1, jnp.where(away < 4, 0, 1))
         steps = jnp.where(carrier == 0, away, N_Z - away)
-        turn = 2 * ((other & 1) ^ carrier) + 1 - ((other // 2) ^ (quad // 2))
-        where = jnp.where(steps == 4, 0, LONG + (3 - steps) * PLANE) + turn * OWN + inner
-        own_place = (2 * ((other & 1) ^ core) + 1 - ((other // 2) ^ (quad // 2))) * OWN + inner
-
-        @pl.when(away == 0)
-        def _():
-            own[own_place] = value
-
-        @pl.when((away != 0) & (carrier == core))
-        def _():
-            mine[where] = value
-
-        @pl.when((away != 0) & (carrier != core) & (where < FIRST))
-        def _():
-            soon[where] = value
-
-        @pl.when((away != 0) & (carrier != core) & (where >= FIRST))
-        def _():
-            later[where - FIRST] = value
-
+        across = 1 - ((other // 2) ^ (quad // 2))
+        where = (2 * ((other & 1) ^ carrier) + across) * OWN + inner
+        where = jnp.where(steps == 4, 0, LONG + (3 - steps) * PLANE) + where
+        near = SENT + (2 * ((other & 1) ^ core) + across) * OWN + inner
+        here = (away == 0) | (carrier == core)
+        good = slot < used
+        value = total[jnp.where(good, first[line], SLOTS)].astype(BF16)
+        kept[jnp.where(good & here, jnp.where(away == 0, near, where), KEPT)] = value
+        soon[jnp.where(good & ~here & (where < FIRST), where, FIRST)] = value
+        later[jnp.where(good & ~here & (where >= FIRST), where - FIRST, SENT - FIRST)] = value
+
+    def place_group(index, carry):
+        for u in range(GROUP):
+            place_line(index * GROUP + u)
         return carry
 
-    lax.fori_loop(0, used, place_line, 0)
+    lax.fori_loop(0, groups, place_group, 0)
 
 
 def adjoint(place, rows, cols, count, tiles, observed, weight, parts):
     return pl.pallas_call(
         adjoint_kernel,
         out_shape=[
-            jax.ShapeDtypeStruct((FIRST, CH, NZ), BF16),
-            jax.ShapeDtypeStruct((SENT - FIRST, CH, NZ), BF16),
-            jax.ShapeDtypeStruct((SENT, CH, NZ), BF16),
-            jax.ShapeDtypeStruct((PLANE, CH, NZ), BF16),
+            jax.ShapeDtypeStruct((FIRST + 1, CH, NZ), BF16),
+            jax.ShapeDtypeStruct((SENT - FIRST + 1, CH, NZ), BF16),
+            jax.ShapeDtypeStruct((KEPT + 1, CH, NZ), BF16),
         ],
         in_specs=[SMEM] * 4 + [VMEM] * (3 + len(parts)),
-        out_specs=[VMEM] * 4,
+        out_specs=[VMEM] * 3,
         scratch_shapes=[
             pltpu.VMEM((RB, CH, NZ), BF16),
-            pltpu.VMEM((SLOTS, CH, NZ), F32),
+            pltpu.VMEM((SLOTS + 1, CH, NZ), F32),
             pltpu.SMEM((LINES,), jnp.int32),
         ],
         compiler_params=params(),
@@ -345,7 +335,7 @@
     return total.astype(BF16)
 
 
-def scatter_gradient(soon, later, mine, own, chains, beside):
+def scatter_gradient(soon, later, kept, chains, beside):
     came_soon = over_row(soon, CORE)
     came_later = over_row(later, CORE)
     turns = {2: 0, 0: 1, 3: 2, 1: 3}
@@ -355,26 +345,30 @@
         size = len(sides) * OWN
         came = came_soon if start < FIRST else came_later
         first = start if start < FIRST else start - FIRST
-        return add(mine[start : start + size], came[first : first + size], *more)
+        return add(kept[start : start + size], came[first : first + size], *more)
 
     ring = {}
+    sent = []
     last = None
     long, short = chains
     for steps, sides in ((4, long), (3, short), (3, long), (2, short), (2, long), (1, short), (1, long)):
         more = [after(ring[sides], last)] if sides in ring else []
         last = chip(steps, sides, *more)
+        sent.append(last)
         ring[sides] = over_row(last, RING)
-    pieces = {}
-    for sides in chains:
-        for i, side in enumerate(sides):
-            turn = turns[side]
-            pieces[side] = (ring[sides][i * OWN : (i + 1) * OWN], own[turn * OWN : (turn + 1) * OWN])
-    give = [add(*pieces[2]), add(*pieces[3])]
-    got = [over_row(v, X_LO) for v in give]
-    result = beside(give)
-    got = after(got, result)
-    other = over_row(add(*pieces[1], got[1]), CORE)
-    return [*pieces[0], got[0], other], result
+
+    def terms(sides, side, *order):
+        at = sides.index(side) * OWN
+        own = SENT + turns[side] * OWN
+        brought = after(ring[sides], order) if order else ring[sides]
+        return brought[at : at + OWN], kept[own : own + OWN]
+
+    give = add(*terms(short, 3, last))
+    other = add(*terms(short, 1, give), over_row(give, X_LO))
+    result = beside(sent[2], last)
+    give = add(*terms(long, 2, give, result))
+    got = over_row(give, X_LO)
+    return [*terms(long, 0, give), got, over_row(other, CORE)], result
 
 
 def body(x_state, langevin_noise, observed, data_weight, sens_tiles, tile_rows, tile_cols, counts):
@@ -396,9 +390,8 @@
     parts = [part] + [
         over_col(part, [(i, (i + by) % N_COL) for i in range(N_COL)]) for by in (2, 4, 6)
     ]
-    far = over_col(after(to_far, part), ACROSS)
-    parts[0] = after(part, (near, far))
-    soon, later, mine, kept = adjoint(
+    parts[0] = after(part, near)
+    soon, later, kept = adjoint(
         place,
         rows,
         cols,
@@ -408,10 +401,11 @@
         data_weight.reshape(RB, NZ),
         parts,
     )
-    def beside(give):
-        return prox_step(start, wide, after(near, give), far, state, noise)
-
-    terms, base = scatter_gradient(soon, later, mine, kept, CHAINS, beside)
+    def beside(early, last):
+        far = over_col(after(to_far, early), ACROSS)
+        return prox_step(start, wide, after(near, last), far, state, noise)
+
+    terms, base = scatter_gradient(soon, later, kept, CHAINS, beside)
     gradient = sum(v.astype(F32) for v in terms)
     out = base - step_size * gradient.reshape(OWN_Y, OWN_X, CH, NZ)
     return out.transpose(0, 1, 3, 2)

time: 112 us -> 108 us (0.964)
  waiting for transfers between devices: 30.1 us -> 25.5 us
  local copies, waits for them, and re-layouts: 0.03 us -> 1.33 us
    ppermute x6, waiting for transfers between devices: 10.3 us -> 7.46 us  [over_col(): return lax.ppermute(value, 'col', pairs)]
    ppermute x26, waiting for transfers between devices: 19.7 us -> 18 us  [over_row(): return lax.ppermute(value, 'row', pairs)]
    unnamed x14, local copies, waits for them, and re-layouts: 0.03 us -> 1.33 us
  transfers between devices with their start and end apart: 32 -> 32, of which waited for: 17 -> 15; matrix products, arithmetic and copies ran while one was open for 1% -> 1% of each run, Pallas kernels for 3% -> 4%
where the time goes in v3:
time: 108 us; the launch traced here: 107 us
  starting transfers between devices  59.7 us (55%)
  waiting for transfers between devices  25.5 us (24%)
  blocking collectives  9.59 us (9%)
  Pallas kernels  6.93 us (6%)
  other arithmetic  2.84 us (3%)
  local copies, waits for them, and re-layouts  1.33 us (1%)
    ppermute x26, starting transfers between devices, over_row(): return lax.ppermute(value, 'row', pairs)  49.5 us
    ppermute x26, waiting for transfers between devices, over_row(): return lax.ppermute(value, 'row', pairs)  18 us
    ppermute x6, starting transfers between devices, over_col(): return lax.ppermute(value, 'col', pairs)  10.1 us
    all_gather x1, blocking collectives, gather_slab(): lax.all_gather(own, 'row', axis=0, tiled=True, axis_index_groups=QUADS)  9.59 us
    ppermute x6, waiting for transfers between devices, over_col(): return lax.ppermute(value, 'col', pairs)  7.46 us
    pallas_call x1, Pallas kernels, prox_step(): pl.pallas_call(prox_kernel, out_shape=jax.ShapeDtypeStruct((OWN_Y, OWN_X,...  3.88 us
  transfers between devices with their start and end apart: 32, of which 15 were waited for; matrix products, arithmetic and copies ran while one was open for 1% of the time, Pallas kernels for 4%

profile of v3, /device:TPU:1, one launch (start us, length us, event | category | flops | bytes accessed | tf_op | source)
XLA Modules:
  0.0 106.7 jit_solution(6127383178210212603)
XLA Ops:
  0.1 1.1 %convert_element_type.135 = bf16[2,8,32,128]{3,2,1,0:T(8,128)(2,1)S(1)} convert(f32[2,8,32,128]{3,2,1,0:T(8,128)} %bitcast.21) | non-fusion elementwise | flops 65536 | bytes 393216 | tf_op jit(solution)/shard_map/convert_element_type | solution.py:381
  1.2 9.6 %all_gather.3.plane = bf16[64,32,128]{2,1,0:T(8,128)(2,1)S(1)} all-gather(bf16[16,32,128]{2,1,0:T(8,128)(2,1)S(1)} %bitcast.31), channel_id=1, replica_groups={{0,8,16,24},{32,40,48,56},{64,72,80,88},{96,104,112,120},{128,136,144,1..., dimensions={0}, use_global_device_ids=true | all-gather | bytes 655360 | tf_op jit(solution)/shard_map/all_gather | solution.py:320
  10.8 4.6 %collective-permute-start = (bf16[32,32,128]{2,1,0:T(8,128)(2,1)S(1)}, bf16[32,32,128]{2,1,0:T(8,128)(2,1)S(1)}, u32[]{:S(2)}, u32[]{:S(2)}) collective-permute-start(bf16[32,32,128]{2,1,0:T(8,128)(2,1)S(1)} %get-tuple-element.50), channel_id=1, source_target_pairs={{0,32},{8,232},{16,48},{24,248},{32,64},{40,8},{48,80},{56,24},{64... | collective-permute-start | bytes 786440 | tf_op jit(solution)/shard_map/ppermute | solution.py:62
  15.4 0.7 collective-permute-start.4
  16.1 2.6 %collective-permute-done.rest_0_ = bf16[32,32,128]{2,1,0:T(8,128)(2,1)S(1)} collective-permute-done((bf16[32,32,128]{2,1,0:T(8,128)(2,1)S(1)}, bf16[32,32,128]{2,1,0:T(8,128)(2,1)S(1)}, u32[]{:S(2)}, u32[]{:S(2)}) %collective-permute-start) | collective-permute-done | bytes 262176 | tf_op jit(solution)/shard_map/ppermute | solution.py:62
  18.7 3.1 %collective-permute-start.1 = (bf16[32,32,128]{2,1,0:T(8,128)(2,1)S(1)}, bf16[32,32,128]{2,1,0:T(8,128)(2,1)S(1)}, u32[]{:S(2)}, u32[]{:S(2)}) collective-permute-start(bf16[32,32,128]{2,1,0:T(8,128)(2,1)S(1)} %collective-permute-done.rest_0_), channel_id=1, source_target_pairs={{0,32},{8,232},{16,48},{24,248},{32,64},{40,8},{48,80},{56,24},{64... | collective-permute-start | bytes 786440 | tf_op jit(solution)/shard_map/ppermute | solution.py:62
  21.8 2.8 %collective-permute-start.5 = (bf16[32,32,128]{2,1,0:T(8,128)(2,1)S(1)}, bf16[32,32,128]{2,1,0:T(8,128)(2,1)S(1)}, u32[]{:S(2)}, u32[]{:S(2)}) collective-permute-start(bf16[32,32,128]{2,1,0:T(8,128)(2,1)S(1)} %collective-permute-done.4.rest_4_), channel_id=1, source_target_pairs={{0,32},{8,232},{16,48},{24,248},{32,64},{40,8},{48,80},{56,24},{64... | collective-permute-start | bytes 786440 | tf_op jit(solution)/shard_map/ppermute | solution.py:62
  24.6 0.5 collective-permute-done.1.rest_1_
  25.1 3.1 %collective-permute-start.2 = (bf16[32,32,128]{2,1,0:T(8,128)(2,1)S(1)}, bf16[32,32,128]{2,1,0:T(8,128)(2,1)S(1)}, u32[]{:S(2)}, u32[]{:S(2)}) collective-permute-start(bf16[32,32,128]{2,1,0:T(8,128)(2,1)S(1)} %collective-permute-done.1.rest_1_), channel_id=1, source_target_pairs={{0,32},{8,232},{16,48},{24,248},{32,64},{40,8},{48,80},{56,24},{64... | collective-permute-start | bytes 786440 | tf_op jit(solution)/shard_map/ppermute | solution.py:62
  28.2 0.5 collective-permute-start.7
  28.7 2.3 %collective-permute-start.6 = (bf16[32,32,128]{2,1,0:T(8,128)(2,1)S(1)}, bf16[32,32,128]{2,1,0:T(8,128)(2,1)S(1)}, u32[]{:S(2)}, u32[]{:S(2)}) collective-permute-start(bf16[32,32,128]{2,1,0:T(8,128)(2,1)S(1)} %collective-permute-done.5.rest_5_), channel_id=1, source_target_pairs={{0,32},{8,232},{16,48},{24,248},{32,64},{40,8},{48,80},{56,24},{64... | collective-permute-start | bytes 786440 | tf_op jit(solution)/shard_map/ppermute | solution.py:62
  31.0 0.5 collective-permute-done.2.rest_2_
  31.6 3.1 %collective-permute-start.3 = (bf16[32,32,128]{2,1,0:T(8,128)(2,1)S(1)}, bf16[32,32,128]{2,1,0:T(8,128)(2,1)S(1)}, u32[]{:S(2)}, u32[]{:S(2)}) collective-permute-start(bf16[32,32,128]{2,1,0:T(8,128)(2,1)S(1)} %collective-permute-done.2.rest_2_), channel_id=1, source_target_pairs={{0,32},{8,232},{16,48},{24,248},{32,64},{40,8},{48,80},{56,24},{64... | collective-permute-start | bytes 786440 | tf_op jit(solution)/shard_map/ppermute | solution.py:62
  34.7 0.7 collective-permute-start.12
  35.9 2.3 %collective-permute-start.13 = (bf16[32,32,128]{2,1,0:T(8,128)(2,1)S(1)}, bf16[32,32,128]{2,1,0:T(8,128)(2,1)S(1)}, u32[]{:S(2)}, u32[]{:S(2)}) collective-permute-start(bf16[32,32,128]{2,1,0:T(8,128)(2,1)S(1)} %collective-permute-done.6.rest_6_), channel_id=1, source_target_pairs={{0,8},{8,0},{16,24},{24,16},{32,40},{40,32},{48,56},{56,48},{64,72... | collective-permute-start | bytes 786440 | tf_op jit(solution)/shard_map/ppermute | solution.py:62
  38.1 4.8 %collective-permute-start.10 = (bf16[32,32,128]{2,1,0:T(8,128)(2,1)S(1)}, bf16[32,32,128]{2,1,0:T(8,128)(2,1)S(1)}, u32[]{:S(2)}, u32[]{:S(2)}) collective-permute-start(bf16[32,32,128]{2,1,0:T(8,128)(2,1)S(1)} %collective-permute-done.3.rest_3_), channel_id=1, source_target_pairs={{0,8},{8,0},{16,24},{24,16},{32,40},{40,32},{48,56},{56,48},{64,72... | collective-permute-start | bytes 786440 | tf_op jit(solution)/shard_map/ppermute | solution.py:62
  44.1 0.7 copy-done.5
  44.7 0.7 copy-done.6
  45.4 1.4 %forward_tiles.1 = (bf16[8,32,128]{2,1,0:T(8,128)(2,1)S(1)}, bf16[8,8,32,128]{3,2,1,0:T(8,128)(2,1)S(1)}, bf16[8,3,32,128]{3,2,1,0:T(8,128)(2,1)S(1)}, bf16[8,3,32,128]{3,2,1,0:T(8,128)(2,1)S(1)}) custom-call(s32[3]{0:T(128)S(1)} %get-tuple-element.52.place, s32[48]{0:T(128)S(1)} %bitcast.26, s32[48]{0:T(128)S(1)} %bitcast.28, s32[1]{0:T(128)} %bitcast.17.count, ...), custom_call_target="tpu_custom_call" | custom-call | flops 50331648 | bytes 12582912 | tf_op jit(solution)/shard_map/forward_tiles/pallas_call | solution.py:120
  46.8 2.5 %collective-permute-start.15 = (bf16[8,32,128]{2,1,0:T(8,128)(2,1)S(1)}, bf16[8,32,128]{2,1,0:T(8,128)(2,1)S(1)}, u32[]{:S(2)}, u32[]{:S(2)}) collective-permute-start(bf16[8,32,128]{2,1,0:T(8,128)(2,1)S(1)} %get-tuple-element.28), channel_id=1, source_target_pairs={{0,1},{1,0},{2,3},{3,2},{4,5},{5,4},{6,7},{7,6},{8,9},{9,8},{10,11... | collective-permute-start | bytes 196616 | tf_op jit(solution)/shard_map/ppermute | solution.py:66
  49.3 0.5 collective-permute-start.14
  49.8 1.6 %collective-permute-done.15 = bf16[8,32,128]{2,1,0:T(8,128)(2,1)S(1)} collective-permute-done((bf16[8,32,128]{2,1,0:T(8,128)(2,1)S(1)}, bf16[8,32,128]{2,1,0:T(8,128)(2,1)S(1)}, u32[]{:S(2)}, u32[]{:S(2)}) %collective-permute-start.15) | collective-permute-done | bytes 65568 | tf_op jit(solution)/shard_map/ppermute | solution.py:66
  51.5 3.3 %collective-permute-start.18 = (bf16[8,32,128]{2,1,0:T(8,128)(2,1)S(1)}, bf16[8,32,128]{2,1,0:T(8,128)(2,1)S(1)}, u32[]{:S(2)}, u32[]{:S(2)}) collective-permute-start(bf16[8,32,128]{2,1,0:T(8,128)(2,1)S(1)} %add_convert_fusion.10.rest_0_), channel_id=1, source_target_pairs={{0,6},{1,7},{2,0},{3,1},{4,2},{5,3},{6,4},{7,5},{8,14},{9,15},{10,... | collective-permute-start | bytes 196616 | tf_op jit(solution)/shard_map/ppermute | solution.py:66
  55.3 0.6 collective-permute-start.16
  55.9 0.7 collective-permute-done.14.near
  56.6 2.9 %collective-permute-done.17.rest_2_ = bf16[8,32,128]{2,1,0:T(8,128)(2,1)S(1)} collective-permute-done((bf16[8,32,128]{2,1,0:T(8,128)(2,1)S(1)}, bf16[8,32,128]{2,1,0:T(8,128)(2,1)S(1)}, u32[]{:S(2)}, u32[]{:S(2)}) %collective-permute-start.17) | collective-permute-done | bytes 65568 | tf_op jit(solution)/shard_map/ppermute | solution.py:66
  59.5 0.6 collective-permute-done.16.rest_1_
  60.2 1.7 %adjoint_tiles.1 = (bf16[97,32,128]{2,1,0:T(8,128)(2,1)S(1)}, bf16[129,32,128]{2,1,0:T(8,128)(2,1)S(1)}, bf16[289,32,128]{2,1,0:T(8,128)(2,1)S(1)}) custom-call(s32[3]{0:T(128)S(1)} %get-tuple-element.52.place, s32[48]{0:T(128)S(1)} %bitcast.27, s32[48]{0:T(128)S(1)} %bitcast.29, s32[1]{0:T(128)} %bitcast.18.count, bf16[48,128,128]{2,1,0:T(8,128)(2,1)S(1)} %bitcast.20, ...), custom_call_target="tpu_custom_call" | custom-call | flops 50331648 | bytes 12582912 | tf_op jit(solution)/shard_map/adjoint_tiles/pallas_call | solution.py:212
  61.8 3.0 %collective-permute-start.20 = (bf16[97,32,128]{2,1,0:T(8,128)(2,1)S(1)}, bf16[97,32,128]{2,1,0:T(8,128)(2,1)S(1)}, u32[]{:S(2)}, u32[]{:S(2)}) collective-permute-start(bf16[97,32,128]{2,1,0:T(8,128)(2,1)S(1)} %get-tuple-element.32), channel_id=1, source_target_pairs={{0,8},{8,0},{16,24},{24,16},{32,40},{40,32},{48,56},{56,48},{64,72... | collective-permute-start | bytes 2383880 | tf_op jit(solution)/shard_map/ppermute | solution.py:62
  65.0 1.8 %collective-permute-done.20 = bf16[97,32,128]{2,1,0:T(8,128)(2,1)S(1)} collective-permute-done((bf16[97,32,128]{2,1,0:T(8,128)(2,1)S(1)}, bf16[97,32,128]{2,1,0:T(8,128)(2,1)S(1)}, u32[]{:S(2)}, u32[]{:S(2)}) %collective-permute-start.20) | collective-permute-done | bytes 794656 | tf_op jit(solution)/shard_map/ppermute | solution.py:62
  67.0 1.0 collective-permute-start.23
  68.0 4.5 %collective-permute-done.21 = bf16[32,32,128]{2,1,0:T(8,128)(2,1)S(1)} collective-permute-done((bf16[32,32,128]{2,1,0:T(8,128)(2,1)S(1)}, bf16[32,32,128]{2,1,0:T(8,128)(2,1)S(1)}, u32[]{:S(2)}, u32[]{:S(2)}) %collective-permute-start.21) | collective-permute-done | bytes 262176 | tf_op jit(solution)/shard_map/ppermute | solution.py:62
  72.7 1.0 collective-permute-start.22
  73.7 1.7 %collective-permute-done.23 = bf16[32,32,128]{2,1,0:T(8,128)(2,1)S(1)} collective-permute-done((bf16[32,32,128]{2,1,0:T(8,128)(2,1)S(1)}, bf16[32,32,128]{2,1,0:T(8,128)(2,1)S(1)}, u32[]{:S(2)}, u32[]{:S(2)}) %collective-permute-start.23) | collective-permute-done | bytes 262176 | tf_op jit(solution)/shard_map/ppermute | solution.py:62
  75.5 1.0 collective-permute-start.25
  76.5 1.5 %collective-permute-done.22 = bf16[32,32,128]{2,1,0:T(8,128)(2,1)S(1)} collective-permute-done((bf16[32,32,128]{2,1,0:T(8,128)(2,1)S(1)}, bf16[32,32,128]{2,1,0:T(8,128)(2,1)S(1)}, u32[]{:S(2)}, u32[]{:S(2)}) %collective-permute-start.22) | collective-permute-done | bytes 262176 | tf_op jit(solution)/shard_map/ppermute | solution.py:62
  78.1 2.2 %collective-permute-start.24 = (bf16[32,32,128]{2,1,0:T(8,128)(2,1)S(1)}, bf16[32,32,128]{2,1,0:T(8,128)(2,1)S(1)}, u32[]{:S(2)}, u32[]{:S(2)}) collective-permute-start(bf16[32,32,128]{2,1,0:T(8,128)(2,1)S(1)} %add_convert_fusion.2), channel_id=1, source_target_pairs={{0,32},{8,232},{16,48},{24,248},{32,64},{40,8},{48,80},{56,24},{64... | collective-permute-start | bytes 786440 | tf_op jit(solution)/shard_map/ppermute | solution.py:62
  80.3 0.8 collective-permute-done.25
  81.2 1.9 %collective-permute-start.28 = (bf16[32,32,128]{2,1,0:T(8,128)(2,1)S(1)}, bf16[32,32,128]{2,1,0:T(8,128)(2,1)S(1)}, u32[]{:S(2)}, u32[]{:S(2)}) collective-permute-start(bf16[32,32,128]{2,1,0:T(8,128)(2,1)S(1)} %add_convert_fusion.1), channel_id=1, source_target_pairs={{0,32},{8,232},{16,48},{24,248},{32,64},{40,8},{48,80},{56,24},{64... | collective-permute-start | bytes 786440 | tf_op jit(solution)/shard_map/ppermute | solution.py:62
  83.1 2.7 %collective-permute-start.26 = (bf16[8,3,32,128]{3,2,1,0:T(8,128)(2,1)S(1)}, bf16[8,3,32,128]{3,2,1,0:T(8,128)(2,1)S(1)}, u32[]{:S(2)}, u32[]{:S(2)}) collective-permute-start(bf16[8,3,32,128]{3,2,1,0:T(8,128)(2,1)S(1)} %get-tuple-element.40), channel_id=1, source_target_pairs={{0,7},{1,2},{2,1},{3,4},{4,3},{5,6},{6,5},{7,0},{8,15},{9,10},{10,... | collective-permute-start | bytes 589832 | tf_op jit(solution)/shard_map/ppermute | solution.py:66
  85.9 2.7 %collective-permute-start.27 = (bf16[32,32,128]{2,1,0:T(8,128)(2,1)S(1)}, bf16[32,32,128]{2,1,0:T(8,128)(2,1)S(1)}, u32[]{:S(2)}, u32[]{:S(2)}) collective-permute-start(bf16[32,32,128]{2,1,0:T(8,128)(2,1)S(1)} %add_convert_fusion), channel_id=1, source_target_pairs={{0,32},{8,232},{16,48},{24,248},{32,64},{40,8},{48,80},{56,24},{64... | collective-permute-start | bytes 786440 | tf_op jit(solution)/shard_map/ppermute | solution.py:62
  88.7 1.0 collective-permute-start.30
  89.7 1.5 %collective-permute-done.26.far = bf16[8,3,32,128]{3,2,1,0:T(8,128)(2,1)S(1)} collective-permute-done((bf16[8,3,32,128]{3,2,1,0:T(8,128)(2,1)S(1)}, bf16[8,3,32,128]{3,2,1,0:T(8,128)(2,1)S(1)}, u32[]{:S(2)}, u32[]{:S(2)}) %collective-permute-start.26) | collective-permute-done | bytes 196640 | tf_op jit(solution)/shard_map/ppermute | solution.py:66
  91.2 3.9 %tv_prox.1 = f32[2,8,32,128]{3,2,1,0:T(8,128)S(1)} custom-call(s32[3]{0:T(128)S(1)} %get-tuple-element.51.start, bf16[8,8,32,128]{3,2,1,0:T(8,128)(2,1)S(1)} %get-tuple-element.26.wide, bf16[8,3,32,128]{3,2,1,0:T(8,128)(2,1)S(1)} %collective-permute-done.14.near, bf16[8,3,32,128]{3,2,1,0:T(8,128)(2,1)S(1)} %collective-permute-done.26.far, ...), custom_call_target="tpu_custom_call" | custom-call | flops 16777216 | bytes 12582912 | tf_op jit(solution)/shard_map/tv_prox/pallas_call | solution.py:302
  95.3 5.4 %collective-permute-start.31 = (bf16[16,32,128]{2,1,0:T(8,128)(2,1)S(1)}, bf16[16,32,128]{2,1,0:T(8,128)(2,1)S(1)}, u32[]{:S(2)}, u32[]{:S(2)}) collective-permute-start(bf16[16,32,128]{2,1,0:T(8,128)(2,1)S(1)} %get-tuple-element.48), channel_id=1, source_target_pairs={{0,8},{8,0},{16,24},{24,16},{32,40},{40,32},{48,56},{56,48},{64,72... | collective-permute-start | bytes 393224 | tf_op jit(solution)/shard_map/ppermute | solution.py:62
  100.7 1.6 %collective-permute-start.29 = (bf16[16,32,128]{2,1,0:T(8,128)(2,1)S(1)}, bf16[16,32,128]{2,1,0:T(8,128)(2,1)S(1)}, u32[]{:S(2)}, u32[]{:S(2)}) collective-permute-start(bf16[16,32,128]{2,1,0:T(8,128)(2,1)S(1)} %get-tuple-element.47), channel_id=1, source_target_pairs={{0,16},{8,24},{16,0},{24,8},{32,48},{40,56},{48,32},{56,40},{64,80... | collective-permute-start | bytes 393224 | tf_op jit(solution)/shard_map/ppermute | solution.py:62
  102.2 3.6 %collective-permute-done.29 = bf16[16,32,128]{2,1,0:T(8,128)(2,1)S(1)} collective-permute-done((bf16[16,32,128]{2,1,0:T(8,128)(2,1)S(1)}, bf16[16,32,128]{2,1,0:T(8,128)(2,1)S(1)}, u32[]{:S(2)}, u32[]{:S(2)}) %collective-permute-start.29) | collective-permute-done | bytes 131104 | tf_op jit(solution)/shard_map/ppermute | solution.py:62
  105.9 0.7 subtract_bitcast_fusion
  (48 shorter events, 2.7 us)
Async XLA Ops:
  0.0 44.1 %copy-start = (bf16[1,1,48,128,128]{4,3,2,1,0:T(8,128)(2,1)S(1)}, bf16[1,1,48,128,128]{4,3,2,1,0:T(8,128)(2,1)}, u32[]{:S(2)}) copy-start(bf16[1,1,48,128,128]{4,3,2,1,0:T(8,128)(2,1)} %param.12) | copy-start | bytes 4718596
  10.8 7.9 %collective-permute-start = (bf16[32,32,128]{2,1,0:T(8,128)(2,1)S(1)}, bf16[32,32,128]{2,1,0:T(8,128)(2,1)S(1)}, u32[]{:S(2)}, u32[]{:S(2)}) collective-permute-start(bf16[32,32,128]{2,1,0:T(8,128)(2,1)S(1)} %get-tuple-element.50), channel_id=1, source_target_pairs={{0,32},{8,232},{16,48},{24,248},{32,64},{40,8},{48,80},{56,24},{64... | collective-permute-start | bytes 786440 | tf_op jit(solution)/shard_map/ppermute | solution.py:62
  15.4 6.4 %collective-permute-start.4 = (bf16[32,32,128]{2,1,0:T(8,128)(2,1)S(1)}, bf16[32,32,128]{2,1,0:T(8,128)(2,1)S(1)}, u32[]{:S(2)}, u32[]{:S(2)}) collective-permute-start(bf16[32,32,128]{2,1,0:T(8,128)(2,1)S(1)} %get-tuple-element.49), channel_id=1, source_target_pairs={{0,32},{8,232},{16,48},{24,248},{32,64},{40,8},{48,80},{56,24},{64... | collective-permute-start | bytes 786440 | tf_op jit(solution)/shard_map/ppermute | solution.py:62
  18.7 6.4 %collective-permute-start.1 = (bf16[32,32,128]{2,1,0:T(8,128)(2,1)S(1)}, bf16[32,32,128]{2,1,0:T(8,128)(2,1)S(1)}, u32[]{:S(2)}, u32[]{:S(2)}) collective-permute-start(bf16[32,32,128]{2,1,0:T(8,128)(2,1)S(1)} %collective-permute-done.rest_0_), channel_id=1, source_target_pairs={{0,32},{8,232},{16,48},{24,248},{32,64},{40,8},{48,80},{56,24},{64... | collective-permute-start | bytes 786440 | tf_op jit(solution)/shard_map/ppermute | solution.py:62
  21.8 6.9 %collective-permute-start.5 = (bf16[32,32,128]{2,1,0:T(8,128)(2,1)S(1)}, bf16[32,32,128]{2,1,0:T(8,128)(2,1)S(1)}, u32[]{:S(2)}, u32[]{:S(2)}) collective-permute-start(bf16[32,32,128]{2,1,0:T(8,128)(2,1)S(1)} %collective-permute-done.4.rest_4_), channel_id=1, source_target_pairs={{0,32},{8,232},{16,48},{24,248},{32,64},{40,8},{48,80},{56,24},{64... | collective-permute-start | bytes 786440 | tf_op jit(solution)/shard_map/ppermute | solution.py:62
  25.1 6.4 %collective-permute-start.2 = (bf16[32,32,128]{2,1,0:T(8,128)(2,1)S(1)}, bf16[32,32,128]{2,1,0:T(8,128)(2,1)S(1)}, u32[]{:S(2)}, u32[]{:S(2)}) collective-permute-start(bf16[32,32,128]{2,1,0:T(8,128)(2,1)S(1)} %collective-permute-done.1.rest_1_), channel_id=1, source_target_pairs={{0,32},{8,232},{16,48},{24,248},{32,64},{40,8},{48,80},{56,24},{64... | collective-permute-start | bytes 786440 | tf_op jit(solution)/shard_map/ppermute | solution.py:62
  28.2 7.1 %collective-permute-start.11 = (bf16[32,32,128]{2,1,0:T(8,128)(2,1)S(1)}, bf16[32,32,128]{2,1,0:T(8,128)(2,1)S(1)}, u32[]{:S(2)}, u32[]{:S(2)}) collective-permute-start(bf16[32,32,128]{2,1,0:T(8,128)(2,1)S(1)} %collective-permute-done.4.rest_4_), channel_id=1, source_target_pairs={{0,8},{8,0},{16,24},{24,16},{32,40},{40,32},{48,56},{56,48},{64,72... | collective-permute-start | bytes 786440 | tf_op jit(solution)/shard_map/ppermute | solution.py:62
  28.2 7.2 %collective-permute-start.7 = (bf16[32,32,128]{2,1,0:T(8,128)(2,1)S(1)}, bf16[32,32,128]{2,1,0:T(8,128)(2,1)S(1)}, u32[]{:S(2)}, u32[]{:S(2)}) collective-permute-start(bf16[32,32,128]{2,1,0:T(8,128)(2,1)S(1)} %collective-permute-done.rest_0_), channel_id=1, source_target_pairs={{0,8},{8,0},{16,24},{24,16},{32,40},{40,32},{48,56},{56,48},{64,72... | collective-permute-start | bytes 786440 | tf_op jit(solution)/shard_map/ppermute | solution.py:62
  28.7 7.1 %collective-permute-start.6 = (bf16[32,32,128]{2,1,0:T(8,128)(2,1)S(1)}, bf16[32,32,128]{2,1,0:T(8,128)(2,1)S(1)}, u32[]{:S(2)}, u32[]{:S(2)}) collective-permute-start(bf16[32,32,128]{2,1,0:T(8,128)(2,1)S(1)} %collective-permute-done.5.rest_5_), channel_id=1, source_target_pairs={{0,32},{8,232},{16,48},{24,248},{32,64},{40,8},{48,80},{56,24},{64... | collective-permute-start | bytes 786440 | tf_op jit(solution)/shard_map/ppermute | solution.py:62
  31.6 6.6 %collective-permute-start.3 = (bf16[32,32,128]{2,1,0:T(8,128)(2,1)S(1)}, bf16[32,32,128]{2,1,0:T(8,128)(2,1)S(1)}, u32[]{:S(2)}, u32[]{:S(2)}) collective-permute-start(bf16[32,32,128]{2,1,0:T(8,128)(2,1)S(1)} %collective-permute-done.2.rest_2_), channel_id=1, source_target_pairs={{0,32},{8,232},{16,48},{24,248},{32,64},{40,8},{48,80},{56,24},{64... | collective-permute-start | bytes 786440 | tf_op jit(solution)/shard_map/ppermute | solution.py:62
  34.7 8.9 %collective-permute-start.12 = (bf16[32,32,128]{2,1,0:T(8,128)(2,1)S(1)}, bf16[32,32,128]{2,1,0:T(8,128)(2,1)S(1)}, u32[]{:S(2)}, u32[]{:S(2)}) collective-permute-start(bf16[32,32,128]{2,1,0:T(8,128)(2,1)S(1)} %collective-permute-done.5.rest_5_), channel_id=1, source_target_pairs={{0,8},{8,0},{16,24},{24,16},{32,40},{40,32},{48,56},{56,48},{64,72... | collective-permute-start | bytes 786440 | tf_op jit(solution)/shard_map/ppermute | solution.py:62
  35.3 8.2 %collective-permute-start.8 = (bf16[32,32,128]{2,1,0:T(8,128)(2,1)S(1)}, bf16[32,32,128]{2,1,0:T(8,128)(2,1)S(1)}, u32[]{:S(2)}, u32[]{:S(2)}) collective-permute-start(bf16[32,32,128]{2,1,0:T(8,128)(2,1)S(1)} %collective-permute-done.1.rest_1_), channel_id=1, source_target_pairs={{0,8},{8,0},{16,24},{24,16},{32,40},{40,32},{48,56},{56,48},{64,72... | collective-permute-start | bytes 786440 | tf_op jit(solution)/shard_map/ppermute | solution.py:62
  35.4 8.2 %collective-permute-start.9 = (bf16[32,32,128]{2,1,0:T(8,128)(2,1)S(1)}, bf16[32,32,128]{2,1,0:T(8,128)(2,1)S(1)}, u32[]{:S(2)}, u32[]{:S(2)}) collective-permute-start(bf16[32,32,128]{2,1,0:T(8,128)(2,1)S(1)} %collective-permute-done.2.rest_2_), channel_id=1, source_target_pairs={{0,8},{8,0},{16,24},{24,16},{32,40},{40,32},{48,56},{56,48},{64,72... | collective-permute-start | bytes 786440 | tf_op jit(solution)/shard_map/ppermute | solution.py:62
  35.9 7.7 %collective-permute-start.13 = (bf16[32,32,128]{2,1,0:T(8,128)(2,1)S(1)}, bf16[32,32,128]{2,1,0:T(8,128)(2,1)S(1)}, u32[]{:S(2)}, u32[]{:S(2)}) collective-permute-start(bf16[32,32,128]{2,1,0:T(8,128)(2,1)S(1)} %collective-permute-done.6.rest_6_), channel_id=1, source_target_pairs={{0,8},{8,0},{16,24},{24,16},{32,40},{40,32},{48,56},{56,48},{64,72... | collective-permute-start | bytes 786440 | tf_op jit(solution)/shard_map/ppermute | solution.py:62
  38.1 5.9 %collective-permute-start.10 = (bf16[32,32,128]{2,1,0:T(8,128)(2,1)S(1)}, bf16[32,32,128]{2,1,0:T(8,128)(2,1)S(1)}, u32[]{:S(2)}, u32[]{:S(2)}) collective-permute-start(bf16[32,32,128]{2,1,0:T(8,128)(2,1)S(1)} %collective-permute-done.3.rest_3_), channel_id=1, source_target_pairs={{0,8},{8,0},{16,24},{24,16},{32,40},{40,32},{48,56},{56,48},{64,72... | collective-permute-start | bytes 786440 | tf_op jit(solution)/shard_map/ppermute | solution.py:62
  44.1 0.7 copy-start.5
  44.7 0.7 copy-start.6
  45.4 14.8 %copy-start.3 = (f32[1024]{0:T(1024)S(1)}, f32[1024]{0:T(1024)}, u32[]{:S(2)}) copy-start(f32[1024]{0:T(1024)} %param.10) | copy-start | bytes 12292
  45.4 14.8 %copy-start.4 = (f32[1024]{0:T(1024)S(1)}, f32[1024]{0:T(1024)}, u32[]{:S(2)}) copy-start(f32[1024]{0:T(1024)} %param.11) | copy-start | bytes 12292
  46.8 4.7 %collective-permute-start.15 = (bf16[8,32,128]{2,1,0:T(8,128)(2,1)S(1)}, bf16[8,32,128]{2,1,0:T(8,128)(2,1)S(1)}, u32[]{:S(2)}, u32[]{:S(2)}) collective-permute-start(bf16[8,32,128]{2,1,0:T(8,128)(2,1)S(1)} %get-tuple-element.28), channel_id=1, source_target_pairs={{0,1},{1,0},{2,3},{3,2},{4,5},{5,4},{6,7},{7,6},{8,9},{9,8},{10,11... | collective-permute-start | bytes 196616 | tf_op jit(solution)/shard_map/ppermute | solution.py:66
  49.3 7.3 %collective-permute-start.14 = (bf16[8,3,32,128]{3,2,1,0:T(8,128)(2,1)S(1)}, bf16[8,3,32,128]{3,2,1,0:T(8,128)(2,1)S(1)}, u32[]{:S(2)}, u32[]{:S(2)}) collective-permute-start(bf16[8,3,32,128]{3,2,1,0:T(8,128)(2,1)S(1)} %get-tuple-element.27), channel_id=1, source_target_pairs={{0,1},{1,0},{2,3},{3,2},{4,5},{5,4},{6,7},{7,6},{8,9},{9,8},{10,11... | collective-permute-start | bytes 589832 | tf_op jit(solution)/shard_map/ppermute | solution.py:66
  51.5 5.1 %collective-permute-start.18 = (bf16[8,32,128]{2,1,0:T(8,128)(2,1)S(1)}, bf16[8,32,128]{2,1,0:T(8,128)(2,1)S(1)}, u32[]{:S(2)}, u32[]{:S(2)}) collective-permute-start(bf16[8,32,128]{2,1,0:T(8,128)(2,1)S(1)} %add_convert_fusion.10.rest_0_), channel_id=1, source_target_pairs={{0,6},{1,7},{2,0},{3,1},{4,2},{5,3},{6,4},{7,5},{8,14},{9,15},{10,... | collective-permute-start | bytes 196616 | tf_op jit(solution)/shard_map/ppermute | solution.py:66
  54.8 4.7 %collective-permute-start.17 = (bf16[8,32,128]{2,1,0:T(8,128)(2,1)S(1)}, bf16[8,32,128]{2,1,0:T(8,128)(2,1)S(1)}, u32[]{:S(2)}, u32[]{:S(2)}) collective-permute-start(bf16[8,32,128]{2,1,0:T(8,128)(2,1)S(1)} %add_convert_fusion.10.rest_0_), channel_id=1, source_target_pairs={{0,4},{1,5},{2,6},{3,7},{4,0},{5,1},{6,2},{7,3},{8,12},{9,13},{10,... | collective-permute-start | bytes 196616 | tf_op jit(solution)/shard_map/ppermute | solution.py:66
  55.3 4.9 %collective-permute-start.16 = (bf16[8,32,128]{2,1,0:T(8,128)(2,1)S(1)}, bf16[8,32,128]{2,1,0:T(8,128)(2,1)S(1)}, u32[]{:S(2)}, u32[]{:S(2)}) collective-permute-start(bf16[8,32,128]{2,1,0:T(8,128)(2,1)S(1)} %add_convert_fusion.10.rest_0_), channel_id=1, source_target_pairs={{0,2},{1,3},{2,4},{3,5},{4,6},{5,7},{6,0},{7,1},{8,10},{9,11},{10,... | collective-permute-start | bytes 196616 | tf_op jit(solution)/shard_map/ppermute | solution.py:66
  61.8 5.0 %collective-permute-start.20 = (bf16[97,32,128]{2,1,0:T(8,128)(2,1)S(1)}, bf16[97,32,128]{2,1,0:T(8,128)(2,1)S(1)}, u32[]{:S(2)}, u32[]{:S(2)}) collective-permute-start(bf16[97,32,128]{2,1,0:T(8,128)(2,1)S(1)} %get-tuple-element.32), channel_id=1, source_target_pairs={{0,8},{8,0},{16,24},{24,16},{32,40},{40,32},{48,56},{56,48},{64,72... | collective-permute-start | bytes 2383880 | tf_op jit(solution)/shard_map/ppermute | solution.py:62
  64.9 10.5 %collective-permute-start.19 = (bf16[129,32,128]{2,1,0:T(8,128)(2,1)S(1)}, bf16[129,32,128]{2,1,0:T(8,128)(2,1)S(1)}, u32[]{:S(2)}, u32[]{:S(2)}) collective-permute-start(bf16[129,32,128]{2,1,0:T(8,128)(2,1)S(1)} %get-tuple-element.31), channel_id=1, source_target_pairs={{0,8},{8,0},{16,24},{24,16},{32,40},{40,32},{48,56},{56,48},{64,72... | collective-permute-start | bytes 3170312 | tf_op jit(solution)/shard_map/ppermute | solution.py:62
  67.0 5.6 %collective-permute-start.21 = (bf16[32,32,128]{2,1,0:T(8,128)(2,1)S(1)}, bf16[32,32,128]{2,1,0:T(8,128)(2,1)S(1)}, u32[]{:S(2)}, u32[]{:S(2)}) collective-permute-start(bf16[32,32,128]{2,1,0:T(8,128)(2,1)S(1)} %get-tuple-element.46), channel_id=1, source_target_pairs={{0,32},{8,232},{16,48},{24,248},{32,64},{40,8},{48,80},{56,24},{64... | collective-permute-start | bytes 786440 | tf_op jit(solution)/shard_map/ppermute | solution.py:62
  67.0 8.3 %collective-permute-start.23 = (bf16[32,32,128]{2,1,0:T(8,128)(2,1)S(1)}, bf16[32,32,128]{2,1,0:T(8,128)(2,1)S(1)}, u32[]{:S(2)}, u32[]{:S(2)}) collective-permute-start(bf16[32,32,128]{2,1,0:T(8,128)(2,1)S(1)} %get-tuple-element.45), channel_id=1, source_target_pairs={{0,32},{8,232},{16,48},{24,248},{32,64},{40,8},{48,80},{56,24},{64... | collective-permute-start | bytes 786440 | tf_op jit(solution)/shard_map/ppermute | solution.py:62
  72.7 18.6 %copy-start.1 = (f32[2,8,128,32]{2,3,1,0:T(8,128)S(1)}, f32[2,8,128,32]{2,3,1,0:T(8,128)}, u32[]{:S(2)}) copy-start(f32[2,8,128,32]{2,3,1,0:T(8,128)} %param.8) | copy-start | bytes 786436
  72.7 18.6 %copy-start.2 = (f32[2,8,128,32]{2,3,1,0:T(8,128)S(1)}, f32[2,8,128,32]{2,3,1,0:T(8,128)}, u32[]{:S(2)}) copy-start(f32[2,8,128,32]{2,3,1,0:T(8,128)} %param.9) | copy-start | bytes 786436
  72.7 5.3 %collective-permute-start.22 = (bf16[32,32,128]{2,1,0:T(8,128)(2,1)S(1)}, bf16[32,32,128]{2,1,0:T(8,128)(2,1)S(1)}, u32[]{:S(2)}, u32[]{:S(2)}) collective-permute-start(bf16[32,32,128]{2,1,0:T(8,128)(2,1)S(1)} %add_convert_fusion.4), channel_id=1, source_target_pairs={{0,32},{8,232},{16,48},{24,248},{32,64},{40,8},{48,80},{56,24},{64... | collective-permute-start | bytes 786440 | tf_op jit(solution)/shard_map/ppermute | solution.py:62
  75.5 5.6 %collective-permute-start.25 = (bf16[32,32,128]{2,1,0:T(8,128)(2,1)S(1)}, bf16[32,32,128]{2,1,0:T(8,128)(2,1)S(1)}, u32[]{:S(2)}, u32[]{:S(2)}) collective-permute-start(bf16[32,32,128]{2,1,0:T(8,128)(2,1)S(1)} %add_convert_fusion.3), channel_id=1, source_target_pairs={{0,32},{8,232},{16,48},{24,248},{32,64},{40,8},{48,80},{56,24},{64... | collective-permute-start | bytes 786440 | tf_op jit(solution)/shard_map/ppermute | solution.py:62
  78.1 7.7 %collective-permute-start.24 = (bf16[32,32,128]{2,1,0:T(8,128)(2,1)S(1)}, bf16[32,32,128]{2,1,0:T(8,128)(2,1)S(1)}, u32[]{:S(2)}, u32[]{:S(2)}) collective-permute-start(bf16[32,32,128]{2,1,0:T(8,128)(2,1)S(1)} %add_convert_fusion.2), channel_id=1, source_target_pairs={{0,32},{8,232},{16,48},{24,248},{32,64},{40,8},{48,80},{56,24},{64... | collective-permute-start | bytes 786440 | tf_op jit(solution)/shard_map/ppermute | solution.py:62
  81.2 7.4 %collective-permute-start.28 = (bf16[32,32,128]{2,1,0:T(8,128)(2,1)S(1)}, bf16[32,32,128]{2,1,0:T(8,128)(2,1)S(1)}, u32[]{:S(2)}, u32[]{:S(2)}) collective-permute-start(bf16[32,32,128]{2,1,0:T(8,128)(2,1)S(1)} %add_convert_fusion.1), channel_id=1, source_target_pairs={{0,32},{8,232},{16,48},{24,248},{32,64},{40,8},{48,80},{56,24},{64... | collective-permute-start | bytes 786440 | tf_op jit(solution)/shard_map/ppermute | solution.py:62
  83.1 8.1 %collective-permute-start.26 = (bf16[8,3,32,128]{3,2,1,0:T(8,128)(2,1)S(1)}, bf16[8,3,32,128]{3,2,1,0:T(8,128)(2,1)S(1)}, u32[]{:S(2)}, u32[]{:S(2)}) collective-permute-start(bf16[8,3,32,128]{3,2,1,0:T(8,128)(2,1)S(1)} %get-tuple-element.40), channel_id=1, source_target_pairs={{0,7},{1,2},{2,1},{3,4},{4,3},{5,6},{6,5},{7,0},{8,15},{9,10},{10,... | collective-permute-start | bytes 589832 | tf_op jit(solution)/shard_map/ppermute | solution.py:66
  85.9 9.2 %collective-permute-start.27 = (bf16[32,32,128]{2,1,0:T(8,128)(2,1)S(1)}, bf16[32,32,128]{2,1,0:T(8,128)(2,1)S(1)}, u32[]{:S(2)}, u32[]{:S(2)}) collective-permute-start(bf16[32,32,128]{2,1,0:T(8,128)(2,1)S(1)} %add_convert_fusion), channel_id=1, source_target_pairs={{0,32},{8,232},{16,48},{24,248},{32,64},{40,8},{48,80},{56,24},{64... | collective-permute-start | bytes 786440 | tf_op jit(solution)/shard_map/ppermute | solution.py:62
  88.7 6.5 %collective-permute-start.30 = (bf16[16,32,128]{2,1,0:T(8,128)(2,1)S(1)}, bf16[16,32,128]{2,1,0:T(8,128)(2,1)S(1)}, u32[]{:S(2)}, u32[]{:S(2)}) collective-permute-start(bf16[16,32,128]{2,1,0:T(8,128)(2,1)S(1)} %add_convert_fusion.9), channel_id=1, source_target_pairs={{0,16},{8,24},{16,0},{24,8},{32,48},{40,56},{48,32},{56,40},{64,80... | collective-permute-start | bytes 393224 | tf_op jit(solution)/shard_map/ppermute | solution.py:62
  95.3 7.0 %collective-permute-start.31 = (bf16[16,32,128]{2,1,0:T(8,128)(2,1)S(1)}, bf16[16,32,128]{2,1,0:T(8,128)(2,1)S(1)}, u32[]{:S(2)}, u32[]{:S(2)}) collective-permute-start(bf16[16,32,128]{2,1,0:T(8,128)(2,1)S(1)} %get-tuple-element.48), channel_id=1, source_target_pairs={{0,8},{8,0},{16,24},{24,16},{32,40},{40,32},{48,56},{56,48},{64,72... | collective-permute-start | bytes 393224 | tf_op jit(solution)/shard_map/ppermute | solution.py:62
  100.7 5.2 %collective-permute-start.29 = (bf16[16,32,128]{2,1,0:T(8,128)(2,1)S(1)}, bf16[16,32,128]{2,1,0:T(8,128)(2,1)S(1)}, u32[]{:S(2)}, u32[]{:S(2)}) collective-permute-start(bf16[16,32,128]{2,1,0:T(8,128)(2,1)S(1)} %get-tuple-element.47), channel_id=1, source_target_pairs={{0,16},{8,24},{16,0},{24,8},{32,48},{40,56},{48,32},{56,40},{64,80... | collective-permute-start | bytes 393224 | tf_op jit(solution)/shard_map/ppermute | solution.py:62

commit v4 on v3

--- a/solution.py
+++ b/solution.py
@@ -53,6 +53,8 @@
 MINE = [(0, steps) for steps in range(1, 5)] + [(1, steps) for steps in range(1, 4)]
 PIECES = MINE + [(1 - flip, -steps) for flip, steps in MINE]
 
+EARLY = [(flip, steps) for flip, steps in PIECES if abs(steps) < 4]
+
 ANY = pl.BlockSpec(memory_space=pl.ANY)
 VMEM = pl.BlockSpec(memory_space=pltpu.VMEM)
 SMEM = pl.BlockSpec(memory_space=pltpu.SMEM)
@@ -75,13 +77,13 @@
 
 
 def forward_kernel(place, rows, cols, count, tiles, plane, *rest):
-    pieces, (out, wide, near, far, field, total, sems) = rest[: len(PIECES)], rest[len(PIECES) :]
+    pieces, (total, wide, near, far, late, field, sems) = rest[: len(EARLY)], rest[len(EARLY) :]
     z = place[0]
     quad = place[1]
     core = quad & 1
     up = 1 - 2 * core
-    copies = [pltpu.make_async_copy(plane, field.at[pl.ds(z * PLANE, PLANE)], sems.at[len(PIECES)])]
-    for i, ((flip, steps), piece) in enumerate(zip(PIECES, pieces)):
+    copies = [pltpu.make_async_copy(plane, field.at[pl.ds(z * PLANE, PLANE)], sems.at[len(EARLY)])]
+    for i, ((flip, steps), piece) in enumerate(zip(EARLY, pieces)):
         from_plane = lax.rem(z - steps * up + 2 * N_Z, N_Z)
         half = core if flip == 0 else 1 - core
         there = field.at[pl.ds(from_plane * PLANE + half * HALF, HALF)]
@@ -93,20 +95,22 @@
     total[...] = jnp.zeros_like(total)
     used = count[0]
 
-    def group(index, carry):
+    def group(index, listed):
         terms = []
         for u in range(GROUP):
             slot = index * GROUP + u
+            away = lax.rem(cols[slot] // PLANE - z + N_Z, N_Z)
             term = lax.dot_general(
                 field[cols[slot]], tiles[slot], (((1,), (1,)), ((), ())), preferred_element_type=F32
             )
-            terms.append(jnp.where(slot < used, term, 0.0))
+            terms.append(jnp.where((slot < used) & (away != 4), term, 0.0))
+            late[1 + listed] = slot
+            listed = listed + jnp.where((slot < used) & (away == 4), 1, 0)
         for u in range(GROUP):
             total[rows[index * GROUP + u]] += terms[u]
-        return carry
-
-    lax.fori_loop(0, (used + GROUP - 1) // GROUP, group, 0)
-    out[...] = total[...].astype(BF16)
+        return listed
+
+    late[0] = lax.fori_loop(0, (used + GROUP - 1) // GROUP, group, jnp.int32(0))
     to_near = jnp.where(place[2] == 0, OWN_X - HALO, 0)
     to_far = OWN_X - HALO - to_near
     for y in range(WIDE_Y):
@@ -120,16 +124,16 @@
     return pl.pallas_call(
         forward_kernel,
         out_shape=[
-            jax.ShapeDtypeStruct((RB, CH, NZ), BF16),
+            jax.ShapeDtypeStruct((RB, CH, NZ), F32),
             jax.ShapeDtypeStruct((WIDE_Y, OWN_X, CH, NZ), BF16),
             jax.ShapeDtypeStruct((WIDE_Y, HALO, CH, NZ), BF16),
             jax.ShapeDtypeStruct((WIDE_Y, HALO, CH, NZ), BF16),
+            jax.ShapeDtypeStruct((SLOTS + 1,), jnp.int32),
         ],
         in_specs=[SMEM] * 4 + [VMEM] + [ANY] * (1 + len(pieces)),
-        out_specs=[VMEM] * 4,
+        out_specs=[VMEM] * 4 + [SMEM],
         scratch_shapes=[
             pltpu.VMEM((LINES, CH, NZ), BF16),
-            pltpu.VMEM((RB, CH, NZ), F32),
             pltpu.SemaphoreType.DMA((1 + len(pieces),)),
         ],
         compiler_params=params(),
@@ -138,6 +142,39 @@
         ),
         name="forward_tiles",
     )(place, rows, cols, count, tiles, plane, *pieces)
+
+
+def late_kernel(place, rows, cols, late, tiles, partial, mine, theirs, out, field, total):
+    core = place[1] & 1
+    field[pl.ds(core * HALF, HALF)] = mine[...]
+    field[pl.ds((1 - core) * HALF, HALF)] = theirs[...]
+    total[...] = partial[...]
+
+    def one(index, carry):
+        slot = late[1 + index]
+        total[rows[slot]] += lax.dot_general(
+            field[lax.rem(cols[slot], PLANE)],
+            tiles[slot],
+            (((1,), (1,)), ((), ())),
+            preferred_element_type=F32,
+        )
+        return carry
+
+    lax.fori_loop(0, late[0], one, 0)
+    out[...] = total[...].astype(BF16)
+
+
+def forward_late(place, rows, cols, late, tiles, partial, mine, theirs):
+    return pl.pallas_call(
+        late_kernel,
+        out_shape=jax.ShapeDtypeStruct((RB, CH, NZ), BF16),
+        in_specs=[SMEM] * 4 + [VMEM] * 4,
+        out_specs=VMEM,
+        scratch_shapes=[pltpu.VMEM((PLANE, CH, NZ), BF16), pltpu.VMEM((RB, CH, NZ), F32)],
+        compiler_params=params(),
+        cost_estimate=pl.CostEstimate(flops=2**24, bytes_accessed=2**21, transcendentals=0),
+        name="forward_late_tiles",
+    )(place, rows, cols, late, tiles, partial, mine, theirs)
 
 
 def adjoint_kernel(
@@ -324,8 +361,9 @@
         for flip in range(2 if steps < 4 else 1):
             chains[flip] = over_row(chains[flip], RING)
             mine[flip, steps] = chains[flip]
-    theirs = [over_row(mine[key], CORE) for key in MINE]
-    return [plane] + [mine[key] for key in MINE] + theirs
+    early = [key for key in MINE if key[1] < 4]
+    theirs = [over_row(mine[key], CORE) for key in early]
+    return plane, [mine[key] for key in early] + theirs, mine[0, 4]
 
 
 def add(*parts):
@@ -382,8 +420,10 @@
     tiles = sens_tiles[0, 0]
     rows, cols, count = tile_rows[0, 0], tile_cols[0, 0], counts[0]
 
-    plane, *pieces = gather_slab(own, row % 2)
-    part, wide, to_near, to_far = forward(place, rows, cols, count, tiles, plane, pieces)
+    plane, early, mine = gather_slab(own, row % 2)
+    partial, wide, to_near, to_far, late = forward(place, rows, cols, count, tiles, plane, early)
+    mine = after(mine, partial)
+    part = forward_late(place, rows, cols, late, tiles, partial, mine, over_row(mine, CORE))
     came = over_col(part, X_HI)
     near = over_col(to_near, X_HI)
     part = add(part, came)

time: 108 us -> 110 us (1.019); the launches traced: 107 us -> 110 us
  starting transfers between devices: 59.7 us -> 51.7 us
  waiting for transfers between devices: 25.5 us -> 31.2 us
  Pallas kernels: 6.93 us -> 12.3 us
    ppermute x26, starting transfers between devices: 49.5 us -> 40 us  [over_row(): return lax.ppermute(value, 'row', pairs)]
    ppermute x26, waiting for transfers between devices: 18 us -> 21 us  [over_row(): return lax.ppermute(value, 'row', pairs)]
    ppermute x6, waiting for transfers between devices: 7.46 us -> 10.2 us  [over_col(): return lax.ppermute(value, 'col', pairs)]
    pallas_call x1, Pallas kernels: 1.66 us -> 4.17 us  [adjoint(): pl.pallas_call(adjoint_kernel, out_shape=[jax.ShapeDtypeStruct((FIRST + 1...]
    pallas_call x1, Pallas kernels: 1.39 us -> 3.16 us  [forward(): pl.pallas_call(forward_kernel, out_shape=[jax.ShapeDtypeStruct((RB, CH, N...]
    ppermute x6, starting transfers between devices: 10.1 us -> 11.7 us  [over_col(): return lax.ppermute(value, 'col', pairs)]
  transfers between devices with their start and end apart: 32 -> 32, of which waited for: 15 -> 16; matrix products, arithmetic and copies ran while one was open for 1% -> 1% of each run, Pallas kernels for 4% -> 6%
where the time goes in v4:
time: 110 us
  starting transfers between devices  51.7 us (47%)
  waiting for transfers between devices  31.2 us (28%)
  Pallas kernels  12.3 us (11%)
  blocking collectives  9.59 us (9%)
  other arithmetic  2.84 us (3%)
  local copies, waits for them, and re-layouts  1.34 us (1%)
    ppermute x26, starting transfers between devices, over_row(): return lax.ppermute(value, 'row', pairs)  40 us
    ppermute x26, waiting for transfers between devices, over_row(): return lax.ppermute(value, 'row', pairs)  21 us
    ppermute x6, starting transfers between devices, over_col(): return lax.ppermute(value, 'col', pairs)  11.7 us
    ppermute x6, waiting for transfers between devices, over_col(): return lax.ppermute(value, 'col', pairs)  10.2 us
    all_gather x1, blocking collectives, gather_slab(): lax.all_gather(own, 'row', axis=0, tiled=True, axis_index_groups=QUADS)  9.59 us
    pallas_call x1, Pallas kernels, adjoint(): pl.pallas_call(adjoint_kernel, out_shape=[jax.ShapeDtypeStruct((FIRST + 1...  4.17 us
    pallas_call x1, Pallas kernels, prox_step(): pl.pallas_call(prox_kernel, out_shape=jax.ShapeDtypeStruct((OWN_Y, OWN_X,...  3.88 us
    pallas_call x1, Pallas kernels, forward(): pl.pallas_call(forward_kernel, out_shape=[jax.ShapeDtypeStruct((RB, CH, N...  3.16 us
  transfers between devices with their start and end apart: 32, of which 16 were waited for; matrix products, arithmetic and copies ran while one was open for 1% of the time, Pallas kernels for 6%

profile of v4, /device:TPU:1, one launch (start us, length us, event | category | flops | bytes accessed | tf_op | source)
XLA Modules:
  0.0 109.9 jit_solution(6366889830895079826)
XLA Ops:
  0.1 1.1 convert_element_type.135
  1.2 9.6 %all_gather.3.plane = bf16[64,32,128]{2,1,0:T(8,128)(2,1)S(1)} all-gather(bf16[16,32,128]{2,1,0:T(8,128)(2,1)S(1)} %bitcast.34), channel_id=1, replica_groups={{0,8,16,24},{32,40,48,56},{64,72,80,88},{96,104,112,120},{128,136,144,1..., dimensions={0}, use_global_device_ids=true | all-gather | bytes 655360 | tf_op jit(solution)/shard_map/all_gather | solution.py:357
  10.8 4.6 %collective-permute-start.3 = (bf16[32,32,128]{2,1,0:T(8,128)(2,1)S(1)}, bf16[32,32,128]{2,1,0:T(8,128)(2,1)S(1)}, u32[]{:S(2)}, u32[]{:S(2)}) collective-permute-start(bf16[32,32,128]{2,1,0:T(8,128)(2,1)S(1)} %get-tuple-element.53), channel_id=1, source_target_pairs={{0,32},{8,232},{16,48},{24,248},{32,64},{40,8},{48,80},{56,24},{64... | collective-permute-start | bytes 786440 | tf_op jit(solution)/shard_map/ppermute | solution.py:64
  15.4 0.7 collective-permute-start
  16.1 2.6 %collective-permute-done.3.rest_3_ = bf16[32,32,128]{2,1,0:T(8,128)(2,1)S(1)} collective-permute-done((bf16[32,32,128]{2,1,0:T(8,128)(2,1)S(1)}, bf16[32,32,128]{2,1,0:T(8,128)(2,1)S(1)}, u32[]{:S(2)}, u32[]{:S(2)}) %collective-permute-start.3) | collective-permute-done | bytes 262176 | tf_op jit(solution)/shard_map/ppermute | solution.py:64
  18.7 3.1 %collective-permute-start.4 = (bf16[32,32,128]{2,1,0:T(8,128)(2,1)S(1)}, bf16[32,32,128]{2,1,0:T(8,128)(2,1)S(1)}, u32[]{:S(2)}, u32[]{:S(2)}) collective-permute-start(bf16[32,32,128]{2,1,0:T(8,128)(2,1)S(1)} %collective-permute-done.3.rest_3_), channel_id=1, source_target_pairs={{0,32},{8,232},{16,48},{24,248},{32,64},{40,8},{48,80},{56,24},{64... | collective-permute-start | bytes 786440 | tf_op jit(solution)/shard_map/ppermute | solution.py:64
  21.8 2.8 %collective-permute-start.1 = (bf16[32,32,128]{2,1,0:T(8,128)(2,1)S(1)}, bf16[32,32,128]{2,1,0:T(8,128)(2,1)S(1)}, u32[]{:S(2)}, u32[]{:S(2)}) collective-permute-start(bf16[32,32,128]{2,1,0:T(8,128)(2,1)S(1)} %collective-permute-done.rest_0_), channel_id=1, source_target_pairs={{0,32},{8,232},{16,48},{24,248},{32,64},{40,8},{48,80},{56,24},{64... | collective-permute-start | bytes 786440 | tf_op jit(solution)/shard_map/ppermute | solution.py:64
  24.6 0.5 collective-permute-done.4.rest_4_
  25.1 3.1 %collective-permute-start.5 = (bf16[32,32,128]{2,1,0:T(8,128)(2,1)S(1)}, bf16[32,32,128]{2,1,0:T(8,128)(2,1)S(1)}, u32[]{:S(2)}, u32[]{:S(2)}) collective-permute-start(bf16[32,32,128]{2,1,0:T(8,128)(2,1)S(1)} %collective-permute-done.4.rest_4_), channel_id=1, source_target_pairs={{0,32},{8,232},{16,48},{24,248},{32,64},{40,8},{48,80},{56,24},{64... | collective-permute-start | bytes 786440 | tf_op jit(solution)/shard_map/ppermute | solution.py:64
  28.2 2.8 %collective-permute-start.2 = (bf16[32,32,128]{2,1,0:T(8,128)(2,1)S(1)}, bf16[32,32,128]{2,1,0:T(8,128)(2,1)S(1)}, u32[]{:S(2)}, u32[]{:S(2)}) collective-permute-start(bf16[32,32,128]{2,1,0:T(8,128)(2,1)S(1)} %collective-permute-done.1.rest_1_), channel_id=1, source_target_pairs={{0,32},{8,232},{16,48},{24,248},{32,64},{40,8},{48,80},{56,24},{64... | collective-permute-start | bytes 786440 | tf_op jit(solution)/shard_map/ppermute | solution.py:64
  31.0 0.5 collective-permute-start.10
  31.6 3.8 %collective-permute-start.11 = (bf16[32,32,128]{2,1,0:T(8,128)(2,1)S(1)}, bf16[32,32,128]{2,1,0:T(8,128)(2,1)S(1)}, u32[]{:S(2)}, u32[]{:S(2)}) collective-permute-start(bf16[32,32,128]{2,1,0:T(8,128)(2,1)S(1)} %collective-permute-done.5.rest_5_), channel_id=1, source_target_pairs={{0,8},{8,0},{16,24},{24,16},{32,40},{40,32},{48,56},{56,48},{64,72... | collective-permute-start | bytes 786440 | tf_op jit(solution)/shard_map/ppermute | solution.py:64
  35.3 2.8 %collective-permute-start.8 = (bf16[32,32,128]{2,1,0:T(8,128)(2,1)S(1)}, bf16[32,32,128]{2,1,0:T(8,128)(2,1)S(1)}, u32[]{:S(2)}, u32[]{:S(2)}) collective-permute-start(bf16[32,32,128]{2,1,0:T(8,128)(2,1)S(1)} %collective-permute-done.2.rest_2_), channel_id=1, source_target_pairs={{0,8},{8,0},{16,24},{24,16},{32,40},{40,32},{48,56},{56,48},{64,72... | collective-permute-start | bytes 786440 | tf_op jit(solution)/shard_map/ppermute | solution.py:64
  38.8 0.5 collective-permute-done.8.rest_8_
  39.3 0.7 copy-done.3
  40.0 0.7 copy-done.4
  40.6 3.2 %forward_tiles.1 = (f32[8,32,128]{2,1,0:T(8,128)S(1)}, bf16[8,8,32,128]{3,2,1,0:T(8,128)(2,1)S(1)}, bf16[8,3,32,128]{3,2,1,0:T(8,128)(2,1)S(1)}, bf16[8,3,32,128]{3,2,1,0:T(8,128)(2,1)S(1)}, s32[49]{0:T(128)S(1)}) custom-call(s32[3]{0:T(128)S(1)} %get-tuple-element.56.place, s32[48]{0:T(128)S(1)} %bitcast.25, s32[48]{0:T(128)S(1)} %bitcast.28, ...), custom_call_target="tpu_custom_call" | custom-call | flops 50331648 | bytes 12582912 | tf_op jit(solution)/shard_map/forward_tiles/pallas_call | solution.py:124
  43.8 1.9 %collective-permute-start.14 = (bf16[32,32,128]{2,1,0:T(8,128)(2,1)S(1)}, bf16[32,32,128]{2,1,0:T(8,128)(2,1)S(1)}, u32[]{:S(2)}, u32[]{:S(2)}) collective-permute-start(bf16[32,32,128]{2,1,0:T(8,128)(2,1)S(1)} %collective-permute-done.13.mine), channel_id=1, source_target_pairs={{0,8},{8,0},{16,24},{24,16},{32,40},{40,32},{48,56},{56,48},{64,72... | collective-permute-start | bytes 786440 | tf_op jit(solution)/shard_map/ppermute | solution.py:64
  45.7 1.2 %collective-permute-done.14.theirs = bf16[32,32,128]{2,1,0:T(8,128)(2,1)S(1)} collective-permute-done((bf16[32,32,128]{2,1,0:T(8,128)(2,1)S(1)}, bf16[32,32,128]{2,1,0:T(8,128)(2,1)S(1)}, u32[]{:S(2)}, u32[]{:S(2)}) %collective-permute-start.14) | collective-permute-done | bytes 262176 | tf_op jit(solution)/shard_map/ppermute | solution.py:64
  46.9 1.1 forward_late_tiles.1
  48.0 2.4 %collective-permute-start.15 = (bf16[8,32,128]{2,1,0:T(8,128)(2,1)S(1)}, bf16[8,32,128]{2,1,0:T(8,128)(2,1)S(1)}, u32[]{:S(2)}, u32[]{:S(2)}) collective-permute-start(bf16[8,32,128]{2,1,0:T(8,128)(2,1)S(1)} %forward_late_tiles.1), channel_id=1, source_target_pairs={{0,1},{1,0},{2,3},{3,2},{4,5},{5,4},{6,7},{7,6},{8,9},{9,8},{10,11... | collective-permute-start | bytes 196616 | tf_op jit(solution)/shard_map/ppermute | solution.py:68
  50.4 0.7 collective-permute-start.12
  51.0 1.6 %collective-permute-done.15 = bf16[8,32,128]{2,1,0:T(8,128)(2,1)S(1)} collective-permute-done((bf16[8,32,128]{2,1,0:T(8,128)(2,1)S(1)}, bf16[8,32,128]{2,1,0:T(8,128)(2,1)S(1)}, u32[]{:S(2)}, u32[]{:S(2)}) %collective-permute-start.15) | collective-permute-done | bytes 65568 | tf_op jit(solution)/shard_map/ppermute | solution.py:68
  52.7 2.7 %collective-permute-start.18 = (bf16[8,32,128]{2,1,0:T(8,128)(2,1)S(1)}, bf16[8,32,128]{2,1,0:T(8,128)(2,1)S(1)}, u32[]{:S(2)}, u32[]{:S(2)}) collective-permute-start(bf16[8,32,128]{2,1,0:T(8,128)(2,1)S(1)} %add_convert_fusion.10.rest_0_), channel_id=1, source_target_pairs={{0,6},{1,7},{2,0},{3,1},{4,2},{5,3},{6,4},{7,5},{8,14},{9,15},{10,... | collective-permute-start | bytes 196616 | tf_op jit(solution)/shard_map/ppermute | solution.py:68
  55.4 2.1 %collective-permute-start.17 = (bf16[8,32,128]{2,1,0:T(8,128)(2,1)S(1)}, bf16[8,32,128]{2,1,0:T(8,128)(2,1)S(1)}, u32[]{:S(2)}, u32[]{:S(2)}) collective-permute-start(bf16[8,32,128]{2,1,0:T(8,128)(2,1)S(1)} %add_convert_fusion.10.rest_0_), channel_id=1, source_target_pairs={{0,4},{1,5},{2,6},{3,7},{4,0},{5,1},{6,2},{7,3},{8,12},{9,13},{10,... | collective-permute-start | bytes 196616 | tf_op jit(solution)/shard_map/ppermute | solution.py:68
  57.5 0.2 collective-permute-done.18.rest_3_
  57.7 2.4 %collective-permute-done.17.rest_2_ = bf16[8,32,128]{2,1,0:T(8,128)(2,1)S(1)} collective-permute-done((bf16[8,32,128]{2,1,0:T(8,128)(2,1)S(1)}, bf16[8,32,128]{2,1,0:T(8,128)(2,1)S(1)}, u32[]{:S(2)}, u32[]{:S(2)}) %collective-permute-start.17) | collective-permute-done | bytes 65568 | tf_op jit(solution)/shard_map/ppermute | solution.py:68
  60.0 2.1 %collective-permute-done.16.rest_1_ = bf16[8,32,128]{2,1,0:T(8,128)(2,1)S(1)} collective-permute-done((bf16[8,32,128]{2,1,0:T(8,128)(2,1)S(1)}, bf16[8,32,128]{2,1,0:T(8,128)(2,1)S(1)}, u32[]{:S(2)}, u32[]{:S(2)}) %collective-permute-start.16) | collective-permute-done | bytes 65568 | tf_op jit(solution)/shard_map/ppermute | solution.py:68
  62.1 4.2 %adjoint_tiles.1 = (bf16[97,32,128]{2,1,0:T(8,128)(2,1)S(1)}, bf16[129,32,128]{2,1,0:T(8,128)(2,1)S(1)}, bf16[289,32,128]{2,1,0:T(8,128)(2,1)S(1)}) custom-call(s32[3]{0:T(128)S(1)} %get-tuple-element.56.place, s32[48]{0:T(128)S(1)} %bitcast.27, s32[48]{0:T(128)S(1)} %bitcast.30, s32[1]{0:T(128)} %bitcast.18.count, bf16[48,128,128]{2,1,0:T(8,128)(2,1)S(1)} %bitcast.21, ...), custom_call_target="tpu_custom_call" | custom-call | flops 50331648 | bytes 12582912 | tf_op jit(solution)/shard_map/adjoint_tiles/pallas_call | solution.py:249
  66.3 1.9 %collective-permute-start.20 = (bf16[97,32,128]{2,1,0:T(8,128)(2,1)S(1)}, bf16[97,32,128]{2,1,0:T(8,128)(2,1)S(1)}, u32[]{:S(2)}, u32[]{:S(2)}) collective-permute-start(bf16[97,32,128]{2,1,0:T(8,128)(2,1)S(1)} %get-tuple-element.36), channel_id=1, source_target_pairs={{0,8},{8,0},{16,24},{24,16},{32,40},{40,32},{48,56},{56,48},{64,72... | collective-permute-start | bytes 2383880 | tf_op jit(solution)/shard_map/ppermute | solution.py:64
  68.3 1.8 %collective-permute-done.20 = bf16[97,32,128]{2,1,0:T(8,128)(2,1)S(1)} collective-permute-done((bf16[97,32,128]{2,1,0:T(8,128)(2,1)S(1)}, bf16[97,32,128]{2,1,0:T(8,128)(2,1)S(1)}, u32[]{:S(2)}, u32[]{:S(2)}) %collective-permute-start.20) | collective-permute-done | bytes 794656 | tf_op jit(solution)/shard_map/ppermute | solution.py:64
  70.4 5.4 %collective-permute-done.21 = bf16[32,32,128]{2,1,0:T(8,128)(2,1)S(1)} collective-permute-done((bf16[32,32,128]{2,1,0:T(8,128)(2,1)S(1)}, bf16[32,32,128]{2,1,0:T(8,128)(2,1)S(1)}, u32[]{:S(2)}, u32[]{:S(2)}) %collective-permute-start.21) | collective-permute-done | bytes 262176 | tf_op jit(solution)/shard_map/ppermute | solution.py:64
  76.0 1.0 collective-permute-start.22
  77.0 1.7 %collective-permute-done.23 = bf16[32,32,128]{2,1,0:T(8,128)(2,1)S(1)} collective-permute-done((bf16[32,32,128]{2,1,0:T(8,128)(2,1)S(1)}, bf16[32,32,128]{2,1,0:T(8,128)(2,1)S(1)}, u32[]{:S(2)}, u32[]{:S(2)}) %collective-permute-start.23) | collective-permute-done | bytes 262176 | tf_op jit(solution)/shard_map/ppermute | solution.py:64
  78.8 1.0 collective-permute-start.25
  79.8 1.5 %collective-permute-done.22 = bf16[32,32,128]{2,1,0:T(8,128)(2,1)S(1)} collective-permute-done((bf16[32,32,128]{2,1,0:T(8,128)(2,1)S(1)}, bf16[32,32,128]{2,1,0:T(8,128)(2,1)S(1)}, u32[]{:S(2)}, u32[]{:S(2)}) %collective-permute-start.22) | collective-permute-done | bytes 262176 | tf_op jit(solution)/shard_map/ppermute | solution.py:64
  81.4 2.2 %collective-permute-start.24 = (bf16[32,32,128]{2,1,0:T(8,128)(2,1)S(1)}, bf16[32,32,128]{2,1,0:T(8,128)(2,1)S(1)}, u32[]{:S(2)}, u32[]{:S(2)}) collective-permute-start(bf16[32,32,128]{2,1,0:T(8,128)(2,1)S(1)} %add_convert_fusion.2), channel_id=1, source_target_pairs={{0,32},{8,232},{16,48},{24,248},{32,64},{40,8},{48,80},{56,24},{64... | collective-permute-start | bytes 786440 | tf_op jit(solution)/shard_map/ppermute | solution.py:64
  83.6 0.8 collective-permute-done.25
  84.5 1.9 %collective-permute-start.28 = (bf16[32,32,128]{2,1,0:T(8,128)(2,1)S(1)}, bf16[32,32,128]{2,1,0:T(8,128)(2,1)S(1)}, u32[]{:S(2)}, u32[]{:S(2)}) collective-permute-start(bf16[32,32,128]{2,1,0:T(8,128)(2,1)S(1)} %add_convert_fusion.1), channel_id=1, source_target_pairs={{0,32},{8,232},{16,48},{24,248},{32,64},{40,8},{48,80},{56,24},{64... | collective-permute-start | bytes 786440 | tf_op jit(solution)/shard_map/ppermute | solution.py:64
  86.4 3.9 %collective-permute-start.26 = (bf16[8,3,32,128]{3,2,1,0:T(8,128)(2,1)S(1)}, bf16[8,3,32,128]{3,2,1,0:T(8,128)(2,1)S(1)}, u32[]{:S(2)}, u32[]{:S(2)}) collective-permute-start(bf16[8,3,32,128]{3,2,1,0:T(8,128)(2,1)S(1)} %get-tuple-element.44), channel_id=1, source_target_pairs={{0,7},{1,2},{2,1},{3,4},{4,3},{5,6},{6,5},{7,0},{8,15},{9,10},{10,... | collective-permute-start | bytes 589832 | tf_op jit(solution)/shard_map/ppermute | solution.py:68
  90.4 0.2 collective-permute-start.27
  90.6 0.2 collective-permute-start.30
  90.8 3.9 %collective-permute-done.26.far = bf16[8,3,32,128]{3,2,1,0:T(8,128)(2,1)S(1)} collective-permute-done((bf16[8,3,32,128]{3,2,1,0:T(8,128)(2,1)S(1)}, bf16[8,3,32,128]{3,2,1,0:T(8,128)(2,1)S(1)}, u32[]{:S(2)}, u32[]{:S(2)}) %collective-permute-start.26) | collective-permute-done | bytes 196640 | tf_op jit(solution)/shard_map/ppermute | solution.py:68
  94.7 3.9 %tv_prox.1 = f32[2,8,32,128]{3,2,1,0:T(8,128)S(1)} custom-call(s32[3]{0:T(128)S(1)} %get-tuple-element.55.start, bf16[8,8,32,128]{3,2,1,0:T(8,128)(2,1)S(1)} %get-tuple-element.28.wide, bf16[8,3,32,128]{3,2,1,0:T(8,128)(2,1)S(1)} %collective-permute-done.12.near, bf16[8,3,32,128]{3,2,1,0:T(8,128)(2,1)S(1)} %collective-permute-done.26.far, ...), custom_call_target="tpu_custom_call" | custom-call | flops 16777216 | bytes 12582912 | tf_op jit(solution)/shard_map/tv_prox/pallas_call | solution.py:339
  98.7 5.3 %collective-permute-start.31 = (bf16[16,32,128]{2,1,0:T(8,128)(2,1)S(1)}, bf16[16,32,128]{2,1,0:T(8,128)(2,1)S(1)}, u32[]{:S(2)}, u32[]{:S(2)}) collective-permute-start(bf16[16,32,128]{2,1,0:T(8,128)(2,1)S(1)} %get-tuple-element.52), channel_id=1, source_target_pairs={{0,8},{8,0},{16,24},{24,16},{32,40},{40,32},{48,56},{56,48},{64,72... | collective-permute-start | bytes 393224 | tf_op jit(solution)/shard_map/ppermute | solution.py:64
  104.0 1.0 collective-permute-done.31
  105.0 4.1 %collective-permute-done.29 = bf16[16,32,128]{2,1,0:T(8,128)(2,1)S(1)} collective-permute-done((bf16[16,32,128]{2,1,0:T(8,128)(2,1)S(1)}, bf16[16,32,128]{2,1,0:T(8,128)(2,1)S(1)}, u32[]{:S(2)}, u32[]{:S(2)}) %collective-permute-start.29) | collective-permute-done | bytes 131104 | tf_op jit(solution)/shard_map/ppermute | solution.py:64
  109.1 0.7 subtract_bitcast_fusion
  (49 shorter events, 1.4 us)
Async XLA Ops:
  0.0 39.3 %copy-start = (bf16[1,1,48,128,128]{4,3,2,1,0:T(8,128)(2,1)S(1)}, bf16[1,1,48,128,128]{4,3,2,1,0:T(8,128)(2,1)}, u32[]{:S(2)}) copy-start(bf16[1,1,48,128,128]{4,3,2,1,0:T(8,128)(2,1)} %param.12) | copy-start | bytes 4718596
  10.8 7.9 %collective-permute-start.3 = (bf16[32,32,128]{2,1,0:T(8,128)(2,1)S(1)}, bf16[32,32,128]{2,1,0:T(8,128)(2,1)S(1)}, u32[]{:S(2)}, u32[]{:S(2)}) collective-permute-start(bf16[32,32,128]{2,1,0:T(8,128)(2,1)S(1)} %get-tuple-element.53), channel_id=1, source_target_pairs={{0,32},{8,232},{16,48},{24,248},{32,64},{40,8},{48,80},{56,24},{64... | collective-permute-start | bytes 786440 | tf_op jit(solution)/shard_map/ppermute | solution.py:64
  15.4 6.4 %collective-permute-start = (bf16[32,32,128]{2,1,0:T(8,128)(2,1)S(1)}, bf16[32,32,128]{2,1,0:T(8,128)(2,1)S(1)}, u32[]{:S(2)}, u32[]{:S(2)}) collective-permute-start(bf16[32,32,128]{2,1,0:T(8,128)(2,1)S(1)} %get-tuple-element.54), channel_id=1, source_target_pairs={{0,32},{8,232},{16,48},{24,248},{32,64},{40,8},{48,80},{56,24},{64... | collective-permute-start | bytes 786440 | tf_op jit(solution)/shard_map/ppermute | solution.py:64
  18.7 6.4 %collective-permute-start.4 = (bf16[32,32,128]{2,1,0:T(8,128)(2,1)S(1)}, bf16[32,32,128]{2,1,0:T(8,128)(2,1)S(1)}, u32[]{:S(2)}, u32[]{:S(2)}) collective-permute-start(bf16[32,32,128]{2,1,0:T(8,128)(2,1)S(1)} %collective-permute-done.3.rest_3_), channel_id=1, source_target_pairs={{0,32},{8,232},{16,48},{24,248},{32,64},{40,8},{48,80},{56,24},{64... | collective-permute-start | bytes 786440 | tf_op jit(solution)/shard_map/ppermute | solution.py:64
  21.8 6.4 %collective-permute-start.1 = (bf16[32,32,128]{2,1,0:T(8,128)(2,1)S(1)}, bf16[32,32,128]{2,1,0:T(8,128)(2,1)S(1)}, u32[]{:S(2)}, u32[]{:S(2)}) collective-permute-start(bf16[32,32,128]{2,1,0:T(8,128)(2,1)S(1)} %collective-permute-done.rest_0_), channel_id=1, source_target_pairs={{0,32},{8,232},{16,48},{24,248},{32,64},{40,8},{48,80},{56,24},{64... | collective-permute-start | bytes 786440 | tf_op jit(solution)/shard_map/ppermute | solution.py:64
  24.6 6.9 %collective-permute-start.9 = (bf16[32,32,128]{2,1,0:T(8,128)(2,1)S(1)}, bf16[32,32,128]{2,1,0:T(8,128)(2,1)S(1)}, u32[]{:S(2)}, u32[]{:S(2)}) collective-permute-start(bf16[32,32,128]{2,1,0:T(8,128)(2,1)S(1)} %collective-permute-done.3.rest_3_), channel_id=1, source_target_pairs={{0,8},{8,0},{16,24},{24,16},{32,40},{40,32},{48,56},{56,48},{64,72... | collective-permute-start | bytes 786440 | tf_op jit(solution)/shard_map/ppermute | solution.py:64
  25.1 6.4 %collective-permute-start.5 = (bf16[32,32,128]{2,1,0:T(8,128)(2,1)S(1)}, bf16[32,32,128]{2,1,0:T(8,128)(2,1)S(1)}, u32[]{:S(2)}, u32[]{:S(2)}) collective-permute-start(bf16[32,32,128]{2,1,0:T(8,128)(2,1)S(1)} %collective-permute-done.4.rest_4_), channel_id=1, source_target_pairs={{0,32},{8,232},{16,48},{24,248},{32,64},{40,8},{48,80},{56,24},{64... | collective-permute-start | bytes 786440 | tf_op jit(solution)/shard_map/ppermute | solution.py:64
  28.2 7.1 %collective-permute-start.2 = (bf16[32,32,128]{2,1,0:T(8,128)(2,1)S(1)}, bf16[32,32,128]{2,1,0:T(8,128)(2,1)S(1)}, u32[]{:S(2)}, u32[]{:S(2)}) collective-permute-start(bf16[32,32,128]{2,1,0:T(8,128)(2,1)S(1)} %collective-permute-done.1.rest_1_), channel_id=1, source_target_pairs={{0,32},{8,232},{16,48},{24,248},{32,64},{40,8},{48,80},{56,24},{64... | collective-permute-start | bytes 786440 | tf_op jit(solution)/shard_map/ppermute | solution.py:64
  31.0 7.1 %collective-permute-start.6 = (bf16[32,32,128]{2,1,0:T(8,128)(2,1)S(1)}, bf16[32,32,128]{2,1,0:T(8,128)(2,1)S(1)}, u32[]{:S(2)}, u32[]{:S(2)}) collective-permute-start(bf16[32,32,128]{2,1,0:T(8,128)(2,1)S(1)} %collective-permute-done.rest_0_), channel_id=1, source_target_pairs={{0,8},{8,0},{16,24},{24,16},{32,40},{40,32},{48,56},{56,48},{64,72... | collective-permute-start | bytes 786440 | tf_op jit(solution)/shard_map/ppermute | solution.py:64
  31.0 7.8 %collective-permute-start.10 = (bf16[32,32,128]{2,1,0:T(8,128)(2,1)S(1)}, bf16[32,32,128]{2,1,0:T(8,128)(2,1)S(1)}, u32[]{:S(2)}, u32[]{:S(2)}) collective-permute-start(bf16[32,32,128]{2,1,0:T(8,128)(2,1)S(1)} %collective-permute-done.4.rest_4_), channel_id=1, source_target_pairs={{0,8},{8,0},{16,24},{24,16},{32,40},{40,32},{48,56},{56,48},{64,72... | collective-permute-start | bytes 786440 | tf_op jit(solution)/shard_map/ppermute | solution.py:64
  31.6 7.3 %collective-permute-start.7 = (bf16[32,32,128]{2,1,0:T(8,128)(2,1)S(1)}, bf16[32,32,128]{2,1,0:T(8,128)(2,1)S(1)}, u32[]{:S(2)}, u32[]{:S(2)}) collective-permute-start(bf16[32,32,128]{2,1,0:T(8,128)(2,1)S(1)} %collective-permute-done.1.rest_1_), channel_id=1, source_target_pairs={{0,8},{8,0},{16,24},{24,16},{32,40},{40,32},{48,56},{56,48},{64,72... | collective-permute-start | bytes 786440 | tf_op jit(solution)/shard_map/ppermute | solution.py:64
  31.6 7.3 %collective-permute-start.11 = (bf16[32,32,128]{2,1,0:T(8,128)(2,1)S(1)}, bf16[32,32,128]{2,1,0:T(8,128)(2,1)S(1)}, u32[]{:S(2)}, u32[]{:S(2)}) collective-permute-start(bf16[32,32,128]{2,1,0:T(8,128)(2,1)S(1)} %collective-permute-done.5.rest_5_), channel_id=1, source_target_pairs={{0,8},{8,0},{16,24},{24,16},{32,40},{40,32},{48,56},{56,48},{64,72... | collective-permute-start | bytes 786440 | tf_op jit(solution)/shard_map/ppermute | solution.py:64
  35.3 4.0 %collective-permute-start.8 = (bf16[32,32,128]{2,1,0:T(8,128)(2,1)S(1)}, bf16[32,32,128]{2,1,0:T(8,128)(2,1)S(1)}, u32[]{:S(2)}, u32[]{:S(2)}) collective-permute-start(bf16[32,32,128]{2,1,0:T(8,128)(2,1)S(1)} %collective-permute-done.2.rest_2_), channel_id=1, source_target_pairs={{0,8},{8,0},{16,24},{24,16},{32,40},{40,32},{48,56},{56,48},{64,72... | collective-permute-start | bytes 786440 | tf_op jit(solution)/shard_map/ppermute | solution.py:64
  38.1 5.7 %collective-permute-start.13 = (bf16[32,32,128]{2,1,0:T(8,128)(2,1)S(1)}, bf16[32,32,128]{2,1,0:T(8,128)(2,1)S(1)}, u32[]{:S(2)}, u32[]{:S(2)}) collective-permute-start(bf16[32,32,128]{2,1,0:T(8,128)(2,1)S(1)} %collective-permute-done.2.rest_2_), channel_id=1, source_target_pairs={{0,32},{8,232},{16,48},{24,248},{32,64},{40,8},{48,80},{56,24},{64... | collective-permute-start | bytes 786440 | tf_op jit(solution)/shard_map/ppermute | solution.py:64
  39.3 0.7 copy-start.3
  40.0 0.7 copy-start.4
  43.8 18.3 %copy-start.5 = (f32[1024]{0:T(1024)S(1)}, f32[1024]{0:T(1024)}, u32[]{:S(2)}) copy-start(f32[1024]{0:T(1024)} %param.10) | copy-start | bytes 12292
  43.8 18.3 %copy-start.6 = (f32[1024]{0:T(1024)S(1)}, f32[1024]{0:T(1024)}, u32[]{:S(2)}) copy-start(f32[1024]{0:T(1024)} %param.11) | copy-start | bytes 12292
  43.8 3.1 %collective-permute-start.14 = (bf16[32,32,128]{2,1,0:T(8,128)(2,1)S(1)}, bf16[32,32,128]{2,1,0:T(8,128)(2,1)S(1)}, u32[]{:S(2)}, u32[]{:S(2)}) collective-permute-start(bf16[32,32,128]{2,1,0:T(8,128)(2,1)S(1)} %collective-permute-done.13.mine), channel_id=1, source_target_pairs={{0,8},{8,0},{16,24},{24,16},{32,40},{40,32},{48,56},{56,48},{64,72... | collective-permute-start | bytes 786440 | tf_op jit(solution)/shard_map/ppermute | solution.py:64
  48.0 4.7 %collective-permute-start.15 = (bf16[8,32,128]{2,1,0:T(8,128)(2,1)S(1)}, bf16[8,32,128]{2,1,0:T(8,128)(2,1)S(1)}, u32[]{:S(2)}, u32[]{:S(2)}) collective-permute-start(bf16[8,32,128]{2,1,0:T(8,128)(2,1)S(1)} %forward_late_tiles.1), channel_id=1, source_target_pairs={{0,1},{1,0},{2,3},{3,2},{4,5},{5,4},{6,7},{7,6},{8,9},{9,8},{10,11... | collective-permute-start | bytes 196616 | tf_op jit(solution)/shard_map/ppermute | solution.py:68
  50.4 7.1 %collective-permute-start.12 = (bf16[8,3,32,128]{3,2,1,0:T(8,128)(2,1)S(1)}, bf16[8,3,32,128]{3,2,1,0:T(8,128)(2,1)S(1)}, u32[]{:S(2)}, u32[]{:S(2)}) collective-permute-start(bf16[8,3,32,128]{3,2,1,0:T(8,128)(2,1)S(1)} %get-tuple-element.29), channel_id=1, source_target_pairs={{0,1},{1,0},{2,3},{3,2},{4,5},{5,4},{6,7},{7,6},{8,9},{9,8},{10,11... | collective-permute-start | bytes 589832 | tf_op jit(solution)/shard_map/ppermute | solution.py:68
  52.7 5.0 %collective-permute-start.18 = (bf16[8,32,128]{2,1,0:T(8,128)(2,1)S(1)}, bf16[8,32,128]{2,1,0:T(8,128)(2,1)S(1)}, u32[]{:S(2)}, u32[]{:S(2)}) collective-permute-start(bf16[8,32,128]{2,1,0:T(8,128)(2,1)S(1)} %add_convert_fusion.10.rest_0_), channel_id=1, source_target_pairs={{0,6},{1,7},{2,0},{3,1},{4,2},{5,3},{6,4},{7,5},{8,14},{9,15},{10,... | collective-permute-start | bytes 196616 | tf_op jit(solution)/shard_map/ppermute | solution.py:68
  55.4 4.6 %collective-permute-start.17 = (bf16[8,32,128]{2,1,0:T(8,128)(2,1)S(1)}, bf16[8,32,128]{2,1,0:T(8,128)(2,1)S(1)}, u32[]{:S(2)}, u32[]{:S(2)}) collective-permute-start(bf16[8,32,128]{2,1,0:T(8,128)(2,1)S(1)} %add_convert_fusion.10.rest_0_), channel_id=1, source_target_pairs={{0,4},{1,5},{2,6},{3,7},{4,0},{5,1},{6,2},{7,3},{8,12},{9,13},{10,... | collective-permute-start | bytes 196616 | tf_op jit(solution)/shard_map/ppermute | solution.py:68
  57.5 4.6 %collective-permute-start.16 = (bf16[8,32,128]{2,1,0:T(8,128)(2,1)S(1)}, bf16[8,32,128]{2,1,0:T(8,128)(2,1)S(1)}, u32[]{:S(2)}, u32[]{:S(2)}) collective-permute-start(bf16[8,32,128]{2,1,0:T(8,128)(2,1)S(1)} %add_convert_fusion.10.rest_0_), channel_id=1, source_target_pairs={{0,2},{1,3},{2,4},{3,5},{4,6},{5,7},{6,0},{7,1},{8,10},{9,11},{10,... | collective-permute-start | bytes 196616 | tf_op jit(solution)/shard_map/ppermute | solution.py:68
  66.3 3.8 %collective-permute-start.20 = (bf16[97,32,128]{2,1,0:T(8,128)(2,1)S(1)}, bf16[97,32,128]{2,1,0:T(8,128)(2,1)S(1)}, u32[]{:S(2)}, u32[]{:S(2)}) collective-permute-start(bf16[97,32,128]{2,1,0:T(8,128)(2,1)S(1)} %get-tuple-element.36), channel_id=1, source_target_pairs={{0,8},{8,0},{16,24},{24,16},{32,40},{40,32},{48,56},{56,48},{64,72... | collective-permute-start | bytes 2383880 | tf_op jit(solution)/shard_map/ppermute | solution.py:64
  68.2 10.5 %collective-permute-start.19 = (bf16[129,32,128]{2,1,0:T(8,128)(2,1)S(1)}, bf16[129,32,128]{2,1,0:T(8,128)(2,1)S(1)}, u32[]{:S(2)}, u32[]{:S(2)}) collective-permute-start(bf16[129,32,128]{2,1,0:T(8,128)(2,1)S(1)} %get-tuple-element.35), channel_id=1, source_target_pairs={{0,8},{8,0},{16,24},{24,16},{32,40},{40,32},{48,56},{56,48},{64,72... | collective-permute-start | bytes 3170312 | tf_op jit(solution)/shard_map/ppermute | solution.py:64
  70.3 5.6 %collective-permute-start.21 = (bf16[32,32,128]{2,1,0:T(8,128)(2,1)S(1)}, bf16[32,32,128]{2,1,0:T(8,128)(2,1)S(1)}, u32[]{:S(2)}, u32[]{:S(2)}) collective-permute-start(bf16[32,32,128]{2,1,0:T(8,128)(2,1)S(1)} %get-tuple-element.50), channel_id=1, source_target_pairs={{0,32},{8,232},{16,48},{24,248},{32,64},{40,8},{48,80},{56,24},{64... | collective-permute-start | bytes 786440 | tf_op jit(solution)/shard_map/ppermute | solution.py:64
  70.3 8.3 %collective-permute-start.23 = (bf16[32,32,128]{2,1,0:T(8,128)(2,1)S(1)}, bf16[32,32,128]{2,1,0:T(8,128)(2,1)S(1)}, u32[]{:S(2)}, u32[]{:S(2)}) collective-permute-start(bf16[32,32,128]{2,1,0:T(8,128)(2,1)S(1)} %get-tuple-element.49), channel_id=1, source_target_pairs={{0,32},{8,232},{16,48},{24,248},{32,64},{40,8},{48,80},{56,24},{64... | collective-permute-start | bytes 786440 | tf_op jit(solution)/shard_map/ppermute | solution.py:64
  76.0 18.7 %copy-start.1 = (f32[2,8,128,32]{2,3,1,0:T(8,128)S(1)}, f32[2,8,128,32]{2,3,1,0:T(8,128)}, u32[]{:S(2)}) copy-start(f32[2,8,128,32]{2,3,1,0:T(8,128)} %param.8) | copy-start | bytes 786436
  76.0 18.7 %copy-start.2 = (f32[2,8,128,32]{2,3,1,0:T(8,128)S(1)}, f32[2,8,128,32]{2,3,1,0:T(8,128)}, u32[]{:S(2)}) copy-start(f32[2,8,128,32]{2,3,1,0:T(8,128)} %param.9) | copy-start | bytes 786436
  76.0 5.3 %collective-permute-start.22 = (bf16[32,32,128]{2,1,0:T(8,128)(2,1)S(1)}, bf16[32,32,128]{2,1,0:T(8,128)(2,1)S(1)}, u32[]{:S(2)}, u32[]{:S(2)}) collective-permute-start(bf16[32,32,128]{2,1,0:T(8,128)(2,1)S(1)} %add_convert_fusion.4), channel_id=1, source_target_pairs={{0,32},{8,232},{16,48},{24,248},{32,64},{40,8},{48,80},{56,24},{64... | collective-permute-start | bytes 786440 | tf_op jit(solution)/shard_map/ppermute | solution.py:64
  78.8 5.6 %collective-permute-start.25 = (bf16[32,32,128]{2,1,0:T(8,128)(2,1)S(1)}, bf16[32,32,128]{2,1,0:T(8,128)(2,1)S(1)}, u32[]{:S(2)}, u32[]{:S(2)}) collective-permute-start(bf16[32,32,128]{2,1,0:T(8,128)(2,1)S(1)} %add_convert_fusion.3), channel_id=1, source_target_pairs={{0,32},{8,232},{16,48},{24,248},{32,64},{40,8},{48,80},{56,24},{64... | collective-permute-start | bytes 786440 | tf_op jit(solution)/shard_map/ppermute | solution.py:64
  81.4 8.9 %collective-permute-start.24 = (bf16[32,32,128]{2,1,0:T(8,128)(2,1)S(1)}, bf16[32,32,128]{2,1,0:T(8,128)(2,1)S(1)}, u32[]{:S(2)}, u32[]{:S(2)}) collective-permute-start(bf16[32,32,128]{2,1,0:T(8,128)(2,1)S(1)} %add_convert_fusion.2), channel_id=1, source_target_pairs={{0,32},{8,232},{16,48},{24,248},{32,64},{40,8},{48,80},{56,24},{64... | collective-permute-start | bytes 786440 | tf_op jit(solution)/shard_map/ppermute | solution.py:64
  84.5 6.1 %collective-permute-start.28 = (bf16[32,32,128]{2,1,0:T(8,128)(2,1)S(1)}, bf16[32,32,128]{2,1,0:T(8,128)(2,1)S(1)}, u32[]{:S(2)}, u32[]{:S(2)}) collective-permute-start(bf16[32,32,128]{2,1,0:T(8,128)(2,1)S(1)} %add_convert_fusion.1), channel_id=1, source_target_pairs={{0,32},{8,232},{16,48},{24,248},{32,64},{40,8},{48,80},{56,24},{64... | collective-permute-start | bytes 786440 | tf_op jit(solution)/shard_map/ppermute | solution.py:64
  86.4 8.3 %collective-permute-start.26 = (bf16[8,3,32,128]{3,2,1,0:T(8,128)(2,1)S(1)}, bf16[8,3,32,128]{3,2,1,0:T(8,128)(2,1)S(1)}, u32[]{:S(2)}, u32[]{:S(2)}) collective-permute-start(bf16[8,3,32,128]{3,2,1,0:T(8,128)(2,1)S(1)} %get-tuple-element.44), channel_id=1, source_target_pairs={{0,7},{1,2},{2,1},{3,4},{4,3},{5,6},{6,5},{7,0},{8,15},{9,10},{10,... | collective-permute-start | bytes 589832 | tf_op jit(solution)/shard_map/ppermute | solution.py:68
  90.4 8.2 %collective-permute-start.27 = (bf16[32,32,128]{2,1,0:T(8,128)(2,1)S(1)}, bf16[32,32,128]{2,1,0:T(8,128)(2,1)S(1)}, u32[]{:S(2)}, u32[]{:S(2)}) collective-permute-start(bf16[32,32,128]{2,1,0:T(8,128)(2,1)S(1)} %add_convert_fusion), channel_id=1, source_target_pairs={{0,32},{8,232},{16,48},{24,248},{32,64},{40,8},{48,80},{56,24},{64... | collective-permute-start | bytes 786440 | tf_op jit(solution)/shard_map/ppermute | solution.py:64
  90.6 8.0 %collective-permute-start.30 = (bf16[16,32,128]{2,1,0:T(8,128)(2,1)S(1)}, bf16[16,32,128]{2,1,0:T(8,128)(2,1)S(1)}, u32[]{:S(2)}, u32[]{:S(2)}) collective-permute-start(bf16[16,32,128]{2,1,0:T(8,128)(2,1)S(1)} %add_convert_fusion.9), channel_id=1, source_target_pairs={{0,16},{8,24},{16,0},{24,8},{32,48},{40,56},{48,32},{56,40},{64,80... | collective-permute-start | bytes 393224 | tf_op jit(solution)/shard_map/ppermute | solution.py:64
  98.7 6.2 %collective-permute-start.31 = (bf16[16,32,128]{2,1,0:T(8,128)(2,1)S(1)}, bf16[16,32,128]{2,1,0:T(8,128)(2,1)S(1)}, u32[]{:S(2)}, u32[]{:S(2)}) collective-permute-start(bf16[16,32,128]{2,1,0:T(8,128)(2,1)S(1)} %get-tuple-element.52), channel_id=1, source_target_pairs={{0,8},{8,0},{16,24},{24,16},{32,40},{40,32},{48,56},{56,48},{64,72... | collective-permute-start | bytes 393224 | tf_op jit(solution)/shard_map/ppermute | solution.py:64
  104.0 5.1 %collective-permute-start.29 = (bf16[16,32,128]{2,1,0:T(8,128)(2,1)S(1)}, bf16[16,32,128]{2,1,0:T(8,128)(2,1)S(1)}, u32[]{:S(2)}, u32[]{:S(2)}) collective-permute-start(bf16[16,32,128]{2,1,0:T(8,128)(2,1)S(1)} %get-tuple-element.51), channel_id=1, source_target_pairs={{0,16},{8,24},{16,0},{24,8},{32,48},{40,56},{48,32},{56,40},{64,80... | collective-permute-start | bytes 393224 | tf_op jit(solution)/shard_map/ppermute | solution.py:64
